TPU v7x, 32 devices: a whole 2x2x4 slice. The times are simulated.
32 devices in a mesh: rows: 16 (over z, y, core), ctx: 2 (over x).
Axes of the slice: x: 2, y: 2, z: 4, core: 2. Of those that a mesh axis runs over, the one named last changes fastest.
Arguments:
- tokens: bfloat16 [32, 512, 1024], P('rows', 'ctx'), may hold values from -6 to 6
- cotangent: bfloat16 [32, 512, 1024], P('rows', 'ctx'), may hold values from -6 to 6
- w_qkv: bfloat16 [1024, 3072], replicated, may hold values from -0.1875 to 0.1875
- w_out: bfloat16 [1024, 1024], replicated, may hold values from -0.1875 to 0.1875
- w_fc1: bfloat16 [1024, 4096], replicated, may hold values from -0.1875 to 0.1875
- w_fc2: bfloat16 [4096, 1024], replicated, may hold values from -0.09375 to 0.09375
- norm_gain: float32 [3, 1024], replicated, may hold values from 0.1 to 1.9
- norm_bias: float32 [3, 1024], replicated, may hold values from -1.5 to 1.5
- mid_gain: float32 [4096], replicated, may hold values from 0.1 to 1.9
- mid_bias: float32 [4096], replicated, may hold values from -1.5 to 1.5
- head_scale: float32 [16], replicated, may hold values from 0.5 to 2
- doc_lengths: int32 [32, 4], P('rows'), may hold values from 1 to 256, 512 in all within a row
Outputs:
- output: bfloat16 [32, 512, 1024], P('rows', 'ctx')
- grad_tokens: float32 [32, 512, 1024], P('rows', 'ctx')
- grad_w_qkv: float32 [1024, 3072], P('ctx')
- grad_w_out: float32 [1024, 1024], P('ctx')
- grad_w_fc1: float32 [1024, 4096], P('ctx')
- grad_w_fc2: float32 [4096, 1024], P('ctx')
- grad_norm_gain: float32 [3, 1024], P(None, 'ctx')
- grad_norm_bias: float32 [3, 1024], P(None, 'ctx')
- grad_mid_gain: float32 [4096], P('ctx')
- grad_mid_bias: float32 [4096], P('ctx')
- grad_head_scale: float32 [16], P('ctx')
Inputs may be any that keep to these rules, and one draw needn't show every extreme that they name: `doc_lengths`: in each row the 4 lengths sum to 512, and the largest is exactly 256.
All inputs are finite; a program needn't handle non-finite values.
Results may differ from a plain program's by a relative error of at most 0.011.
Values may be sent and summed in bfloat16 or wider, within the bound.
A program may use at most 256 MiB of HBM per device.

v0:
```python
import jax
import jax.numpy as jnp
from jax import lax
from jax.sharding import PartitionSpec as P

epsilon = 1e-05
masked_value = -1e30


def layer_norm(values, gain_vec, offset_vec):
    average = jnp.mean(values, axis=-1, keepdims=True)
    centered = values - average
    variance = jnp.mean(centered * centered, axis=-1, keepdims=True)
    return centered * lax.rsqrt(variance + epsilon) * gain_vec + offset_vec


def mid_block(first_out, gain_vec, offset_vec):
    return layer_norm(jax.nn.gelu(first_out, approximate=False), gain_vec, offset_vec)


def contract_rows(left_mat, right_mat):
    return lax.dot_general(
        left_mat, right_mat, (((0,), (0,)), ((), ())), preferred_element_type=jnp.float32
    )


def times_transposed(left_mat, right_mat):
    return lax.dot_general(
        left_mat, right_mat, (((1,), (1,)), ((), ())), preferred_element_type=jnp.float32
    )


def block_mask(labels, start_row, block_rows):
    length_total = labels.shape[1]
    places = jnp.arange(length_total, dtype=jnp.int32)
    place_blk = start_row + jnp.arange(block_rows, dtype=jnp.int32)
    same_doc = labels[:, :, None] == labels[:, None, :]
    return same_doc & (place_blk[None, :, None] >= places[None, None, :])


def block_scores(query_rows, key_rows, labels, start_row, block_rows):
    score_scale = query_rows.shape[3] ** (-0.5)
    scores = (
        jnp.einsum("rqhd,rkhd->rhqk", query_rows, key_rows, preferred_element_type=jnp.float32)
        * score_scale
    )
    allowed = block_mask(labels, start_row, block_rows)
    return (query_rows, jnp.where(allowed[:, None], scores, masked_value))


def attend_forward(query_rows, key_rows, value_rows, labels, block_rows):
    block_count = key_rows.shape[1] // block_rows

    def one_block(number):
        start_row = number * block_rows
        query_blk, scores = block_scores(query_rows, key_rows, labels, start_row, block_rows)
        row_max = jnp.max(scores, axis=-1, keepdims=True)
        powers = jnp.exp(scores - row_max)
        totals = jnp.sum(powers, axis=-1, keepdims=True)
        attn_probs = (powers / totals).astype(jnp.bfloat16)
        attended = jnp.einsum(
            "rhqk,rkhd->rqhd", attn_probs, value_rows, preferred_element_type=jnp.float32
        )
        return (attended, (row_max + jnp.log(totals))[..., 0])

    attended, log_totals = lax.map(one_block, jnp.arange(block_count, dtype=jnp.int32))
    attended = jnp.moveaxis(attended, 0, 1).reshape(query_rows.shape)
    return (attended, log_totals)


def attend_backward(
    query_rows, key_rows, value_rows, labels, log_totals, grad_attended, block_rows
):
    block_count = key_rows.shape[1] // block_rows
    score_scale = query_rows.shape[3] ** (-0.5)

    def one_block(carried, number):
        grad_keys, grad_values = carried
        start_row = number * block_rows
        query_blk, scores = block_scores(query_rows, key_rows, labels, start_row, block_rows)
        attn_probs = jnp.exp(scores - log_totals[number][..., None])
        probs_low = attn_probs.astype(jnp.bfloat16)
        grad_values = grad_values + jnp.einsum(
            "rhqk,rqhd->rkhd", probs_low, grad_attended, preferred_element_type=jnp.float32
        )
        grad_probs = jnp.einsum(
            "rqhd,rkhd->rhqk", grad_attended, value_rows, preferred_element_type=jnp.float32
        )
        row_dot = jnp.sum(grad_probs * attn_probs, axis=-1, keepdims=True)
        grad_scores = (attn_probs * (grad_probs - row_dot) * score_scale).astype(jnp.bfloat16)
        grad_query = jnp.einsum(
            "rhqk,rkhd->rqhd", grad_scores, key_rows, preferred_element_type=jnp.float32
        )
        grad_keys = grad_keys + jnp.einsum(
            "rhqk,rqhd->rkhd", grad_scores, query_blk, preferred_element_type=jnp.float32
        )
        return ((grad_keys, grad_values), grad_query)

    zeros_init = jnp.zeros(key_rows.shape, jnp.float32)
    (grad_keys, grad_values), grad_query = lax.scan(
        one_block, (zeros_init, zeros_init), jnp.arange(block_count, dtype=jnp.int32)
    )
    grad_query = jnp.moveaxis(grad_query, 0, 1).reshape(query_rows.shape)
    return (grad_query, grad_keys, grad_values)


def local(
    tokens,
    cotangent,
    w_qkv,
    w_out,
    w_fc1,
    w_fc2,
    norm_gain,
    norm_bias,
    mid_gain,
    mid_bias,
    head_scale,
    doc_lengths,
):
    rows_dev, seg_len, model_width = tokens.shape
    ctx_count = lax.axis_size("ctx")
    head_count = head_scale.shape[0]
    head_size = model_width // head_count
    local_heads = head_count // ctx_count
    length_total = seg_len * ctx_count
    block_rows = min(512, length_total)
    token_count = rows_dev * seg_len
    first_head = lax.axis_index("ctx") * local_heads
    local_scale = lax.dynamic_slice_in_dim(head_scale, first_head, local_heads, 0)
    bounds = jnp.cumsum(doc_lengths, axis=-1, dtype=jnp.int32)
    places = jnp.arange(length_total, dtype=jnp.int32)
    labels = jnp.sum(
        (places[None, :, None] >= bounds[:, None, :]).astype(jnp.int32), axis=-1, dtype=jnp.int32
    )
    inputs = tokens.astype(jnp.float32).reshape(token_count, model_width)

    def project_qkv():
        normed = layer_norm(inputs, norm_gain[0], norm_bias[0]).astype(jnp.bfloat16)
        qkv_local = jnp.dot(normed, w_qkv, preferred_element_type=jnp.float32).astype(jnp.bfloat16)
        return (normed, qkv_local.reshape(rows_dev, seg_len, 3, head_count, head_size))

    normed, qkv_local = project_qkv()
    qkv_heads = lax.all_to_all(qkv_local, "ctx", split_axis=3, concat_axis=1, tiled=True)
    attended, log_totals = attend_forward(
        qkv_heads[:, :, 0], qkv_heads[:, :, 1], qkv_heads[:, :, 2], labels, block_rows
    )
    sent_heads = (attended * local_scale[None, None, :, None]).astype(jnp.bfloat16)
    returned = lax.all_to_all(sent_heads, "ctx", split_axis=1, concat_axis=2, tiled=True).reshape(
        token_count, model_width
    )
    projected = jnp.dot(returned, w_out, preferred_element_type=jnp.float32)
    post_norm, post_pull = jax.vjp(layer_norm, projected, norm_gain[1], norm_bias[1])
    hidden = inputs + post_norm
    ffn_norm, ffn_pull = jax.vjp(layer_norm, hidden, norm_gain[2], norm_bias[2])
    ffn_in = ffn_norm.astype(jnp.bfloat16)
    first_out = jnp.dot(ffn_in, w_fc1, preferred_element_type=jnp.float32)
    middle, mid_pull = jax.vjp(mid_block, first_out, mid_gain, mid_bias)
    middle_low = middle.astype(jnp.bfloat16)
    second_out = jnp.dot(middle_low, w_fc2, preferred_element_type=jnp.float32)
    output = (hidden + second_out).astype(jnp.bfloat16).reshape(tokens.shape)
    grad_top = cotangent.reshape(token_count, model_width)
    grad_fc2 = contract_rows(middle_low, grad_top)
    grad_middle = times_transposed(grad_top, w_fc2)
    grad_first, grad_mid_gain, grad_mid_bias = mid_pull(grad_middle)
    grad_first_low = grad_first.astype(jnp.bfloat16)
    grad_fc1 = contract_rows(ffn_in, grad_first_low)
    grad_ffn_in = times_transposed(grad_first_low, w_fc1)
    hidden_part, gain_two, bias_two = ffn_pull(grad_ffn_in)
    grad_hidden = grad_top.astype(jnp.float32) + hidden_part
    grad_projected, gain_one, bias_one = post_pull(grad_hidden)
    grad_proj_low = grad_projected.astype(jnp.bfloat16)
    grad_out_w = contract_rows(returned, grad_proj_low)
    grad_sent = times_transposed(grad_proj_low, w_out).astype(jnp.bfloat16)
    grad_sent = grad_sent.reshape(rows_dev, seg_len, head_count, head_size)
    grad_heads = lax.all_to_all(grad_sent, "ctx", split_axis=2, concat_axis=1, tiled=True).astype(
        jnp.float32
    )
    scale_local = jnp.sum(grad_heads * attended, axis=(0, 1, 3))
    grad_scale = lax.dynamic_update_slice(
        jnp.zeros((head_count,), jnp.float32), scale_local, (first_head,)
    )
    grad_attended = (grad_heads * local_scale[None, None, :, None]).astype(jnp.bfloat16)
    normed, qkv_local = project_qkv()
    qkv_heads = lax.all_to_all(qkv_local, "ctx", split_axis=3, concat_axis=1, tiled=True)
    grad_query, grad_keys, grad_values = attend_backward(
        qkv_heads[:, :, 0],
        qkv_heads[:, :, 1],
        qkv_heads[:, :, 2],
        labels,
        log_totals,
        grad_attended,
        block_rows,
    )
    grad_qkv = jnp.stack([grad_query, grad_keys, grad_values], axis=2).astype(jnp.bfloat16)
    grad_local = lax.all_to_all(grad_qkv, "ctx", split_axis=1, concat_axis=3, tiled=True).reshape(
        token_count, 3 * model_width
    )
    grad_qkv_w = contract_rows(normed, grad_local)
    grad_normed = times_transposed(grad_local, w_qkv)
    unused_norm, first_pull = jax.vjp(layer_norm, inputs, norm_gain[0], norm_bias[0])
    input_part, gain_zero, bias_zero = first_pull(grad_normed)
    grad_inputs = (grad_hidden + input_part).reshape(tokens.shape)
    share = (
        lax.psum_scatter(grad_qkv_w, "ctx", scatter_dimension=0, tiled=True),
        lax.psum_scatter(grad_out_w, "ctx", scatter_dimension=0, tiled=True),
        lax.psum_scatter(grad_fc1, "ctx", scatter_dimension=0, tiled=True),
        lax.psum_scatter(grad_fc2, "ctx", scatter_dimension=0, tiled=True),
        lax.psum_scatter(
            jnp.stack([gain_zero, gain_one, gain_two], axis=1),
            "ctx",
            scatter_dimension=0,
            tiled=True,
        ),
        lax.psum_scatter(
            jnp.stack([bias_zero, bias_one, bias_two], axis=1),
            "ctx",
            scatter_dimension=0,
            tiled=True,
        ),
        lax.psum_scatter(grad_mid_gain, "ctx", scatter_dimension=0, tiled=True),
        lax.psum_scatter(grad_mid_bias, "ctx", scatter_dimension=0, tiled=True),
        lax.psum_scatter(grad_scale, "ctx", scatter_dimension=0, tiled=True),
    )
    summed = lax.psum(
        (share[0], share[1], share[2], share[3], share[4], share[5], share[6], share[7], share[8]),
        "rows",
    )
    return (
        output,
        grad_inputs,
        summed[0],
        summed[1],
        summed[2],
        summed[3],
        summed[4].T,
        summed[5].T,
        summed[6],
        summed[7],
        summed[8],
    )


def solution(mesh):
    in_specs = (
        P("rows", "ctx", None),
        P("rows", "ctx", None),
        P(),
        P(),
        P(),
        P(),
        P(),
        P(),
        P(),
        P(),
        P(),
        P("rows", None),
    )
    out_specs = (
        P("rows", "ctx", None),
        P("rows", "ctx", None),
        P("ctx", None),
        P("ctx", None),
        P("ctx", None),
        P("ctx", None),
        P(None, "ctx"),
        P(None, "ctx"),
        P("ctx"),
        P("ctx"),
        P("ctx"),
    )
    return jax.shard_map(local, mesh=mesh, in_specs=in_specs, out_specs=out_specs, check_vma=False)
```

profile of v0, /device:TPU:0, one launch (start us, length us, event | category | flops | bytes accessed | tf_op | source)
XLA Modules:
  0.0 1473.4 jit_solution(6777186878300915070)
XLA Ops:
  15.0 7.5 convolution_convert_fusion
  22.6 8.5 reshape.277
  31.1 11.2 copy.82
  42.3 5.2 all-to-all-start
  48.5 36.7 %all-to-all-done = bf16[2,256,3,16,64]{1,0,4,2,3:T(2,128)(2,1)} async-done(((bf16[2,256,3,16,64]{1,0,4,2,3:T(2,128)(2,1)}), bf16[2,256,3,16,64]{1,0,4,2,3:T(2,128)(2,1)}, u32[]{:S(2)}, u32[]{:S(2)}) %all-to-all-start) | async-done | bytes 3145760 | tf_op jit(solution)/shard_map/all_to_all | solution.py:144
  85.1 8.5 copy.114
  93.7 6.2 all_to_all.50
  99.8 10.0 fusion.3
  109.9 9.3 fusion.2
  119.1 9.6 fusion.40
  128.7 3.8 copy.85
  135.4 16.7 %all_to_all.62 = bf16[2,2,131072]{2,1,0:T(2,128)(2,1)} all-to-all(bf16[2,2,131072]{2,1,0:T(2,128)(2,1)S(1)} %reshape.286), channel_id=1, replica_groups=mesh['rows'=16,'ctx'=2] {'ctx'}, dimensions={0} | all-to-all | bytes 2097152 | tf_op jit(solution)/shard_map/all_to_all | solution.py:149
  152.1 3.7 reshape.287
  155.8 4.5 copy.86
  165.9 26.3 %fusion.105 = (f32[512]{0:T(512)S(1)}, f32[512,4096]{1,0:T(8,128)S(1)}, f32[512,4096]{1,0:T(8,128)}, f32[512,4096]{1,0:T(8,128)}) fusion(bf16[1024,4096]{1,0:T(8,128)(2,1)S(1)} %bitcast.197, f32[512,1024]{1,0:T(8,128)S(1)} %get-tuple-element.98, f32[1024]{0:T(1024)S(1)} %bitcast.194, f32[1024]{0:T(1024)S(1)} %bitcast.186, f32[512]{0:T(512)S(1)} %fusion.78, ...), kind=kOutput, calls=%fused_computation.148 | convolution fusion | flops 4433903104 | bytes 35665920 | tf_op jit(solution)/shard_map/dot_general | solution.py:157
  192.2 15.9 %multiply_reduce_fusion.2 = (f32[512]{0:T(512)S(1)}, f32[512]{0:T(512)S(1)}, f32[4096]{0:T(1024)}, f32[512,4096]{1,0:T(8,128)}) fusion(f32[512,4096]{1,0:T(8,128)S(1)} %get-tuple-element.95, f32[4096]{0:T(1024)S(1)} %copy-done.24, f32[512]{0:T(512)S(1)} %broadcast_multiply_fusion, bf16[512,1024]{1,0:T(8,128)(2,1)} %bitcast.162, bf16[4096,1024]{1,0:T(8,128)(2,1)} %param.17), kind=kOutput, calls=%fused_computation.20 | convolution fusion | flops 4309642240 | bytes 26253312 | tf_op jit(solution)/shard_map/dot_general | solution.py:28
  208.1 6.2 multiply_reduce_fusion.1
  214.3 12.9 add_convert_fusion
  227.2 10.3 multiply_reduce_fusion.4
  242.2 3.3 fusion.97
  252.2 3.6 all-to-all-start.2
  255.8 25.3 %all-to-all-done.2 = bf16[2,256,16,64]{1,3,0,2:T(8,128)(2,1)S(1)} async-done(((bf16[2,256,16,64]{1,3,0,2:T(8,128)(2,1)}), bf16[2,256,16,64]{1,3,0,2:T(8,128)(2,1)S(1)}, u32[]{:S(2)}, u32[]{:S(2)}) %all-to-all-start.2) | async-done | bytes 1048608 | tf_op jit(solution)/shard_map/all_to_all | solution.py:176
  281.8 10.2 fusion.75
  292.1 25.3 %fusion.69 = bf16[2,512,1,8,64]{1,4,3,0,2:T(8,128)(2,1)} fusion(f32[2,8,512,512]{2,3,1,0:T(8,128)} %fusion.75, f32[2,8,512,512]{2,3,1,0:T(8,128)} %get-tuple-element.112, f32[2,8,512]{2,1,0:T(8,128)S(1)} %log_add_fusion, pred[2,512,512]{1,2,0:T(8,128)(4,1)S(1)} %copy-done.14, bf16[2,512,3,8,64]{1,4,3,0,2:T(8,128)(2,1)} %all_to_all.50), kind=kOutput, calls=%fused_computation.95 | convolution fusion | flops 583541248 | bytes 70320128 | tf_op jit(solution)/shard_map/while/body/eval_jaxpr/rhqk,rkhd->rqhd/dot_general | solution.py:91
  317.3 24.8 %fusion.66 = bf16[2,512,1,8,64]{1,4,3,0,2:T(8,128)(2,1)} fusion(f32[2,8,512,512]{2,3,1,0:T(8,128)} %fusion.75, f32[2,8,512,512]{2,3,1,0:T(8,128)} %get-tuple-element.112, f32[2,8,512]{2,1,0:T(8,128)S(1)} %log_add_fusion, pred[2,512,512]{1,2,0:T(8,128)(4,1)S(1)} %copy-done.14, bf16[2,512,3,8,64]{1,4,3,0,2:T(8,128)(2,1)} %all_to_all.50), kind=kOutput, calls=%fused_computation.94 | convolution fusion | flops 583541248 | bytes 70320128 | tf_op jit(solution)/shard_map/while/body/eval_jaxpr/rhqk,rqhd->rkhd/dot_general | solution.py:94
  342.1 8.3 fusion.72
  352.5 8.5 copy.94
  361.1 8.0 reshape.288
  369.1 5.2 all-to-all-start.3
  374.8 33.7 %all-to-all-done.3 = bf16[2,2,393216]{2,1,0:T(2,128)(2,1)} async-done(((bf16[2,2,393216]{2,1,0:T(2,128)(2,1)}), bf16[2,2,393216]{2,1,0:T(2,128)(2,1)}, u32[]{:S(2)}, u32[]{:S(2)}) %all-to-all-start.3) | async-done | bytes 3145760 | tf_op jit(solution)/shard_map/all_to_all | solution.py:196
  408.5 7.9 reshape.289
  416.4 11.2 copy.95
  431.7 6.4 fusion.111
  439.3 12.3 fusion.101
  451.7 13.4 fusion.99
  465.8 8.8 fusion.102
  479.4 103.2 %reduce-scatter.11.cloned.1.call-done = f32[512,3072]{1,0:T(8,128)} async-done(((f32[1024,3072]{1,0:T(8,128)}), f32[512,3072]{1,0:T(8,128)}) %reduce-scatter.11.cloned.1.call-update) | async-done | bytes 6291472 | tf_op jit(solution)/shard_map/reduce_scatter | solution.py:205
  582.6 191.6 %reduce-scatter.17.cloned.1.call-done = f32[2048,1024]{1,0:T(8,128)} async-done(((f32[4096,1024]{1,0:T(8,128)}), f32[2048,1024]{1,0:T(8,128)}) %reduce-scatter.17.cloned.1.call-update) | async-done | bytes 8388624 | tf_op jit(solution)/shard_map/reduce_scatter | solution.py:208
  774.2 191.3 %reduce-scatter.15.cloned.1.call-done = f32[512,4096]{1,0:T(8,128)} async-done(((f32[1024,4096]{1,0:T(8,128)}), f32[512,4096]{1,0:T(8,128)}) %reduce-scatter.15.cloned.1.call-update) | async-done | bytes 8388624 | tf_op jit(solution)/shard_map/reduce_scatter | solution.py:207
  968.1 12.2 add_convert_fusion.3
  981.1 7.1 all-reduce.5
  988.3 4.2 add_add_fusion.4
  993.6 5.9 reduce-scatter.19.cloned.1.call-done
  1000.6 65.0 %all-reduce.3 = (f32[3,512]{1,0:T(4,128)}, f32[3,512]{1,0:T(4,128)}, f32[2048]{0:T(1024)}, f32[2048]{0:T(1024)}, f32[8]{0:T(128)}) all-reduce(f32[3,512]{1,0:T(4,128)S(1)} %bitcast.176, f32[3,512]{1,0:T(4,128)S(1)} %bitcast.175, f32[2048]{0:T(1024)S(1)} %dynamic-slice.1, ...), channel_id=1, replica_groups=mesh['rows'=16,'ctx'=2] {'rows'}, use_global_device_ids=true, to_apply=%region_33.34 | all-reduce | flops 7176 | bytes 57408 | tf_op jit(solution)/shard_map/psum | solution.py:225
  1065.6 382.9 %all-reduce.8.cloned.1.call-done = (f32[512,3072]{1,0:T(8,128)}, f32[512,1024]{1,0:T(8,128)}, f32[512,4096]{1,0:T(8,128)}, f32[2048,1024]{1,0:T(8,128)}) async-done(((f32[512,3072]{1,0:T(8,128)}, f32[512,1024]{1,0:T(8,128)}, f32[512,4096]{1,0:T(8,128)}, f32[2048,1024]{1,0:T(8,128)}), (f32[512,3072]{1,0:T(8,128)}, f32[512,1024]{1,0:T(8,128)}, f32[512,4096]{1,0:T(8,128)}, ...) | async-done | bytes 25165840 | tf_op jit(solution)/shard_map/psum | solution.py:225
  1448.5 6.9 copy.120
  1457.2 4.3 copy.122
  1462.9 3.4 copy.123
  (177 shorter events, 49.9 us)
Async XLA Ops:
  7.2 154.7 %copy-start = (bf16[1024,1024]{1,0:T(8,128)(2,1)S(1)}, bf16[1024,1024]{1,0:T(8,128)(2,1)}, u32[]{:S(2)}) copy-start(bf16[1024,1024]{1,0:T(8,128)(2,1)} %param.15) | copy-start | bytes 6291460
  8.8 4.0 copy-start.34
  11.0 1.8 copy-start.32
  11.0 1.8 copy-start.28
  31.1 16.4 %copy-start.38 = (s32[2,4]{1,0:T(2,128)S(1)}, s32[2,4]{1,0:T(2,128)}, u32[]{:S(2)}) copy-start(s32[2,4]{1,0:T(2,128)} %param.23) | copy-start | bytes 100
  31.1 16.6 %copy-start.40 = (f32[16]{0:T(128)S(1)}, f32[16]{0:T(128)}, u32[]{:S(2)}) copy-start(f32[16]{0:T(128)} %param.22) | copy-start | bytes 196
  42.3 42.8 %all-to-all-start = ((bf16[2,256,3,16,64]{1,0,4,2,3:T(2,128)(2,1)}), bf16[2,256,3,16,64]{1,0,4,2,3:T(2,128)(2,1)}, u32[]{:S(2)}, u32[]{:S(2)}) async-start(bf16[2,256,3,16,64]{1,0,4,2,3:T(2,128)(2,1)} %copy.82), calls=%async_computation | async-start | bytes 6291456 | tf_op jit(solution)/shard_map/all_to_all | solution.py:144
  47.5 431.9 %reduce-scatter.13.cloned.1.call-start = ((), (), s32[]{:S(2)}) async-start(), calls=%async_computation.11 | async-start | bytes 6291456 | tf_op jit(solution)/shard_map/reduce_scatter | solution.py:206
  48.4 70.7 %copy-start.13 = (pred[2,512,512]{1,2,0:T(8,128)(4,1)}, pred[2,512,512]{1,2,0:T(8,128)(4,1)S(1)}, u32[]{:S(2)}) copy-start(pred[2,512,512]{1,2,0:T(8,128)(4,1)S(1)} %compare_and_fusion) | copy-start | bytes 1572868
  152.1 11.5 copy-start.2
  160.2 4.4 slice-start.4
  161.9 2.8 copy-start.10
  163.2 2.6 slice-start.5
  164.3 27.8 %copy-start.7 = (f32[512,1024]{1,0:T(8,128)}, f32[512,1024]{1,0:T(8,128)S(1)}, u32[]{:S(2)}) copy-start(f32[512,1024]{1,0:T(8,128)S(1)} %get-tuple-element.98) | copy-start | bytes 6291460
  165.9 26.3 %copy-start.24 = (f32[4096]{0:T(1024)S(1)}, f32[4096]{0:T(1024)}, u32[]{:S(2)}) copy-start(f32[4096]{0:T(1024)} %param.20) | copy-start | bytes 49156
  192.1 22.1 %copy-start.4 = (f32[512,4096]{1,0:T(8,128)}, f32[512,4096]{1,0:T(8,128)S(1)}, u32[]{:S(2)}) copy-start(f32[512,4096]{1,0:T(8,128)S(1)} %get-tuple-element.95) | copy-start | bytes 25165828
  227.2 10.3 copy-start.8
  227.2 11.1 copy-start.18
  238.2 4.0 copy-start.11
  252.2 28.9 %all-to-all-start.2 = ((bf16[2,256,16,64]{1,3,0,2:T(8,128)(2,1)}), bf16[2,256,16,64]{1,3,0,2:T(8,128)(2,1)S(1)}, u32[]{:S(2)}, u32[]{:S(2)}) async-start(bf16[2,256,16,64]{1,3,0,2:T(8,128)(2,1)} %copy.88), calls=%async_computation.2 | async-start | bytes 2097152 | tf_op jit(solution)/shard_map/all_to_all | solution.py:176
  281.8 60.4 %copy-start.5 = (f32[2,2,8,8,8,256]{5,4,1,3,2,0:T(8,128)}, f32[2,2,8,8,8,256]{5,4,1,3,2,0:T(8,128)S(1)}, u32[]{:S(2)}) copy-start(f32[2,2,8,8,8,256]{5,4,1,3,2,0:T(8,128)S(1)} %copy.108) | copy-start | bytes 6291460
  281.8 10.3 copy-start.14
  342.1 8.4 copy-start.20
  342.1 8.4 copy-start.21
  361.0 13.3 copy-start.3
  361.1 13.3 copy-start.23
  361.1 13.3 copy-start.27
  361.1 13.3 copy-start.35
  361.1 13.3 copy-start.37
  369.1 39.4 %all-to-all-start.3 = ((bf16[2,2,393216]{2,1,0:T(2,128)(2,1)}), bf16[2,2,393216]{2,1,0:T(2,128)(2,1)}, u32[]{:S(2)}, u32[]{:S(2)}) async-start(bf16[2,2,393216]{2,1,0:T(2,128)(2,1)} %reshape.288), calls=%async_computation.3 | async-start | bytes 6291456 | tf_op jit(solution)/shard_map/all_to_all | solution.py:196
  374.3 208.3 %reduce-scatter.11.cloned.1.call-start = ((), (), s32[]{:S(2)}) async-start(), calls=%async_computation.10 | async-start | bytes 18874368 | tf_op jit(solution)/shard_map/reduce_scatter | solution.py:205
  438.1 336.1 %reduce-scatter.17.cloned.1.call-start = ((), (), s32[]{:S(2)}) async-start(), calls=%async_computation.13 | async-start | bytes 25165824 | tf_op jit(solution)/shard_map/reduce_scatter | solution.py:208
  451.6 513.9 %reduce-scatter.15.cloned.1.call-start = ((), (), s32[]{:S(2)}) async-start(), calls=%async_computation.12 | async-start | bytes 25165824 | tf_op jit(solution)/shard_map/reduce_scatter | solution.py:207
  465.1 10.5 copy-start.33
  465.1 10.6 copy-start.29
  465.2 527.4 %reduce-scatter.21.cloned.1.call-start = ((), (), s32[]{:S(2)}) async-start(), calls=%async_computation.15 | async-start | bytes 786432
  475.7 523.9 %reduce-scatter.19.cloned.1.call-start = ((), (), s32[]{:S(2)}) async-start(), calls=%async_computation.14 | async-start | bytes 786432
  479.4 969.2 %all-reduce.8.cloned.1.call-start = ((), (), s32[]{:S(2)}) async-start(), calls=%async_computation.16 | async-start | bytes 50331648 | tf_op jit(solution)/shard_map/psum | solution.py:225
  968.0 12.3 copy-start.6
  968.0 12.3 copy-start.16
  968.1 13.0 copy-start.25
  968.1 13.0 copy-start.36
  1448.5 6.9 copy-start.17
  1448.5 8.2 slice-start.2
  1448.5 8.7 slice-start.3
  1455.4 6.0 slice-start
  1457.2 5.8 slice-start.1
  1457.2 9.2 copy-start.1
  (10 other events, 10.6 us)
Sparse Core Ops, SparseCore 0:
  245.6 65.7 reduce-scatter.12
  438.2 144.3 reduce-scatter.10
  585.0 189.1 reduce-scatter.16
  776.3 189.1 reduce-scatter.14
  967.7 14.5 reduce-scatter.20
  985.0 14.5 reduce-scatter.18
  1005.2 443.2 all-reduce.7
where the time goes:
time: 1480 us; the launch traced here: 1470 us
  waiting for transfers between devices  971 us (66%)
  matrix products  209 us (14%)
  local copies, waits for them, and re-layouts  125 us (8%)
  blocking collectives  88.8 us (6%)
  other arithmetic  48.8 us (3%)
  between operations  16.3 us (1%)
    psum x1, waiting for transfers between devices, local(): lax.psum((share[0], share[1], share[2], share[3], share[4], share[5], sha...  383 us
    reduce_scatter x1, waiting for transfers between devices, local(): lax.psum_scatter(grad_fc2, 'ctx', scatter_dimension=0, tiled=True)  192 us
    reduce_scatter x1, waiting for transfers between devices, local(): lax.psum_scatter(grad_fc1, 'ctx', scatter_dimension=0, tiled=True)  191 us
    reduce_scatter x1, waiting for transfers between devices, local(): lax.psum_scatter(grad_qkv_w, 'ctx', scatter_dimension=0, tiled=True)  103 us
    psum x1, blocking collectives, local(): lax.psum((share[0], share[1], share[2], share[3], share[4], share[5], sha...  65 us
    unnamed x116, local copies, waits for them, and re-layouts  56.7 us
    dot_general x4, matrix products, times_transposed(): lax.dot_general(left_mat, right_mat, (((1,), (1,)), ((), ())), preferred_...  37.9 us
    all_to_all x1, waiting for transfers between devices, local(): lax.all_to_all(qkv_local, 'ctx', split_axis=3, concat_axis=1, tiled=True)  36.7 us
  transfers between devices with their start and end apart: 10, of which 8 were waited for; matrix products, arithmetic and copies ran while one was open for 12% of the time, Pallas kernels for 0%

commit v1 on v0

v1 whole, which is shorter than its diff:
```python
import functools

import jax
import jax.numpy as jnp
from jax import lax
from jax.experimental import pallas as pl
from jax.experimental.pallas import tpu as pltpu
from jax.sharding import PartitionSpec as P

EPS = 1e-05
MASKED = -1e30
BF = jnp.bfloat16
F32 = jnp.float32
REACH = 256
QB = 128
TILE = 1024


def dot(a, b, ca, cb):
    return lax.dot_general(a, b, (((ca,), (cb,)), ((), ())), preferred_element_type=F32)


def ln_stats(v):
    mean = jnp.mean(v, axis=-1, keepdims=True)
    cen = v - mean
    inv = lax.rsqrt(jnp.mean(cen * cen, axis=-1, keepdims=True) + EPS)
    return cen * inv, inv


def ln_back(e, gain, n, inv):
    a = e * gain
    return inv * (
        a - jnp.mean(a, axis=-1, keepdims=True) - n * jnp.mean(a * n, axis=-1, keepdims=True)
    )


def colsum(v):
    return jnp.sum(v, axis=0, keepdims=True)


def params(mib=60):
    return pltpu.CompilerParams(vmem_limit_bytes=mib * 2**20)


def cost(macs, nbytes, trans=0):
    return pl.CostEstimate(flops=2 * macs, bytes_accessed=nbytes, transcendentals=trans)


def call(kernel, grid, scalars, in_specs, out_specs, out_shape, scratch, ce):
    return pl.pallas_call(
        kernel,
        grid_spec=pltpu.PrefetchScalarGridSpec(
            num_scalar_prefetch=1,
            grid=grid,
            in_specs=in_specs,
            out_specs=out_specs,
            scratch_shapes=scratch,
        ),
        out_shape=out_shape,
        compiler_params=params(),
        cost_estimate=ce,
    )


def const_spec(shape):
    return pl.BlockSpec(shape, lambda i, s: (0,) * len(shape))


def struct(shape, dtype):
    return jax.ShapeDtypeStruct(shape, dtype)


def qkv_kernel(s, x, w, g, b, normed, qkv):
    @pl.when(pl.program_id(0) == 0)
    def _():
        n, _ = ln_stats(x[...].astype(F32))
        normed[...] = (n * g[...] + b[...]).astype(BF)

    qkv[0] = dot(normed[...], w[...], 1, 0).astype(BF)


def qkv_call(idx, x, w, g, b):
    t, d = x.shape
    return call(
        qkv_kernel,
        (3,),
        1,
        [
            const_spec((t, d)),
            pl.BlockSpec((d, d), lambda i, s: (0, i)),
            const_spec((1, d)),
            const_spec((1, d)),
        ],
        [const_spec((t, d)), pl.BlockSpec((1, t, d), lambda i, s: (i, 0, 0))],
        [struct((t, d), BF), struct((3, t, d), BF)],
        [],
        cost(3 * t * d * d, 2 * (3 * d * d + 5 * t * d)),
    )(idx, x, w, g, b)


def key_range(i):
    return max(0, i * QB - REACH), (i + 1) * QB


def fill_bias(start, bias, t):
    for i in range(t // QB):
        k0, k1 = key_range(i)
        u = lax.broadcasted_iota(jnp.int32, (k1 - k0, QB), 0) + k0
        q = lax.broadcasted_iota(jnp.int32, (k1 - k0, QB), 1) + i * QB
        first = start[:, i * QB : (i + 1) * QB]
        ok = (u >= first) & (u <= q)
        one = jnp.where(ok, 0.0, MASKED).astype(F32)
        bias[i, 0 : k1 - k0, 0:QB] = one
        bias[i, 0 : k1 - k0, QB : 2 * QB] = one


def both_heads(v, hd):
    lane = lax.broadcasted_iota(jnp.int32, v.shape, 1)
    zero = jnp.zeros_like(v)
    return jnp.concatenate([jnp.where(lane < hd, v, zero), jnp.where(lane < hd, zero, v)], axis=0)


def attn_fwd_kernel(s, q, k, v, start, scale, sent, lse, bias):
    t, w = q.shape[1], q.shape[2]
    hd = w // 2

    @pl.when(pl.program_id(0) == 0)
    def _():
        fill_bias(start, bias, t)

    vt = v[0].astype(F32).T.astype(BF)
    for i in range(t // QB):
        k0, k1 = key_range(i)
        qs = slice(i * QB, (i + 1) * QB)
        qm = both_heads(q[0, qs, :], hd) * (hd**-0.5)
        st = dot(k[0, k0:k1, :], qm.astype(BF), 1, 1) + bias[i, 0 : k1 - k0, :]
        top = jnp.max(st, axis=0, keepdims=True)
        pt = jnp.exp(st - top)
        total = jnp.sum(pt, axis=0, keepdims=True)
        ot = dot(vt[:, k0:k1], pt.astype(BF), 1, 0) * (1.0 / total)
        o = jnp.concatenate([ot[0:hd, 0:QB], ot[hd:, QB:]], axis=0).T
        sent[qs, :] = (o * scale[...]).astype(BF)
        ls = top + jnp.log(total)
        lse[0, 0:1, qs] = ls[:, 0:QB]
        lse[0, 1:2, qs] = ls[:, QB:]


def attn_fwd_call(idx, qkv, start, scale):
    _, t, d = qkv.shape
    pairs = d // 128
    part = lambda j: pl.BlockSpec((1, t, 128), lambda i, s: (j, 0, i))
    return call(
        attn_fwd_kernel,
        (pairs,),
        1,
        [part(0), part(1), part(2), const_spec((1, t)), pl.BlockSpec((1, 128), lambda i, s: (0, i))],
        [
            pl.BlockSpec((t, 128), lambda i, s: (0, i)),
            pl.BlockSpec((1, 2, t), lambda i, s: (i, 0, 0)),
        ],
        [struct((t, d), BF), struct((pairs, 2, t), F32)],
        [pltpu.VMEM((t // QB, QB + REACH, 2 * QB), F32)],
        cost(t * d * t * 2, 8 * t * d, t * t * 8),
    )(idx, qkv, qkv, qkv, start, scale)


def attn_bwd_kernel(s, q, k, v, gs, sent, lse, start, scale, send, keep, hsum, bias, gk, gv, gqt):
    t, w = q.shape[1], q.shape[2]
    hd = w // 2
    pid = pl.program_id(0)
    half = pl.num_programs(0) // 2

    @pl.when(pid == 0)
    def _():
        fill_bias(start, bias, t)

    kt = k[0].astype(F32).T.astype(BF)
    gsf = gs[...].astype(F32)
    prod = (gsf * sent[...].astype(F32)).T
    d0 = jnp.sum(prod[0:hd], axis=0, keepdims=True)
    d1 = jnp.sum(prod[hd:], axis=0, keepdims=True)
    hsum[0] = jnp.concatenate([d0, d1], axis=0)
    ga = (gsf * scale[...]).astype(BF)
    gk[...] = jnp.zeros_like(gk)
    gv[...] = jnp.zeros_like(gv)
    for i in range(t // QB):
        k0, k1 = key_range(i)
        qs = slice(i * QB, (i + 1) * QB)
        qm = (both_heads(q[0, qs, :], hd) * (hd**-0.5)).astype(BF)
        gm = both_heads(ga[qs, :], hd)
        st = dot(k[0, k0:k1, :], qm, 1, 1) + bias[i, 0 : k1 - k0, :]
        ls = jnp.concatenate([lse[0, 0:1, qs], lse[0, 1:2, qs]], axis=1)
        dd = jnp.concatenate([d0[:, qs], d1[:, qs]], axis=1)
        pt = jnp.exp(st - ls)
        gp = dot(v[0, k0:k1, :], gm, 1, 1)
        ds = (pt * (gp - dd)).astype(BF)
        gv[k0:k1, :] += dot(pt.astype(BF), gm, 1, 0)
        gk[k0:k1, :] += dot(ds, qm, 1, 0)
        gq = dot(kt[:, k0:k1], ds, 1, 0) * (hd**-0.5)
        gqt[:, qs] = jnp.concatenate([gq[0:hd, 0:QB], gq[hd:, QB:]], axis=0)

    def put(out):
        out[0] = gqt[...].T.astype(BF)
        out[1] = gk[...].astype(BF)
        out[2] = gv[...].astype(BF)

    pl.when(pid < half)(lambda: put(send))
    pl.when(pid >= half)(lambda: put(keep))


def attn_bwd_call(idx, qkv, gs, sent, lse, start, scale):
    _, t, d = qkv.shape
    pairs = d // 128
    half = pairs // 2

    def at(i, s):
        return jnp.where(i < half, i + (1 - s[1]) * half, i - half + s[1] * half)

    part = lambda j: pl.BlockSpec((1, t, 128), lambda i, s: (j, 0, at(i, s)))
    flat = pl.BlockSpec((t, 128), lambda i, s: (0, at(i, s)))
    return call(
        attn_bwd_kernel,
        (pairs,),
        1,
        [
            part(0),
            part(1),
            part(2),
            flat,
            flat,
            pl.BlockSpec((1, 2, t), lambda i, s: (at(i, s), 0, 0)),
            const_spec((1, t)),
            pl.BlockSpec((1, 128), lambda i, s: (0, at(i, s))),
        ],
        [
            pl.BlockSpec((3, t, 128), lambda i, s: (0, 0, jnp.minimum(i, half - 1))),
            pl.BlockSpec((3, t, 128), lambda i, s: (0, 0, jnp.maximum(i - half, 0))),
            pl.BlockSpec((1, 2, t), lambda i, s: (at(i, s), 0, 0)),
        ],
        [
            struct((3, t, d // 2), BF),
            struct((3, t, d // 2), BF),
            struct((pairs, 2, t), F32),
        ],
        [
            pltpu.VMEM((t // QB, QB + REACH, 2 * QB), F32),
            pltpu.VMEM((t, 128), F32),
            pltpu.VMEM((t, 128), F32),
            pltpu.VMEM((128, t), F32),
        ],
        cost(t * d * t * 5, 16 * t * d, t * t * 8),
    )(idx, qkv, qkv, qkv, gs, sent, lse, start, scale)


def ffn_block(i, s):
    return (i % 2) * 2 + jnp.where(i < 2, 1 - s[1], s[1])


def ffn_fwd_kernel(
    s, sent, x, wo, g, b, w1, mg, mb, n1, s1, n2, s2, ffn_in, slope, nmid, smid, send, keep, act, tot
):
    i = pl.program_id(0)
    blocks = pl.num_programs(0) // 2
    width = blocks * act.shape[2]

    @pl.when(i == 0)
    def _():
        n, inv = ln_stats(dot(sent[...], wo[...], 1, 0))
        n1[...] = n
        s1[...] = inv
        hidden = x[...].astype(F32) + n * g[1:2, :] + b[1:2, :]
        n, inv = ln_stats(hidden)
        n2[...] = n
        s2[...] = inv
        ffn_in[...] = (n * g[2:3, :] + b[2:3, :]).astype(BF)
        tot[...] = jnp.zeros_like(tot)

    @pl.when(i < blocks)
    def _():
        f = dot(ffn_in[...], w1[...], 1, 0)
        phi = 0.5 + 0.5 * lax.erf(f * (0.5**0.5))
        a = f * phi
        slope[0] = (phi + f * (jnp.exp(-0.5 * f * f) * 0.3989422804014327)).astype(BF)
        act[i] = a
        tot[...] += jnp.sum(a, axis=-1, keepdims=True)

    @pl.when(i == blocks)
    def _():
        mean = tot[...] * (1.0 / width)
        sq = jnp.zeros_like(mean)
        for j in range(4):
            c = act[j] - mean
            act[j] = c
            sq += jnp.sum(c * c, axis=-1, keepdims=True)
        smid[...] = lax.rsqrt(sq * (1.0 / width) + EPS)

    @pl.when(i >= blocks)
    def _():
        n = act[i - blocks] * smid[...]
        nmid[0] = n.astype(BF)
        m = (n * mg[...] + mb[...]).astype(BF)

        @pl.when(i < blocks + blocks // 2)
        def _():
            send[0] = m

        @pl.when(i >= blocks + blocks // 2)
        def _():
            keep[0] = m


def ffn_fwd_call(idx, sent, x, wo, g, b, w1, mg, mb):
    t, d = x.shape
    ff = w1.shape[1]
    bw = ff // 4
    first = lambda i: jnp.minimum(i, 3)
    second = lambda i: jnp.maximum(i - 4, 0)
    vec = pl.BlockSpec((1, bw), lambda i, s: (0, ffn_block(second(i), s)))
    return call(
        ffn_fwd_kernel,
        (8,),
        1,
        [
            const_spec((t, d)),
            const_spec((t, d)),
            const_spec((d, d)),
            const_spec((3, d)),
            const_spec((3, d)),
            pl.BlockSpec((d, bw), lambda i, s: (0, ffn_block(first(i), s))),
            vec,
            vec,
        ],
        [
            const_spec((t, d)),
            const_spec((t, 1)),
            const_spec((t, d)),
            const_spec((t, 1)),
            const_spec((t, d)),
            pl.BlockSpec((1, t, bw), lambda i, s: (first(i), 0, 0)),
            pl.BlockSpec((1, t, bw), lambda i, s: (second(i), 0, 0)),
            const_spec((t, 1)),
            pl.BlockSpec((1, t, bw), lambda i, s: (jnp.clip(i - 4, 0, 1), 0, 0)),
            pl.BlockSpec((1, t, bw), lambda i, s: (jnp.clip(i - 6, 0, 1), 0, 0)),
        ],
        [
            struct((t, d), F32),
            struct((t, 1), F32),
            struct((t, d), F32),
            struct((t, 1), F32),
            struct((t, d), BF),
            struct((4, t, bw), BF),
            struct((4, t, bw), BF),
            struct((t, 1), F32),
            struct((2, t, bw), BF),
            struct((2, t, bw), BF),
        ],
        [pltpu.VMEM((4, t, bw), F32), pltpu.VMEM((t, 1), F32)],
        cost(t * d * (d + ff), 2 * d * (d + ff) + 30 * t * d, 2 * t * ff),
    )(idx, sent, x, wo, g, b, w1, mg, mb)


def out_kernel(s, send, keep, w2, x, n1, g, b, out, acc):
    i = pl.program_id(0)

    @pl.when(i == 0)
    def _():
        acc[...] = x[...].astype(F32) + n1[...] * g[1:2, :] + b[1:2, :]

    @pl.when(i < 2)
    def _():
        acc[...] += dot(send[0], w2[...], 1, 0)

    @pl.when(i >= 2)
    def _():
        acc[...] += dot(keep[0], w2[...], 1, 0)

    @pl.when(i == 3)
    def _():
        out[...] = acc[...].astype(BF)


def out_call(idx, send, keep, w2, x, n1, g, b):
    t, d = x.shape
    ff = w2.shape[0]
    bw = ff // 4
    return call(
        out_kernel,
        (4,),
        1,
        [
            pl.BlockSpec((1, t, bw), lambda i, s: (jnp.clip(i, 0, 1), 0, 0)),
            pl.BlockSpec((1, t, bw), lambda i, s: (jnp.clip(i - 2, 0, 1), 0, 0)),
            pl.BlockSpec((bw, d), lambda i, s: (ffn_block(i, s), 0)),
            const_spec((t, d)),
            const_spec((t, d)),
            const_spec((3, d)),
            const_spec((3, d)),
        ],
        const_spec((t, d)),
        struct((t, d), BF),
        [pltpu.VMEM((t, d), F32)],
        cost(t * d * ff, 2 * d * ff + 16 * t * d),
    )(idx, send, keep, w2, x, n1, g, b)


def ffn_bwd_kernel(
    s, cot, w2, mg, nmid, smid, slope, w1, n1, s1, n2, s2, g, wo,
    send, keep, ghid, gp_send, gp_keep, gsent, gmg, gmb, gn, bn, ebuf, ta, tan, acc,
):
    i = pl.program_id(0)
    blocks = pl.num_programs(0) // 2
    width = blocks * ebuf.shape[2]

    @pl.when(i == 0)
    def _():
        ta[...] = jnp.zeros_like(ta)
        tan[...] = jnp.zeros_like(tan)
        acc[...] = jnp.zeros_like(acc)

    @pl.when(i < blocks)
    def _():
        e = dot(cot[...], w2[...], 1, 1)
        n = nmid[0].astype(F32)
        gmg[...] = colsum(e * n)
        gmb[...] = colsum(e)
        a = e * mg[...]
        ebuf[i] = a
        ta[...] += jnp.sum(a, axis=-1, keepdims=True)
        tan[...] += jnp.sum(a * n, axis=-1, keepdims=True)

    @pl.when(i >= blocks)
    def _():
        n = nmid[0].astype(F32)
        a = ebuf[i - blocks] - ta[...] * (1.0 / width) - n * (tan[...] * (1.0 / width))
        gf = (a * smid[...] * slope[0].astype(F32)).astype(BF)

        @pl.when(i < blocks + blocks // 2)
        def _():
            send[0] = gf

        @pl.when(i >= blocks + blocks // 2)
        def _():
            keep[0] = gf

        acc[...] += dot(gf, w1[...], 1, 1)

    @pl.when(i == 2 * blocks - 1)
    def _():
        e = acc[...]
        n = n2[...]
        gn[1:2, :] = colsum(e * n)
        bn[1:2, :] = colsum(e)
        gh = cot[...].astype(F32) + ln_back(e, g[2:3, :], n, s2[...])
        ghid[...] = gh
        n = n1[...]
        gn[0:1, :] = colsum(gh * n)
        bn[0:1, :] = colsum(gh)
        gp = ln_back(gh, g[1:2, :], n, s1[...]).astype(BF)
        gsent[...] = dot(gp, wo[...], 1, 1).astype(BF)
        h = gp.shape[1] // 2

        @pl.when(s[1] == 0)
        def _():
            gp_keep[...] = gp[:, :h]
            gp_send[...] = gp[:, h:]

        @pl.when(s[1] == 1)
        def _():
            gp_keep[...] = gp[:, h:]
            gp_send[...] = gp[:, :h]


def ffn_bwd_call(idx, cot, w2, mg, nmid, smid, slope, w1, n1, s1, n2, s2, g, wo):
    t, d = cot.shape
    ff = w1.shape[1]
    bw = ff // 4
    first = lambda i: jnp.minimum(i, 3)
    second = lambda i: jnp.maximum(i - 4, 0)
    vec = pl.BlockSpec((1, bw), lambda i, s: (0, ffn_block(first(i), s)))
    return call(
        ffn_bwd_kernel,
        (8,),
        1,
        [
            const_spec((t, d)),
            pl.BlockSpec((bw, d), lambda i, s: (ffn_block(first(i), s), 0)),
            vec,
            pl.BlockSpec((1, t, bw), lambda i, s: (i % 4, 0, 0)),
            const_spec((t, 1)),
            pl.BlockSpec((1, t, bw), lambda i, s: (second(i), 0, 0)),
            pl.BlockSpec((d, bw), lambda i, s: (0, ffn_block(second(i), s))),
            const_spec((t, d)),
            const_spec((t, 1)),
            const_spec((t, d)),
            const_spec((t, 1)),
            const_spec((3, d)),
            const_spec((d, d)),
        ],
        [
            pl.BlockSpec((1, t, bw), lambda i, s: (jnp.clip(i - 4, 0, 1), 0, 0)),
            pl.BlockSpec((1, t, bw), lambda i, s: (jnp.clip(i - 6, 0, 1), 0, 0)),
            const_spec((t, d)),
            const_spec((t, d // 2)),
            const_spec((t, d // 2)),
            const_spec((t, d)),
            vec,
            vec,
            const_spec((2, d)),
            const_spec((2, d)),
        ],
        [
            struct((2, t, bw), BF),
            struct((2, t, bw), BF),
            struct((t, d), F32),
            struct((t, d // 2), BF),
            struct((t, d // 2), BF),
            struct((t, d), BF),
            struct((1, ff), F32),
            struct((1, ff), F32),
            struct((2, d), F32),
            struct((2, d), F32),
        ],
        [
            pltpu.VMEM((4, t, bw), F32),
            pltpu.VMEM((t, 1), F32),
            pltpu.VMEM((t, 1), F32),
            pltpu.VMEM((t, d), F32),
        ],
        cost(t * d * (d + 2 * ff), 2 * d * (d + 2 * ff) + 40 * t * d),
    )(idx, cot, w2, mg, nmid, smid, slope, w1, n1, s1, n2, s2, g, wo)


def in_bwd_kernel(s, send, keep, w, x, ghid, g, gx, gn, bn, acc):
    i = pl.program_id(0)

    @pl.when(i == 0)
    def _():
        acc[...] = jnp.zeros_like(acc)

    @pl.when(i < 3)
    def _():
        acc[...] += dot(send[0], w[...], 1, 1)

    @pl.when(i >= 3)
    def _():
        acc[...] += dot(keep[0], w[...], 1, 1)

    @pl.when(i == 5)
    def _():
        e = acc[...]
        n, inv = ln_stats(x[...].astype(F32))
        gn[...] = colsum(e * n)
        bn[...] = colsum(e)
        gx[...] = ghid[...] + ln_back(e, g[0:1, :], n, inv)


def in_bwd_call(idx, send, keep, w, x, ghid, g):
    t, d = x.shape
    h = d // 2
    return call(
        in_bwd_kernel,
        (6,),
        1,
        [
            pl.BlockSpec((1, t, h), lambda i, s: (jnp.minimum(i, 2), 0, 0)),
            pl.BlockSpec((1, t, h), lambda i, s: (jnp.maximum(i - 3, 0), 0, 0)),
            pl.BlockSpec((d, h), lambda i, s: (0, (i % 3) * 2 + jnp.where(i < 3, 1 - s[1], s[1]))),
            const_spec((t, d)),
            const_spec((t, d)),
            const_spec((3, d)),
        ],
        [const_spec((t, d)), const_spec((1, d)), const_spec((1, d))],
        [struct((t, d), F32), struct((1, d), F32), struct((1, d), F32)],
        [pltpu.VMEM((t, d), F32)],
        cost(3 * t * d * d, 6 * d * d + 24 * t * d),
    )(idx, send, keep, w, x, ghid, g)


def wgrad_kernel(s, a0, a1, b0, b1, send, keep):
    get = lambda r: r[...].reshape(r.shape[-2:])
    v = dot(get(a0), get(b0), 0, 0) + dot(get(a1), get(b1), 0, 0)

    @pl.when(pl.program_id(0) == 0)
    def _():
        send[...] = v.astype(BF)

    @pl.when(pl.program_id(0) == 1)
    def _():
        keep[...] = v.astype(BF)


def wgrad(idx, a, b, a_at, b_at):
    far = lambda i, s: jnp.where(i == 0, 1 - s[0], s[0])
    spec = lambda at: pl.BlockSpec(at[0], lambda i, s: at[1](far(i, s)))
    t, rows, cols = a_at[0][-2], a_at[0][-1], b_at[0][-1]
    return call(
        wgrad_kernel,
        (2,),
        1,
        [spec(a_at), spec(a_at), spec(b_at), spec(b_at)],
        [const_spec((rows, cols)), const_spec((rows, cols))],
        [struct((rows, cols), BF), struct((rows, cols), BF)],
        [],
        cost(4 * t * rows * cols, 8 * t * rows + 8 * t * cols + 4 * rows * cols),
    )(idx, a[0], a[1], b[0], b[1])


def add_split_kernel(s, *refs, terms, slot):
    f = len(refs) - terms
    i = pl.program_id(0)
    v = refs[0][...].astype(F32)
    for r in refs[1:terms]:
        v = v + r[...].astype(F32)
    v = v.astype(BF)
    for j in range(f):
        @pl.when(i == j)
        def _(j=j):
            refs[terms + j][...] = v


def add_split(idx, arrays, f, slot):
    rows, cols = arrays[0].shape
    part = rows // f
    own = pl.BlockSpec((part, cols), lambda i, s: (i ^ s[slot] if f > 1 else i, 0))
    return call(
        functools.partial(add_split_kernel, terms=len(arrays), slot=slot),
        (f,),
        1,
        [own] * len(arrays),
        [const_spec((part, cols))] * f,
        [struct((part, cols), BF)] * f,
        [],
        cost(rows * cols, (len(arrays) + 1) * 2 * rows * cols),
    )(idx, *arrays)


def factors_of(n):
    out, want, rest = [2], 2, n // 2
    while rest > 1:
        f = min(want, rest)
        out.append(f)
        rest //= f
        want *= 2
    return out


def swap(v, stride, n):
    return lax.ppermute(v, "rows", [(i, i ^ stride) for i in range(n)])


def swap_ctx(v):
    return lax.ppermute(v, "ctx", [(0, 1), (1, 0)])


def strides_of(factors):
    out, s = [], 1
    for f in factors:
        out.append(s)
        s *= f
    return out


def all_gather_pieces(piece, factors, n):
    cur = [piece]
    for f, st in reversed(list(zip(factors, strides_of(factors)))):
        if len(cur) > 2:
            cur = [jnp.concatenate(cur, axis=0)]
        cur = cur + [swap(c, j * st, n) for j in range(1, f) for c in cur]
    return cur


def all_reduce(idx, send, keep, factors):
    n = 1
    for f in factors:
        n *= f
    shape = keep.shape
    short = shape[0] * 2 // n
    if short < 16:
        keep = keep.reshape(shape[0] * 16 // short, -1)
        send = send.reshape(keep.shape)
    terms = [keep, swap_ctx(send)]
    for k, (f, st) in enumerate(list(zip(factors, strides_of(factors)))[1:]):
        parts = add_split(idx, terms, f, 2 + k)
        terms = [parts[0]] + [swap(parts[j], j * st, n) for j in range(1, f)]
    [piece] = add_split(idx, terms, 1, 2)
    return all_gather_pieces(piece, factors, n)


def finish_kernel(s, *refs, pieces, slots):
    out = refs[-1]
    i = pl.program_id(0)
    z = 0
    for slot, f in slots:
        z = z * f + s[slot]
    for j, src in enumerate(refs[:-1]):

        @pl.when(i == j)
        def _(src=src):
            part = src.shape[0] // pieces
            for k in range(pieces):
                rows = pl.ds(pl.multiple_of((k ^ z) * part, part), part)
                out[k * part : (k + 1) * part, :] = src[rows, :].astype(F32)


def finish(idx, groups, shape, place, factors):
    pieces = 1
    for f in factors[2:]:
        pieces *= f
    slots = [(3 + k, f) for k, f in enumerate(factors[2:])]
    rows, cols = groups[0][0].shape
    flat = [v for g in groups for v in g]

    def at(i, s):
        chunk = i // 4
        core = ((i // 2) % 2) ^ s[1]
        y = (i % 2) ^ s[2]
        r, c = place(chunk, core)
        return (r * 2 + y, c)

    return call(
        functools.partial(finish_kernel, pieces=pieces, slots=slots),
        (4 * len(groups),),
        1,
        [const_spec((rows, cols))] * len(flat),
        pl.BlockSpec((rows, cols), at),
        struct(shape, F32),
        [],
        cost(rows * cols * len(flat), 6 * rows * cols * len(flat)),
    )(idx, *flat)


def finish_all(idx, groups, chunk, blocks, place, factors):
    rows, cols = chunk
    shape = (blocks[0] * rows, blocks[1] * cols)
    r, c = groups[0][0].shape
    if r * 2 == rows:
        return finish(idx, groups, shape, place, factors)
    count = len(groups)
    flat = finish(idx, groups, (count * 4 * r, c), lambda j, core: (j * 2 + core, 0), factors)
    flat = flat.reshape(count, 2, rows, cols)
    out = jnp.zeros(shape, F32)
    for j in range(count):
        for core in range(2):
            a, b = place(j, core)
            out = lax.dynamic_update_slice(out, flat[j, core], (a * rows, b * cols))
    return out


def local(
    tokens, cotangent, w_qkv, w_out, w_fc1, w_fc2, norm_gain, norm_bias, mid_gain, mid_bias, head_scale, doc_lengths
):
    n = lax.axis_size("rows")
    factors = factors_of(n)
    d = tokens.shape[2]
    ff = w_fc1.shape[1]
    heads = head_scale.shape[0]
    ctx = lax.axis_index("ctx")
    row = lax.axis_index("rows")
    places = []
    rest = row
    for f in factors:
        places.append(rest % f)
        rest = rest // f
    idx = jnp.stack([ctx] + places).astype(jnp.int32)

    def whole_row(v):
        mine = lax.dynamic_index_in_dim(v, ctx, 0, False)
        got = swap_ctx(lax.dynamic_index_in_dim(v, 1 - ctx, 0, False))
        lo = jnp.where(ctx == 0, mine, got)
        hi = jnp.where(ctx == 0, got, mine)
        return jnp.concatenate([lo, hi], axis=0)

    x = whole_row(tokens)
    cot = whole_row(cotangent)
    t = x.shape[0]
    lengths = lax.dynamic_index_in_dim(doc_lengths, ctx, 0, False)
    at = jnp.arange(t, dtype=jnp.int32)
    start = jnp.zeros((t,), jnp.int32)
    bound = jnp.zeros((), jnp.int32)
    for i in range(lengths.shape[0]):
        bound = bound + lengths[i]
        start = jnp.where(at >= bound, bound, start)
    start = start[None, :]
    scale = jnp.repeat(head_scale, d // heads)[None, :]
    mg, mb = mid_gain[None, :], mid_bias[None, :]

    core = lambda v: (v, swap(v, 1, n))
    normed, qkv = qkv_call(idx, x, w_qkv, norm_gain[0:1], norm_bias[0:1])
    sent, lse = attn_fwd_call(idx, qkv, start, scale)
    n1, s1, n2, s2, ffn_in, slope, nmid, smid, mid_send, mid_keep = ffn_fwd_call(
        idx, sent, x, w_out, norm_gain, norm_bias, w_fc1, mg, mb
    )
    mid_pair = (mid_keep, swap(mid_send, 1, n))
    cot_pair = core(cot)
    gf_send, gf_keep, ghid, gp_send, gp_keep, gsent, gmg, gmb, gn12, bn12 = ffn_bwd_call(
        idx, cot, w_fc2, mg, nmid, smid, slope, w_fc1, n1, s1, n2, s2, norm_gain, w_out
    )
    half = d // 2

    def chunks(*args):
        return all_reduce(idx, *wgrad(idx, *args), factors)

    got2 = [
        chunks(mid_pair, cot_pair, ((1, t, half), lambda x, j=j: (x, 0, j)), ((t, d), lambda x: (0, 0)))
        for j in range(2)
    ]
    gf_pair = (gf_keep, swap(gf_send, 1, n))
    in_pair = core(ffn_in)
    got1 = [
        chunks(in_pair, gf_pair, ((t, half), lambda x: (0, x)), ((1, t, ff // 4), lambda x, j=j: (j, 0, 0)))
        for j in range(2)
    ]
    sent_pair = core(sent)
    gp_pair = (gp_keep, swap(gp_send, 1, n))
    got_o = [chunks(sent_pair, gp_pair, ((t, half), lambda x: (0, x)), ((t, half), lambda x: (0, 0)))]
    gq_send, gq_keep, hsum = attn_bwd_call(idx, qkv, gsent, sent, lse, start, scale)
    gq_pair = (gq_keep, swap(gq_send, 1, n))
    normed_pair = core(normed)
    got_q = [
        chunks(normed_pair, gq_pair, ((t, half), lambda x: (0, x)), ((1, t, half), lambda x, j=j: (j, 0, 0)))
        for j in range(3)
    ]
    gx, gn0, bn0 = in_bwd_call(idx, gq_send, gq_keep, w_qkv, x, ghid, norm_gain)
    out = out_call(idx, mid_send, mid_keep, w_fc2, x, n1, norm_gain, norm_bias)

    ghs = jnp.sum(hsum, axis=-1).reshape(-1) / head_scale
    small = jnp.concatenate(
        [jnp.concatenate([gn0, gn12]).reshape(-1), jnp.concatenate([bn0, bn12]).reshape(-1), gmg[0], gmb[0], ghs]
    )
    small = lax.psum(small, ("rows", "ctx"))

    def take(v, axis):
        size = v.shape[axis] // 2
        return lax.dynamic_slice_in_dim(v, ctx * size, size, axis)

    gn = take(small[: 3 * d].reshape(3, d), 1)
    bn = take(small[3 * d : 6 * d].reshape(3, d), 1)
    gmg = take(small[6 * d : 6 * d + ff], 0)
    gmb = take(small[6 * d + ff : 6 * d + 2 * ff], 0)
    ghs = take(small[6 * d + 2 * ff :], 0)

    def halves(v):
        seg = t // 2
        mine = lax.dynamic_slice_in_dim(v, ctx * seg, seg, 0)
        other = lax.dynamic_slice_in_dim(v, (1 - ctx) * seg, seg, 0)
        got = swap_ctx(other.astype(BF)).astype(v.dtype)
        lo = jnp.where(ctx == 0, mine, got)
        hi = jnp.where(ctx == 0, got, mine)
        return jnp.stack([lo, hi])

    g2 = finish_all(idx, got2, (half, d), (4, 1), lambda j, c: (c * 2 + j, 0), factors)
    g1 = finish_all(idx, got1, (half, d), (1, 4), lambda j, c: (0, j * 2 + c), factors)
    go = finish_all(idx, got_o, (half, half), (1, 2), lambda j, c: (0, c), factors)
    gq = finish_all(idx, got_q, (half, half), (1, 6), lambda j, c: (0, j * 2 + c), factors)
    return (halves(out), halves(gx), gq, go, g1, g2, gn, bn, gmg, gmb, ghs)


def solution(mesh):
    rows = P("rows", "ctx", None)
    in_specs = (rows, rows) + (P(),) * 9 + (P("rows", None),)
    ctx0 = P("ctx", None)
    out_specs = (rows, rows, ctx0, ctx0, ctx0, ctx0, P(None, "ctx"), P(None, "ctx"), P("ctx"), P("ctx"), P("ctx"))
    return jax.shard_map(local, mesh=mesh, in_specs=in_specs, out_specs=out_specs, check_vma=False)
```

time: 1480 us -> 600 us (0.41)
  waiting for transfers between devices: 971 us -> 135 us
  Pallas kernels: 0 us -> 259 us
  matrix products: 209 us -> 0 us
  local copies, waits for them, and re-layouts: 125 us -> 21.7 us
  starting transfers between devices: 14.5 us -> 115 us
  blocking collectives: 88.8 us -> 38.6 us
  other arithmetic: 48.8 us -> 16.5 us
    reduce_scatter x4 -> x0, waiting for transfers between devices: 486 us -> none  [the longest x1 192 us: local(): lax.psum_scatter(grad_fc2, 'ctx', scatter_dimension=0, tiled=True)]
    psum x1 -> x0, waiting for transfers between devices: 383 us -> none  [local(): lax.psum((share[0], share[1], share[2], share[3], share[4], share[5], sha...]
    pallas_call x0 -> x43, Pallas kernels: none -> 259 us  [the longest x24 72.5 us: add_split(): call(functools.partial(add_split_kernel, terms=len(arrays), slot=slot), (...]
    dot_general x18 -> x0, matrix products: 209 us -> none  [the longest x4 37.9 us: times_transposed(): lax.dot_general(left_mat, right_mat, (((1,), (1,)), ((), ())), preferred_...]
    ppermute x0 -> x100, waiting for transfers between devices: none -> 135 us  [the longest x88 108 us: swap(): return lax.ppermute(v, 'rows', [(i, i ^ stride) for i in range(n)])]
    ppermute x0 -> x100, starting transfers between devices: none -> 115 us  [the longest x88 100 us: swap(): return lax.ppermute(v, 'rows', [(i, i ^ stride) for i in range(n)])]
    all_to_all x3 -> x0, waiting for transfers between devices: 95.7 us -> none  [the longest x1 36.7 us: local(): lax.all_to_all(qkv_local, 'ctx', split_axis=3, concat_axis=1, tiled=True)]
    unnamed x116 -> x208, local copies, waits for them, and re-layouts: 56.7 us -> 8.45 us
  transfers between devices with their start and end apart: 10 -> 100, of which waited for: 8 -> 26; matrix products, arithmetic and copies ran while one was open for 12% -> 5% of each run, Pallas kernels for 0% -> 43%
where the time goes in v1:
time: 600 us; the launch traced here: 590 us
  Pallas kernels  259 us (43%)
  waiting for transfers between devices  135 us (22%)
  starting transfers between devices  115 us (19%)
  blocking collectives  38.6 us (6%)
  local copies, waits for them, and re-layouts  21.7 us (4%)
  other arithmetic  16.5 us (3%)
    ppermute x88, waiting for transfers between devices, swap(): return lax.ppermute(v, 'rows', [(i, i ^ stride) for i in range(n)])  108 us
    ppermute x88, starting transfers between devices, swap(): return lax.ppermute(v, 'rows', [(i, i ^ stride) for i in range(n)])  100 us
    pallas_call x24, Pallas kernels, add_split(): call(functools.partial(add_split_kernel, terms=len(arrays), slot=slot), (...  72.5 us
    pallas_call x8, Pallas kernels, wgrad(): call(wgrad_kernel, (2,), 1, [spec(a_at), spec(a_at), spec(b_at), spec(b_a...  46.2 us
    psum x1, blocking collectives, local(): small = lax.psum(small, ('rows', 'ctx'))  38.6 us
    pallas_call x1, Pallas kernels, ffn_bwd_call(): call(ffn_bwd_kernel, (8,), 1, [const_spec((t, d)), pl.BlockSpec((bw, d),...  29.3 us
    pallas_call x4, Pallas kernels, finish(): call(functools.partial(finish_kernel, pieces=pieces, slots=slots), (4 * l...  26.9 us
    ppermute x12, waiting for transfers between devices, swap_ctx(): return lax.ppermute(v, 'ctx', [(0, 1), (1, 0)])  26.7 us
  transfers between devices with their start and end apart: 100, of which 26 were waited for; matrix products, arithmetic and copies ran while one was open for 5% of the time, Pallas kernels for 43%

profile of v1, /device:TPU:0, one launch (start us, length us, event | category | flops | bytes accessed | tf_op | source)
XLA Modules:
  0.0 590.1 jit_solution(11149703063320922168)
XLA Ops:
  18.7 8.8 %shard_map.203 = (bf16[512,1024]{1,0:T(8,128)(2,1)}, bf16[3,512,1024]{2,1,0:T(8,128)(2,1)}) custom-call(s32[4]{0:T(128)} %pad_add_fusion.s, bf16[512,1024]{1,0:T(8,128)(2,1)} %pad_maximum_fusion.1.x, bf16[1024,3072]{1,0:T(8,128)(2,1)} %w.3, f32[1,1024]{1,0:T(1,128)} %slice.37.g, f32[1,1024]{1,0:T(1,128)} %slice.38.b), custom_call_target="tpu_custom_call" | custom-call | flops 3221225472 | bytes 11534336 | tf_op jit(solution)/shard_map/pallas_call | solution.py:84
  27.5 14.6 %shard_map.204 = (bf16[512,1024]{1,0:T(8,128)(2,1)}, f32[8,2,512]{2,1,0:T(2,128)}) custom-call(s32[4]{0:T(128)} %pad_add_fusion.s, bf16[3,512,1024]{2,1,0:T(8,128)(2,1)} %get-tuple-element.105.q.k.v, bf16[3,512,1024]{2,1,0:T(8,128)(2,1)} %get-tuple-element.105.q.k.v, bf16[3,512,1024]{2,1,0:T(8,128)(2,1)} %get-tuple-element.105.q.k.v, ...), custom_call_target="tpu_custom_call" | custom-call | flops 1073741824 | bytes 4194304 | tf_op jit(solution)/shard_map/pallas_call | solution.py:152
  43.2 22.7 %shard_map.205 = (f32[512,1024]{1,0:T(8,128)}, f32[512,1]{1,0:T(8,128)}, f32[512,1024]{1,0:T(8,128)}, f32[512,1]{1,0:T(8,128)}, bf16[512,1024]{1,0:T(8,128)(2,1)...) custom-call(s32[4]{0:T(128)} %pad_add_fusion.s, ...), custom_call_target="tpu_custom_call" | custom-call | flops 5368709120 | bytes 26214400 | tf_op jit(solution)/shard_map/pallas_call | solution.py:319
  66.0 29.3 %shard_map.207 = (bf16[2,512,1024]{2,1,0:T(8,128)(2,1)}, bf16[2,512,1024]{2,1,0:T(8,128)(2,1)}, f32[512,1024]{1,0:T(8,128)}, bf16[512,512]{1,0:T(8,128)(2,1)}, b...) custom-call(s32[4]{0:T(128)} %pad_add_fusion.s, ...), custom_call_target="tpu_custom_call" | custom-call | flops 9663676416 | bytes 39845888 | tf_op jit(solution)/shard_map/pallas_call | solution.py:480
  95.8 11.1 %shard_map.206 = bf16[512,1024]{1,0:T(8,128)(2,1)} custom-call(s32[4]{0:T(128)} %pad_add_fusion.s, bf16[2,512,1024]{2,1,0:T(8,128)(2,1)} %get-tuple-element.107.send, bf16[2,512,1024]{2,1,0:T(8,128)(2,1)} %get-tuple-element.108.keep.a0, bf16[4096,1024]{1,0:T(8,128)(2,1)} %w2.3, bf16[512,1024]{1,0:T(8,128)(2,1)} %pad_maximum_fusion.1.x, ...), custom_call_target="tpu_custom_call" | custom-call | flops 4294967296 | bytes 16777216 | tf_op jit(solution)/shard_map/pallas_call | solution.py:386
  110.9 14.3 %shard_map.208 = (bf16[3,512,512]{2,1,0:T(8,128)(2,1)}, bf16[3,512,512]{2,1,0:T(8,128)(2,1)}, f32[8,2,512]{2,1,0:T(2,128)}) custom-call(s32[4]{0:T(128)} %pad_add_fusion.s, bf16[3,512,1024]{2,1,0:T(8,128)(2,1)} %get-tuple-element.105.q.k.v, bf16[3,512,1024]{2,1,0:T(8,128)(2,1)} %get-tuple-element.105.q.k.v, bf16[3,512,1024]{2,1,0:T(8,128)(2,1)} %get-tuple-element.105.q.k.v, ...), custom_call_target="tpu_custom_call" | custom-call | flops 2684354560 | bytes 8388608 | tf_op jit(solution)/shard_map/pallas_call | solution.py:221
  125.7 4.8 shard_map.223
  130.5 12.5 %shard_map.209 = (f32[512,1024]{1,0:T(8,128)}, f32[1,1024]{1,0:T(1,128)}, f32[1,1024]{1,0:T(1,128)}) custom-call(s32[4]{0:T(128)} %pad_add_fusion.s, bf16[3,512,512]{2,1,0:T(8,128)(2,1)} %get-tuple-element.118.send, bf16[3,512,512]{2,1,0:T(8,128)(2,1)} %get-tuple-element.119.keep.b0, bf16[1024,3072]{1,0:T(8,128)(2,1)} %w.3, ...), custom_call_target="tpu_custom_call" | custom-call | flops 3221225472 | bytes 18874368 | tf_op jit(solution)/shard_map/pallas_call | solution.py:560
  151.4 7.8 %collective-permute-done.3 = bf16[256,1024]{1,0:T(8,128)(2,1)} collective-permute-done((bf16[256,1024]{1,0:T(8,128)(2,1)}, bf16[256,1024]{1,0:T(8,128)(2,1)}, u32[]{:S(2)}, u32[]{:S(2)}) %collective-permute-start.3) | collective-permute-done | bytes 524320 | tf_op jit(solution)/shard_map/ppermute | solution.py:652
  160.5 3.3 shard_map.225
  165.7 4.8 shard_map.210
  174.0 4.8 shard_map.214
  186.3 4.8 shard_map.218
  195.5 9.5 %collective-permute-done.17.refs_1_ = bf16[512,512]{1,0:T(8,128)(2,1)S(1)} collective-permute-done((bf16[512,512]{1,0:T(8,128)(2,1)}, bf16[512,512]{1,0:T(8,128)(2,1)S(1)}, u32[]{:S(2)}, u32[]{:S(2)}) %collective-permute-start.17) | collective-permute-done | bytes 524320 | tf_op jit(solution)/shard_map/ppermute | solution.py:652
  220.3 5.6 collective-permute-done.18.refs_1_
  227.5 3.3 shard_map.212
  241.6 6.8 %shard_map.228 = (bf16[512,1024]{1,0:T(8,128)(2,1)}, bf16[512,1024]{1,0:T(8,128)(2,1)}) custom-call(s32[4]{0:T(128)} %pad_add_fusion.s, bf16[512,1024]{1,0:T(8,128)(2,1)} %get-tuple-element.157.a0, bf16[512,1024]{1,0:T(8,128)(2,1)} %collective-permute-done.52.a1, bf16[2,512,1024]{2,1,0:T(8,128)(2,1)} %get-tuple-element.158.b0, ...), custom_call_target="tpu_custom_call" | custom-call | flops 2147483648 | bytes 8388608 | tf_op jit(solution)/shard_map/pallas_call | solution.py:596
  248.4 3.3 shard_map.220
  257.9 6.6 %shard_map.232 = (bf16[512,1024]{1,0:T(8,128)(2,1)}, bf16[512,1024]{1,0:T(8,128)(2,1)}) custom-call(s32[4]{0:T(128)} %pad_add_fusion.s, bf16[512,1024]{1,0:T(8,128)(2,1)} %get-tuple-element.157.a0, bf16[512,1024]{1,0:T(8,128)(2,1)} %collective-permute-done.52.a1, bf16[2,512,1024]{2,1,0:T(8,128)(2,1)} %get-tuple-element.158.b0, ...), custom_call_target="tpu_custom_call" | custom-call | flops 2147483648 | bytes 8388608 | tf_op jit(solution)/shard_map/pallas_call | solution.py:596
  271.3 7.1 %shard_map.237 = (bf16[512,1024]{1,0:T(8,128)(2,1)}, bf16[512,1024]{1,0:T(8,128)(2,1)}) custom-call(s32[4]{0:T(128)} %pad_add_fusion.s, bf16[2,512,1024]{2,1,0:T(8,128)(2,1)} %get-tuple-element.108.keep.a0, bf16[2,512,1024]{2,1,0:T(8,128)(2,1)} %collective-permute-done.76.a1, bf16[512,1024]{1,0:T(8,128)(2,1)} %pad_maximum_fusion.3.cot.b0, ...), custom_call_target="tpu_custom_call" | custom-call | flops 2147483648 | bytes 8388608 | tf_op jit(solution)/shard_map/pallas_call | solution.py:596
  281.8 6.6 %shard_map.241 = (bf16[512,1024]{1,0:T(8,128)(2,1)}, bf16[512,1024]{1,0:T(8,128)(2,1)}) custom-call(s32[4]{0:T(128)} %pad_add_fusion.s, bf16[2,512,1024]{2,1,0:T(8,128)(2,1)} %get-tuple-element.108.keep.a0, bf16[2,512,1024]{2,1,0:T(8,128)(2,1)} %collective-permute-done.76.a1, bf16[512,1024]{1,0:T(8,128)(2,1)} %pad_maximum_fusion.3.cot.b0, ...), custom_call_target="tpu_custom_call" | custom-call | flops 2147483648 | bytes 8388608 | tf_op jit(solution)/shard_map/pallas_call | solution.py:596
  293.9 3.7 collective-permute-done.24
  297.6 6.0 %collective-permute-done.23 = bf16[64,512]{1,0:T(8,128)(2,1)S(1)} collective-permute-done((bf16[64,512]{1,0:T(8,128)(2,1)}, bf16[64,512]{1,0:T(8,128)(2,1)S(1)}, u32[]{:S(2)}, u32[]{:S(2)}) %collective-permute-start.23) | collective-permute-done | bytes 65568 | tf_op jit(solution)/shard_map/ppermute | solution.py:648
  310.6 4.5 collective-permute-done.35
  316.0 4.6 collective-permute-done.34
  322.1 3.5 shard_map.229
  330.7 3.4 shard_map.233
  338.3 3.6 shard_map.238
  341.9 3.7 shard_map.242
  352.3 3.9 shard_map.230
  356.1 3.6 collective-permute-done.66.refs_1_
  359.8 3.7 shard_map.234
  363.5 22.4 %collective-permute-done.36.refs_9_ = bf16[256,512]{1,0:T(8,128)(2,1)S(1)} collective-permute-done((bf16[256,512]{1,0:T(8,128)(2,1)S(1)}, bf16[256,512]{1,0:T(8,128)(2,1)S(1)}, u32[]{:S(2)}, u32[]{:S(2)}) %collective-permute-start.36) | collective-permute-done | bytes 262176 | tf_op jit(solution)/shard_map/ppermute | solution.py:648
  393.7 3.7 shard_map.239
  397.4 3.7 shard_map.243
  402.9 7.5 %collective-permute-start.81 = (bf16[64,1024]{1,0:T(8,128)(2,1)}, bf16[64,1024]{1,0:T(8,128)(2,1)S(1)}, u32[]{:S(2)}, u32[]{:S(2)}) collective-permute-start(bf16[64,1024]{1,0:T(8,128)(2,1)} %get-tuple-element.182), channel_id=1, source_target_pairs={{0,16},{2,18},{4,20},{6,22},{8,24},{10,26},{12,28},{14,30},{16,0},... | collective-permute-start | bytes 393224 | tf_op jit(solution)/shard_map/ppermute | solution.py:648
  412.5 7.7 %collective-permute-start.92 = (bf16[64,1024]{1,0:T(8,128)(2,1)}, bf16[64,1024]{1,0:T(8,128)(2,1)S(1)}, u32[]{:S(2)}, u32[]{:S(2)}) collective-permute-start(bf16[64,1024]{1,0:T(8,128)(2,1)} %get-tuple-element.190), channel_id=1, source_target_pairs={{0,16},{2,18},{4,20},{6,22},{8,24},{10,26},{12,28},{14,30},{16,0},... | collective-permute-start | bytes 393224 | tf_op jit(solution)/shard_map/ppermute | solution.py:648
  433.6 6.9 %collective-permute-done.92.refs_2_ = bf16[64,1024]{1,0:T(8,128)(2,1)S(1)} collective-permute-done((bf16[64,1024]{1,0:T(8,128)(2,1)}, bf16[64,1024]{1,0:T(8,128)(2,1)S(1)}, u32[]{:S(2)}, u32[]{:S(2)}) %collective-permute-start.92) | collective-permute-done | bytes 131104 | tf_op jit(solution)/shard_map/ppermute | solution.py:648
  447.4 7.1 %collective-permute-done.60 = bf16[64,1024]{1,0:T(8,128)(2,1)S(1)} collective-permute-done((bf16[64,1024]{1,0:T(8,128)(2,1)}, bf16[64,1024]{1,0:T(8,128)(2,1)S(1)}, u32[]{:S(2)}, u32[]{:S(2)}) %collective-permute-start.60) | collective-permute-done | bytes 131104 | tf_op jit(solution)/shard_map/ppermute | solution.py:648
  459.0 38.6 %psum.7 = f32[14352]{0:T(1024)S(1)} all-reduce(f32[14352]{0:T(1024)S(1)} %constant_dynamic-update-slice_fusion), channel_id=1, replica_groups=mesh['rows'=16,'ctx'=2] {'rows','ctx'}, use_global_device_ids=true, to_apply=%region_1.2 | all-reduce | flops 14352 | bytes 114816 | tf_op jit(solution)/shard_map/psum | solution.py:830
  509.8 6.0 %collective-permute-done.95 = bf16[64,1024]{1,0:T(8,128)(2,1)S(1)} collective-permute-done((bf16[64,1024]{1,0:T(8,128)(2,1)}, bf16[64,1024]{1,0:T(8,128)(2,1)S(1)}, u32[]{:S(2)}, u32[]{:S(2)}) %collective-permute-start.95) | collective-permute-done | bytes 131104 | tf_op jit(solution)/shard_map/ppermute | solution.py:648
  528.7 5.3 collective-permute-done.73.refs_5_
  534.5 10.7 %collective-permute-done.86.refs_1_ = bf16[256,1024]{1,0:T(8,128)(2,1)} collective-permute-done((bf16[256,1024]{1,0:T(8,128)(2,1)S(1)}, bf16[256,1024]{1,0:T(8,128)(2,1)}, u32[]{:S(2)}, u32[]{:S(2)}) %collective-permute-start.86) | collective-permute-done | bytes 524320 | tf_op jit(solution)/shard_map/ppermute | solution.py:648
  545.2 10.6 %collective-permute-done.97.refs_5_ = bf16[256,1024]{1,0:T(8,128)(2,1)} collective-permute-done((bf16[256,1024]{1,0:T(8,128)(2,1)S(1)}, bf16[256,1024]{1,0:T(8,128)(2,1)}, u32[]{:S(2)}, u32[]{:S(2)}) %collective-permute-start.97) | collective-permute-done | bytes 524320 | tf_op jit(solution)/shard_map/ppermute | solution.py:648
  560.3 3.8 shard_map.227
  564.0 8.0 %shard_map.222 = f32[512,3072]{1,0:T(8,128)} custom-call(s32[4]{0:T(128)} %pad_add_fusion.s, bf16[256,512]{1,0:T(8,128)(2,1)} %copy-done.14, bf16[256,512]{1,0:T(8,128)(2,1)} %copy-done.36, bf16[256,512]{1,0:T(8,128)(2,1)} %copy-done.38, bf16[256,512]{1,0:T(8,128)(2,1)} %copy-done.42, bf16[256,512]{1,0:T(8,128)(2,1)} %copy-done.15, ...), custom_call_target="tpu_custom_call" | custom-call | flops 3145728 | bytes 9437184 | tf_op jit(solution)/shard_map/pallas_call | solution.py:720
  572.8 7.5 %shard_map.236 = f32[512,4096]{1,0:T(8,128)} custom-call(s32[4]{0:T(128)} %pad_add_fusion.s, bf16[256,1024]{1,0:T(8,128)(2,1)} %copy-done.6, bf16[256,1024]{1,0:T(8,128)(2,1)} %collective-permute-done.62.refs_1_, bf16[256,1024]{1,0:T(8,128)(2,1)} %copy-done.20, bf16[256,1024]{1,0:T(8,128)(2,1)} %collective-permute-done.64.refs_3_, ...), custom_call_target="tpu_custom_call" | custom-call | flops 4194304 | bytes 12582912 | tf_op jit(solution)/shard_map/pallas_call | solution.py:720
  582.3 7.6 %shard_map.245 = f32[2048,1024]{1,0:T(8,128)} custom-call(s32[4]{0:T(128)} %pad_add_fusion.s, bf16[256,1024]{1,0:T(8,128)(2,1)} %copy-done.7, bf16[256,1024]{1,0:T(8,128)(2,1)} %collective-permute-done.86.refs_1_, bf16[256,1024]{1,0:T(8,128)(2,1)} %copy-done.21, bf16[256,1024]{1,0:T(8,128)(2,1)} %copy-done.23, bf16[256,1024]{1,0:T(8,128)(2,1)} %copy-done.8, ...), custom_call_target="tpu_custom_call" | custom-call | flops 4194304 | bytes 12582912 | tf_op jit(solution)/shard_map/pallas_call | solution.py:720
  (448 shorter events, 192.1 us)
Async XLA Ops:
  5.9 36.1 %collective-permute-start.2 = (bf16[256,1024]{1,0:T(8,128)(2,1)S(1)}, bf16[256,1024]{1,0:T(8,128)(2,1)S(1)}, u32[]{:S(2)}, u32[]{:S(2)}) collective-permute-start(bf16[256,1024]{1,0:T(8,128)(2,1)S(1)} %dynamic-slice_bitcast_fusion), channel_id=1, source_target_pairs={{0,1},{1,0},{2,3},{3,2},{4,5},{5,4},{6,7},{7,6},{8,9},{9,8},{10,11... | collective-permute-start | bytes 1572872 | tf_op jit(solution)/shard_map/ppermute | solution.py:652
  42.1 83.7 %collective-permute-start.39 = (bf16[512,1024]{1,0:T(8,128)(2,1)}, bf16[512,1024]{1,0:T(8,128)(2,1)}, u32[]{:S(2)}, u32[]{:S(2)}) collective-permute-start(bf16[512,1024]{1,0:T(8,128)(2,1)} %get-tuple-element.106.sent.a0), channel_id=1, source_target_pairs={{0,2},{2,0},{4,6},{6,4},{8,10},{10,8},{12,14},{14,12},{16,18},{18,... | collective-permute-start | bytes 3145736 | tf_op jit(solution)/shard_map/ppermute | solution.py:648
  95.3 30.4 %collective-permute-start.40 = (bf16[512,512]{1,0:T(8,128)(2,1)}, bf16[512,512]{1,0:T(8,128)(2,1)}, u32[]{:S(2)}, u32[]{:S(2)}) collective-permute-start(bf16[512,512]{1,0:T(8,128)(2,1)} %get-tuple-element.148), channel_id=1, source_target_pairs={{0,2},{2,0},{4,6},{6,4},{8,10},{10,8},{12,14},{14,12},{16,18},{18,... | collective-permute-start | bytes 1572872 | tf_op jit(solution)/shard_map/ppermute | solution.py:648
  108.8 41.1 %collective-permute-start.1 = (bf16[256,1024]{1,0:T(8,128)(2,1)}, bf16[256,1024]{1,0:T(8,128)(2,1)}, u32[]{:S(2)}, u32[]{:S(2)}) collective-permute-start(bf16[256,1024]{1,0:T(8,128)(2,1)} %constant_dynamic-slice_fusion.2), channel_id=1, source_target_pairs={{0,1},{1,0},{2,3},{3,2},{4,5},{5,4},{6,7},{7,6},{8,9},{9,8},{10,11... | collective-permute-start | bytes 1572872 | tf_op jit(solution)/shard_map/ppermute | solution.py:652
  110.9 48.4 %collective-permute-start.4 = (bf16[512,1024]{1,0:T(8,128)(2,1)S(1)}, bf16[512,1024]{1,0:T(8,128)(2,1)S(1)}, u32[]{:S(2)}, u32[]{:S(2)}) collective-permute-start(bf16[512,1024]{1,0:T(8,128)(2,1)S(1)} %copy-done.3), channel_id=1, source_target_pairs={{0,2},{2,0},{4,6},{6,4},{8,10},{10,8},{12,14},{14,12},{16,18},{18,... | collective-permute-start | bytes 3145736 | tf_op jit(solution)/shard_map/ppermute | solution.py:648
  125.2 38.6 %collective-permute-start.5 = (bf16[3,512,512]{2,1,0:T(8,128)(2,1)}, bf16[3,512,512]{2,1,0:T(8,128)(2,1)S(1)}, u32[]{:S(2)}, u32[]{:S(2)}) collective-permute-start(bf16[3,512,512]{2,1,0:T(8,128)(2,1)} %get-tuple-element.118.send), channel_id=1, source_target_pairs={{0,2},{2,0},{4,6},{6,4},{8,10},{10,8},{12,14},{14,12},{16,18},{18,... | collective-permute-start | bytes 4718600 | tf_op jit(solution)/shard_map/ppermute | solution.py:648
  147.1 23.3 %collective-permute-start.52 = (bf16[512,1024]{1,0:T(8,128)(2,1)}, bf16[512,1024]{1,0:T(8,128)(2,1)}, u32[]{:S(2)}, u32[]{:S(2)}) collective-permute-start(bf16[512,1024]{1,0:T(8,128)(2,1)} %get-tuple-element.157.a0), channel_id=1, source_target_pairs={{0,2},{2,0},{4,6},{6,4},{8,10},{10,8},{12,14},{14,12},{16,18},{18,... | collective-permute-start | bytes 3145736 | tf_op jit(solution)/shard_map/ppermute | solution.py:648
  159.3 74.8 %collective-permute-start.53 = (bf16[2,512,1024]{2,1,0:T(8,128)(2,1)}, bf16[2,512,1024]{2,1,0:T(8,128)(2,1)}, u32[]{:S(2)}, u32[]{:S(2)}) collective-permute-start(bf16[2,512,1024]{2,1,0:T(8,128)(2,1)} %get-tuple-element.159), channel_id=1, source_target_pairs={{0,2},{2,0},{4,6},{6,4},{8,10},{10,8},{12,14},{14,12},{16,18},{18,... | collective-permute-start | bytes 6291464 | tf_op jit(solution)/shard_map/ppermute | solution.py:648
  159.3 76.3 %collective-permute-start.76 = (bf16[2,512,1024]{2,1,0:T(8,128)(2,1)}, bf16[2,512,1024]{2,1,0:T(8,128)(2,1)}, u32[]{:S(2)}, u32[]{:S(2)}) collective-permute-start(bf16[2,512,1024]{2,1,0:T(8,128)(2,1)} %get-tuple-element.107.send), channel_id=1, source_target_pairs={{0,2},{2,0},{4,6},{6,4},{8,10},{10,8},{12,14},{14,12},{16,18},{18,... | collective-permute-start | bytes 6291464 | tf_op jit(solution)/shard_map/ppermute | solution.py:648
  159.8 23.5 %collective-permute-start.77 = (bf16[512,1024]{1,0:T(8,128)(2,1)}, bf16[512,1024]{1,0:T(8,128)(2,1)}, u32[]{:S(2)}, u32[]{:S(2)}) collective-permute-start(bf16[512,1024]{1,0:T(8,128)(2,1)} %pad_maximum_fusion.3.cot.b0), channel_id=1, source_target_pairs={{0,2},{2,0},{4,6},{6,4},{8,10},{10,8},{12,14},{14,12},{16,18},{18,... | collective-permute-start | bytes 3145736 | tf_op jit(solution)/shard_map/ppermute | solution.py:648
  180.4 24.6 %collective-permute-start.17 = (bf16[512,512]{1,0:T(8,128)(2,1)}, bf16[512,512]{1,0:T(8,128)(2,1)S(1)}, u32[]{:S(2)}, u32[]{:S(2)}) collective-permute-start(bf16[512,512]{1,0:T(8,128)(2,1)} %get-tuple-element.132), channel_id=1, source_target_pairs={{0,1},{1,0},{2,3},{3,2},{4,5},{5,4},{6,7},{7,6},{8,9},{9,8},{10,11... | collective-permute-start | bytes 1572872 | tf_op jit(solution)/shard_map/ppermute | solution.py:652
  191.1 23.7 %collective-permute-start.28 = (bf16[512,512]{1,0:T(8,128)(2,1)}, bf16[512,512]{1,0:T(8,128)(2,1)S(1)}, u32[]{:S(2)}, u32[]{:S(2)}) collective-permute-start(bf16[512,512]{1,0:T(8,128)(2,1)} %get-tuple-element.140), channel_id=1, source_target_pairs={{0,1},{1,0},{2,3},{3,2},{4,5},{5,4},{6,7},{7,6},{8,9},{9,8},{10,11... | collective-permute-start | bytes 1572872 | tf_op jit(solution)/shard_map/ppermute | solution.py:652
  214.8 22.4 %collective-permute-start.49 = (bf16[256,512]{1,0:T(8,128)(2,1)S(1)}, bf16[256,512]{1,0:T(8,128)(2,1)S(1)}, u32[]{:S(2)}, u32[]{:S(2)}) collective-permute-start(bf16[256,512]{1,0:T(8,128)(2,1)S(1)} %pad_maximum_fusion.11.refs_0_), channel_id=1, source_target_pairs={{0,4},{2,6},{4,0},{6,2},{8,12},{10,14},{12,8},{14,10},{16,20},{18,... | collective-permute-start | bytes 786440 | tf_op jit(solution)/shard_map/ppermute | solution.py:648
  251.7 69.4 %collective-permute-start.54 = (bf16[512,1024]{1,0:T(8,128)(2,1)}, bf16[512,1024]{1,0:T(8,128)(2,1)S(1)}, u32[]{:S(2)}, u32[]{:S(2)}) collective-permute-start(bf16[512,1024]{1,0:T(8,128)(2,1)} %get-tuple-element.161), channel_id=1, source_target_pairs={{0,1},{1,0},{2,3},{3,2},{4,5},{5,4},{6,7},{7,6},{8,9},{9,8},{10,11... | collective-permute-start | bytes 3145736 | tf_op jit(solution)/shard_map/ppermute | solution.py:652
  253.3 26.6 %collective-permute-start.51 = (bf16[256,512]{1,0:T(8,128)(2,1)S(1)}, bf16[256,512]{1,0:T(8,128)(2,1)S(1)}, u32[]{:S(2)}, u32[]{:S(2)}) collective-permute-start(bf16[256,512]{1,0:T(8,128)(2,1)S(1)} %collective-permute-done.49.refs_1_), channel_id=1, source_target_pairs={{0,2},{2,0},{4,6},{6,4},{8,10},{10,8},{12,14},{14,12},{16,18},{18,... | collective-permute-start | bytes 786440 | tf_op jit(solution)/shard_map/ppermute | solution.py:648
  266.8 62.3 %collective-permute-start.65 = (bf16[512,1024]{1,0:T(8,128)(2,1)}, bf16[512,1024]{1,0:T(8,128)(2,1)S(1)}, u32[]{:S(2)}, u32[]{:S(2)}) collective-permute-start(bf16[512,1024]{1,0:T(8,128)(2,1)} %get-tuple-element.169), channel_id=1, source_target_pairs={{0,1},{1,0},{2,3},{3,2},{4,5},{5,4},{6,7},{7,6},{8,9},{9,8},{10,11... | collective-permute-start | bytes 3145736 | tf_op jit(solution)/shard_map/ppermute | solution.py:652
  278.4 55.8 %collective-permute-start.78 = (bf16[512,1024]{1,0:T(8,128)(2,1)}, bf16[512,1024]{1,0:T(8,128)(2,1)S(1)}, u32[]{:S(2)}, u32[]{:S(2)}) collective-permute-start(bf16[512,1024]{1,0:T(8,128)(2,1)} %get-tuple-element.177), channel_id=1, source_target_pairs={{0,1},{1,0},{2,3},{3,2},{4,5},{5,4},{6,7},{7,6},{8,9},{9,8},{10,11... | collective-permute-start | bytes 3145736 | tf_op jit(solution)/shard_map/ppermute | solution.py:652
  288.5 49.8 %collective-permute-start.89 = (bf16[512,1024]{1,0:T(8,128)(2,1)}, bf16[512,1024]{1,0:T(8,128)(2,1)}, u32[]{:S(2)}, u32[]{:S(2)}) collective-permute-start(bf16[512,1024]{1,0:T(8,128)(2,1)} %get-tuple-element.185), channel_id=1, source_target_pairs={{0,1},{1,0},{2,3},{3,2},{4,5},{5,4},{6,7},{7,6},{8,9},{9,8},{10,11... | collective-permute-start | bytes 3145736 | tf_op jit(solution)/shard_map/ppermute | solution.py:652
  325.7 19.8 %collective-permute-start.15 = (bf16[256,512]{1,0:T(8,128)(2,1)S(1)}, bf16[256,512]{1,0:T(8,128)(2,1)S(1)}, u32[]{:S(2)}, u32[]{:S(2)}) collective-permute-start(bf16[256,512]{1,0:T(8,128)(2,1)S(1)} %pad_maximum_fusion.8.refs_0_), channel_id=1, source_target_pairs={{0,2},{2,0},{4,6},{6,4},{8,10},{10,8},{12,14},{14,12},{16,18},{18,... | collective-permute-start | bytes 786440 | tf_op jit(solution)/shard_map/ppermute | solution.py:648
  327.7 23.8 %collective-permute-start.55 = (bf16[256,1024]{1,0:T(8,128)(2,1)}, bf16[256,1024]{1,0:T(8,128)(2,1)S(1)}, u32[]{:S(2)}, u32[]{:S(2)}) collective-permute-start(bf16[256,1024]{1,0:T(8,128)(2,1)} %get-tuple-element.163), channel_id=1, source_target_pairs={{0,4},{2,6},{4,0},{6,2},{8,12},{10,14},{12,8},{14,10},{16,20},{18,... | collective-permute-start | bytes 1572872 | tf_op jit(solution)/shard_map/ppermute | solution.py:648
  334.1 25.5 %collective-permute-start.66 = (bf16[256,1024]{1,0:T(8,128)(2,1)}, bf16[256,1024]{1,0:T(8,128)(2,1)}, u32[]{:S(2)}, u32[]{:S(2)}) collective-permute-start(bf16[256,1024]{1,0:T(8,128)(2,1)} %get-tuple-element.171), channel_id=1, source_target_pairs={{0,4},{2,6},{4,0},{6,2},{8,12},{10,14},{12,8},{14,10},{16,20},{18,... | collective-permute-start | bytes 1572872 | tf_op jit(solution)/shard_map/ppermute | solution.py:648
  345.5 43.7 %collective-permute-start.79 = (bf16[256,1024]{1,0:T(8,128)(2,1)}, bf16[256,1024]{1,0:T(8,128)(2,1)S(1)}, u32[]{:S(2)}, u32[]{:S(2)}) collective-permute-start(bf16[256,1024]{1,0:T(8,128)(2,1)} %get-tuple-element.179), channel_id=1, source_target_pairs={{0,4},{2,6},{4,0},{6,2},{8,12},{10,14},{12,8},{14,10},{16,20},{18,... | collective-permute-start | bytes 1572872 | tf_op jit(solution)/shard_map/ppermute | solution.py:648
  348.5 40.9 %collective-permute-start.90 = (bf16[256,1024]{1,0:T(8,128)(2,1)}, bf16[256,1024]{1,0:T(8,128)(2,1)S(1)}, u32[]{:S(2)}, u32[]{:S(2)}) collective-permute-start(bf16[256,1024]{1,0:T(8,128)(2,1)} %get-tuple-element.187), channel_id=1, source_target_pairs={{0,4},{2,6},{4,0},{6,2},{8,12},{10,14},{12,8},{14,10},{16,20},{18,... | collective-permute-start | bytes 1572872 | tf_op jit(solution)/shard_map/ppermute | solution.py:648
  349.8 36.1 %collective-permute-start.36 = (bf16[256,512]{1,0:T(8,128)(2,1)S(1)}, bf16[256,512]{1,0:T(8,128)(2,1)S(1)}, u32[]{:S(2)}, u32[]{:S(2)}) collective-permute-start(bf16[256,512]{1,0:T(8,128)(2,1)S(1)} %pad_maximum_fusion.10.refs_8_), channel_id=1, source_target_pairs={{0,4},{2,6},{4,0},{6,2},{8,12},{10,14},{12,8},{14,10},{16,20},{18,... | collective-permute-start | bytes 786440 | tf_op jit(solution)/shard_map/ppermute | solution.py:648
  351.5 35.7 %collective-permute-start.37 = (bf16[256,512]{1,0:T(8,128)(2,1)S(1)}, bf16[256,512]{1,0:T(8,128)(2,1)S(1)}, u32[]{:S(2)}, u32[]{:S(2)}) collective-permute-start(bf16[256,512]{1,0:T(8,128)(2,1)S(1)} %pad_maximum_fusion.10.refs_8_), channel_id=1, source_target_pairs={{0,2},{2,0},{4,6},{6,4},{8,10},{10,8},{12,14},{14,12},{16,18},{18,... | collective-permute-start | bytes 786440 | tf_op jit(solution)/shard_map/ppermute | solution.py:648
  359.7 31.9 %collective-permute-start.56 = (bf16[64,1024]{1,0:T(8,128)(2,1)}, bf16[64,1024]{1,0:T(8,128)(2,1)S(1)}, u32[]{:S(2)}, u32[]{:S(2)}) collective-permute-start(bf16[64,1024]{1,0:T(8,128)(2,1)} %get-tuple-element.165), channel_id=1, source_target_pairs={{0,8},{2,10},{4,12},{6,14},{8,0},{10,2},{12,4},{14,6},{16,24},{18,... | collective-permute-start | bytes 393224 | tf_op jit(solution)/shard_map/ppermute | solution.py:648
  389.2 21.2 %collective-permute-start.67 = (bf16[64,1024]{1,0:T(8,128)(2,1)}, bf16[64,1024]{1,0:T(8,128)(2,1)S(1)}, u32[]{:S(2)}, u32[]{:S(2)}) collective-permute-start(bf16[64,1024]{1,0:T(8,128)(2,1)} %get-tuple-element.173), channel_id=1, source_target_pairs={{0,8},{2,10},{4,12},{6,14},{8,0},{10,2},{12,4},{14,6},{16,24},{18,... | collective-permute-start | bytes 393224 | tf_op jit(solution)/shard_map/ppermute | solution.py:648
  389.4 23.1 %collective-permute-start.68 = (bf16[64,1024]{1,0:T(8,128)(2,1)}, bf16[64,1024]{1,0:T(8,128)(2,1)S(1)}, u32[]{:S(2)}, u32[]{:S(2)}) collective-permute-start(bf16[64,1024]{1,0:T(8,128)(2,1)} %get-tuple-element.174), channel_id=1, source_target_pairs={{0,16},{2,18},{4,20},{6,22},{8,24},{10,26},{12,28},{14,30},{16,0},... | collective-permute-start | bytes 393224 | tf_op jit(solution)/shard_map/ppermute | solution.py:648
  391.6 20.9 %collective-permute-start.69 = (bf16[64,1024]{1,0:T(8,128)(2,1)}, bf16[64,1024]{1,0:T(8,128)(2,1)S(1)}, u32[]{:S(2)}, u32[]{:S(2)}) collective-permute-start(bf16[64,1024]{1,0:T(8,128)(2,1)} %get-tuple-element.175), channel_id=1, source_target_pairs={{0,24},{2,26},{4,28},{6,30},{8,16},{10,18},{12,20},{14,22},{16,8},... | collective-permute-start | bytes 393224 | tf_op jit(solution)/shard_map/ppermute | solution.py:648
  402.8 24.2 %collective-permute-start.80 = (bf16[64,1024]{1,0:T(8,128)(2,1)}, bf16[64,1024]{1,0:T(8,128)(2,1)S(1)}, u32[]{:S(2)}, u32[]{:S(2)}) collective-permute-start(bf16[64,1024]{1,0:T(8,128)(2,1)} %get-tuple-element.181), channel_id=1, source_target_pairs={{0,8},{2,10},{4,12},{6,14},{8,0},{10,2},{12,4},{14,6},{16,24},{18,... | collective-permute-start | bytes 393224 | tf_op jit(solution)/shard_map/ppermute | solution.py:648
  402.9 26.3 %collective-permute-start.81 = (bf16[64,1024]{1,0:T(8,128)(2,1)}, bf16[64,1024]{1,0:T(8,128)(2,1)S(1)}, u32[]{:S(2)}, u32[]{:S(2)}) collective-permute-start(bf16[64,1024]{1,0:T(8,128)(2,1)} %get-tuple-element.182), channel_id=1, source_target_pairs={{0,16},{2,18},{4,20},{6,22},{8,24},{10,26},{12,28},{14,30},{16,0},... | collective-permute-start | bytes 393224 | tf_op jit(solution)/shard_map/ppermute | solution.py:648
  410.4 20.5 %collective-permute-start.82 = (bf16[64,1024]{1,0:T(8,128)(2,1)}, bf16[64,1024]{1,0:T(8,128)(2,1)S(1)}, u32[]{:S(2)}, u32[]{:S(2)}) collective-permute-start(bf16[64,1024]{1,0:T(8,128)(2,1)} %get-tuple-element.183), channel_id=1, source_target_pairs={{0,24},{2,26},{4,28},{6,30},{8,16},{10,18},{12,20},{14,22},{16,8},... | collective-permute-start | bytes 393224 | tf_op jit(solution)/shard_map/ppermute | solution.py:648
  412.5 28.0 %collective-permute-start.92 = (bf16[64,1024]{1,0:T(8,128)(2,1)}, bf16[64,1024]{1,0:T(8,128)(2,1)S(1)}, u32[]{:S(2)}, u32[]{:S(2)}) collective-permute-start(bf16[64,1024]{1,0:T(8,128)(2,1)} %get-tuple-element.190), channel_id=1, source_target_pairs={{0,16},{2,18},{4,20},{6,22},{8,24},{10,26},{12,28},{14,30},{16,0},... | collective-permute-start | bytes 393224 | tf_op jit(solution)/shard_map/ppermute | solution.py:648
  431.0 23.6 %collective-permute-start.60 = (bf16[64,1024]{1,0:T(8,128)(2,1)}, bf16[64,1024]{1,0:T(8,128)(2,1)S(1)}, u32[]{:S(2)}, u32[]{:S(2)}) collective-permute-start(bf16[64,1024]{1,0:T(8,128)(2,1)} %shard_map.231), channel_id=1, source_target_pairs={{0,16},{2,18},{4,20},{6,22},{8,24},{10,26},{12,28},{14,30},{16,0},... | collective-permute-start | bytes 393224 | tf_op jit(solution)/shard_map/ppermute | solution.py:648
  431.5 24.8 %collective-permute-start.59 = (bf16[64,1024]{1,0:T(8,128)(2,1)}, bf16[64,1024]{1,0:T(8,128)(2,1)S(1)}, u32[]{:S(2)}, u32[]{:S(2)}) collective-permute-start(bf16[64,1024]{1,0:T(8,128)(2,1)} %shard_map.231), channel_id=1, source_target_pairs={{0,8},{2,10},{4,12},{6,14},{8,0},{10,2},{12,4},{14,6},{16,24},{18,... | collective-permute-start | bytes 393224 | tf_op jit(solution)/shard_map/ppermute | solution.py:648
  444.8 56.6 %collective-permute-start.71 = (bf16[64,1024]{1,0:T(8,128)(2,1)}, bf16[64,1024]{1,0:T(8,128)(2,1)S(1)}, u32[]{:S(2)}, u32[]{:S(2)}) collective-permute-start(bf16[64,1024]{1,0:T(8,128)(2,1)} %shard_map.235), channel_id=1, source_target_pairs={{0,16},{2,18},{4,20},{6,22},{8,24},{10,26},{12,28},{14,30},{16,0},... | collective-permute-start | bytes 393224 | tf_op jit(solution)/shard_map/ppermute | solution.py:648
  444.9 58.5 %collective-permute-start.70 = (bf16[64,1024]{1,0:T(8,128)(2,1)}, bf16[64,1024]{1,0:T(8,128)(2,1)S(1)}, u32[]{:S(2)}, u32[]{:S(2)}) collective-permute-start(bf16[64,1024]{1,0:T(8,128)(2,1)} %shard_map.235), channel_id=1, source_target_pairs={{0,8},{2,10},{4,12},{6,14},{8,0},{10,2},{12,4},{14,6},{16,24},{18,... | collective-permute-start | bytes 393224 | tf_op jit(solution)/shard_map/ppermute | solution.py:648
  454.5 50.3 %collective-permute-start.85 = (bf16[64,1024]{1,0:T(8,128)(2,1)}, bf16[64,1024]{1,0:T(8,128)(2,1)S(1)}, u32[]{:S(2)}, u32[]{:S(2)}) collective-permute-start(bf16[64,1024]{1,0:T(8,128)(2,1)} %shard_map.240), channel_id=1, source_target_pairs={{0,24},{2,26},{4,28},{6,30},{8,16},{10,18},{12,20},{14,22},{16,8},... | collective-permute-start | bytes 393224 | tf_op jit(solution)/shard_map/ppermute | solution.py:648
  456.3 49.5 %collective-permute-start.84 = (bf16[64,1024]{1,0:T(8,128)(2,1)}, bf16[64,1024]{1,0:T(8,128)(2,1)S(1)}, u32[]{:S(2)}, u32[]{:S(2)}) collective-permute-start(bf16[64,1024]{1,0:T(8,128)(2,1)} %shard_map.240), channel_id=1, source_target_pairs={{0,16},{2,18},{4,20},{6,22},{8,24},{10,26},{12,28},{14,30},{16,0},... | collective-permute-start | bytes 393224 | tf_op jit(solution)/shard_map/ppermute | solution.py:648
  457.0 51.1 %collective-permute-start.83 = (bf16[64,1024]{1,0:T(8,128)(2,1)}, bf16[64,1024]{1,0:T(8,128)(2,1)S(1)}, u32[]{:S(2)}, u32[]{:S(2)}) collective-permute-start(bf16[64,1024]{1,0:T(8,128)(2,1)} %shard_map.240), channel_id=1, source_target_pairs={{0,8},{2,10},{4,12},{6,14},{8,0},{10,2},{12,4},{14,6},{16,24},{18,... | collective-permute-start | bytes 393224 | tf_op jit(solution)/shard_map/ppermute | solution.py:648
  521.2 24.0 %collective-permute-start.86 = (bf16[256,1024]{1,0:T(8,128)(2,1)S(1)}, bf16[256,1024]{1,0:T(8,128)(2,1)}, u32[]{:S(2)}, u32[]{:S(2)}) collective-permute-start(bf16[256,1024]{1,0:T(8,128)(2,1)S(1)} %pad_maximum_fusion.6.refs_0_), channel_id=1, source_target_pairs={{0,4},{2,6},{4,0},{6,2},{8,12},{10,14},{12,8},{14,10},{16,20},{18,... | collective-permute-start | bytes 1572872 | tf_op jit(solution)/shard_map/ppermute | solution.py:648
  521.4 34.5 %collective-permute-start.97 = (bf16[256,1024]{1,0:T(8,128)(2,1)S(1)}, bf16[256,1024]{1,0:T(8,128)(2,1)}, u32[]{:S(2)}, u32[]{:S(2)}) collective-permute-start(bf16[256,1024]{1,0:T(8,128)(2,1)S(1)} %pad_maximum_fusion.7.refs_4_), channel_id=1, source_target_pairs={{0,4},{2,6},{4,0},{6,2},{8,12},{10,14},{12,8},{14,10},{16,20},{18,... | collective-permute-start | bytes 1572872 | tf_op jit(solution)/shard_map/ppermute | solution.py:648
  524.1 31.7 %collective-permute-start.64 = (bf16[256,1024]{1,0:T(8,128)(2,1)}, bf16[256,1024]{1,0:T(8,128)(2,1)}, u32[]{:S(2)}, u32[]{:S(2)}) collective-permute-start(bf16[256,1024]{1,0:T(8,128)(2,1)} %collective-permute-done.62.refs_1_), channel_id=1, source_target_pairs={{0,2},{2,0},{4,6},{6,4},{8,10},{10,8},{12,14},{14,12},{16,18},{18,... | collective-permute-start | bytes 1572872 | tf_op jit(solution)/shard_map/ppermute | solution.py:648
  534.0 46.3 %collective-permute-start.87 = (bf16[256,1024]{1,0:T(8,128)(2,1)S(1)}, bf16[256,1024]{1,0:T(8,128)(2,1)S(1)}, u32[]{:S(2)}, u32[]{:S(2)}) collective-permute-start(bf16[256,1024]{1,0:T(8,128)(2,1)S(1)} %pad_maximum_fusion.6.refs_0_), channel_id=1, source_target_pairs={{0,2},{2,0},{4,6},{6,4},{8,10},{10,8},{12,14},{14,12},{16,18},{18,... | collective-permute-start | bytes 1572872 | tf_op jit(solution)/shard_map/ppermute | solution.py:648
  534.0 46.3 %collective-permute-start.98 = (bf16[256,1024]{1,0:T(8,128)(2,1)S(1)}, bf16[256,1024]{1,0:T(8,128)(2,1)S(1)}, u32[]{:S(2)}, u32[]{:S(2)}) collective-permute-start(bf16[256,1024]{1,0:T(8,128)(2,1)S(1)} %pad_maximum_fusion.7.refs_4_), channel_id=1, source_target_pairs={{0,2},{2,0},{4,6},{6,4},{8,10},{10,8},{12,14},{14,12},{16,18},{18,... | collective-permute-start | bytes 1572872 | tf_op jit(solution)/shard_map/ppermute | solution.py:648
  545.2 26.8 %collective-permute-start.75 = (bf16[256,1024]{1,0:T(8,128)(2,1)}, bf16[256,1024]{1,0:T(8,128)(2,1)S(1)}, u32[]{:S(2)}, u32[]{:S(2)}) collective-permute-start(bf16[256,1024]{1,0:T(8,128)(2,1)} %collective-permute-done.73.refs_5_), channel_id=1, source_target_pairs={{0,2},{2,0},{4,6},{6,4},{8,10},{10,8},{12,14},{14,12},{16,18},{18,... | collective-permute-start | bytes 1572872 | tf_op jit(solution)/shard_map/ppermute | solution.py:648
  555.8 24.5 %collective-permute-start.88 = (bf16[256,1024]{1,0:T(8,128)(2,1)}, bf16[256,1024]{1,0:T(8,128)(2,1)S(1)}, u32[]{:S(2)}, u32[]{:S(2)}) collective-permute-start(bf16[256,1024]{1,0:T(8,128)(2,1)} %collective-permute-done.86.refs_1_), channel_id=1, source_target_pairs={{0,2},{2,0},{4,6},{6,4},{8,10},{10,8},{12,14},{14,12},{16,18},{18,... | collective-permute-start | bytes 1572872 | tf_op jit(solution)/shard_map/ppermute | solution.py:648
  555.9 24.5 %collective-permute-start.99 = (bf16[256,1024]{1,0:T(8,128)(2,1)}, bf16[256,1024]{1,0:T(8,128)(2,1)S(1)}, u32[]{:S(2)}, u32[]{:S(2)}) collective-permute-start(bf16[256,1024]{1,0:T(8,128)(2,1)} %collective-permute-done.97.refs_5_), channel_id=1, source_target_pairs={{0,2},{2,0},{4,6},{6,4},{8,10},{10,8},{12,14},{14,12},{16,18},{18,... | collective-permute-start | bytes 1572872 | tf_op jit(solution)/shard_map/ppermute | solution.py:648
  (154 other events, 2793.8 us)

commit v2 on v1

--- a/solution.py
+++ b/solution.py
@@ -576,62 +576,64 @@
     )(idx, send, keep, w, x, ghid, g)
 
 
-def wgrad_kernel(s, a0, a1, b0, b1, send, keep):
+def wgrad_kernel(s, *refs):
+    ops, (send, keep) = refs[:-2], refs[-2:]
+    i = pl.program_id(0)
     get = lambda r: r[...].reshape(r.shape[-2:])
-    v = dot(get(a0), get(b0), 0, 0) + dot(get(a1), get(b1), 0, 0)
-
-    @pl.when(pl.program_id(0) == 0)
-    def _():
-        send[...] = v.astype(BF)
-
-    @pl.when(pl.program_id(0) == 1)
-    def _():
-        keep[...] = v.astype(BF)
-
-
-def wgrad(idx, a, b, a_at, b_at):
-    far = lambda i, s: jnp.where(i == 0, 1 - s[0], s[0])
-    spec = lambda at: pl.BlockSpec(at[0], lambda i, s: at[1](far(i, s)))
-    t, rows, cols = a_at[0][-2], a_at[0][-1], b_at[0][-1]
+
+    def chunk(at):
+        a0, a1, b0, b1 = [get(r) for r in ops[4 * at : 4 * at + 4]]
+        v = (dot(a0, b0, 0, 0) + dot(a1, b1, 0, 0)).astype(BF)
+
+        @pl.when(i % 2 == 0)
+        def _():
+            send[0] = v
+
+        @pl.when(i % 2 == 1)
+        def _():
+            keep[0] = v
+
+    k = i // 2
+    pl.when(k < 4)(lambda: chunk(0))
+    pl.when((k >= 4) & (k < 8))(lambda: chunk(1))
+    pl.when(k == 8)(lambda: chunk(2))
+    pl.when(k > 8)(lambda: chunk(3))
+
+
+def wgrad_call(idx, mid, cot, ffn_in, gf, sent, gp, normed, gq):
+    t, d = cot[0].shape
+    h = d // 2
+
+    def spec(shape, at, lo, hi):
+        def index(i, s):
+            i = jnp.clip(i, 2 * lo, 2 * hi + 1)
+            x = jnp.where(i % 2 == 0, 1 - s[0], s[0])
+            return at(i // 2 - lo, x)
+
+        return pl.BlockSpec(shape, index)
+
+    pair = lambda *a: [spec(*a)] * 2
+    specs = (
+        pair((1, t, h), lambda k, x: (x, 0, k // 2), 0, 3)
+        + pair((t, h), lambda k, x: (0, k % 2), 0, 3)
+        + pair((t, h), lambda k, x: (0, x), 4, 7)
+        + pair((1, t, h), lambda k, x: (k // 2, 0, k % 2), 4, 7)
+        + pair((t, h), lambda k, x: (0, x), 8, 8)
+        + pair((t, h), lambda k, x: (0, 0), 8, 8)
+        + pair((t, h), lambda k, x: (0, x), 9, 11)
+        + pair((1, t, h), lambda k, x: (k, 0, 0), 9, 11)
+    )
+    out = lambda o: pl.BlockSpec((1, h, h), lambda i, s: (jnp.clip((i - o) // 2, 0, 11), 0, 0))
     return call(
         wgrad_kernel,
-        (2,),
+        (24,),
         1,
-        [spec(a_at), spec(a_at), spec(b_at), spec(b_at)],
-        [const_spec((rows, cols)), const_spec((rows, cols))],
-        [struct((rows, cols), BF), struct((rows, cols), BF)],
+        specs,
+        [pl.BlockSpec((1, h, h), lambda i, s: (i // 2, 0, 0))] * 2,
+        [struct((12, h, h), BF)] * 2,
         [],
-        cost(4 * t * rows * cols, 8 * t * rows + 8 * t * cols + 4 * rows * cols),
-    )(idx, a[0], a[1], b[0], b[1])
-
-
-def add_split_kernel(s, *refs, terms, slot):
-    f = len(refs) - terms
-    i = pl.program_id(0)
-    v = refs[0][...].astype(F32)
-    for r in refs[1:terms]:
-        v = v + r[...].astype(F32)
-    v = v.astype(BF)
-    for j in range(f):
-        @pl.when(i == j)
-        def _(j=j):
-            refs[terms + j][...] = v
-
-
-def add_split(idx, arrays, f, slot):
-    rows, cols = arrays[0].shape
-    part = rows // f
-    own = pl.BlockSpec((part, cols), lambda i, s: (i ^ s[slot] if f > 1 else i, 0))
-    return call(
-        functools.partial(add_split_kernel, terms=len(arrays), slot=slot),
-        (f,),
-        1,
-        [own] * len(arrays),
-        [const_spec((part, cols))] * f,
-        [struct((part, cols), BF)] * f,
-        [],
-        cost(rows * cols, (len(arrays) + 1) * 2 * rows * cols),
-    )(idx, *arrays)
+        cost(48 * t * h * h, 48 * t * h * 2),
+    )(idx, *mid, *cot, *ffn_in, *gf, *sent, *gp, *normed, *gq)
 
 
 def factors_of(n):
@@ -644,106 +646,272 @@
     return out
 
 
-def swap(v, stride, n):
-    return lax.ppermute(v, "rows", [(i, i ^ stride) for i in range(n)])
-
-
-def swap_ctx(v):
-    return lax.ppermute(v, "ctx", [(0, 1), (1, 0)])
-
-
-def strides_of(factors):
-    out, s = [], 1
-    for f in factors:
-        out.append(s)
-        s *= f
-    return out
-
-
-def all_gather_pieces(piece, factors, n):
-    cur = [piece]
-    for f, st in reversed(list(zip(factors, strides_of(factors)))):
-        if len(cur) > 2:
-            cur = [jnp.concatenate(cur, axis=0)]
-        cur = cur + [swap(c, j * st, n) for j in range(1, f) for c in cur]
-    return cur
-
-
-def all_reduce(idx, send, keep, factors):
+def reduce_kernel(factors, send, keep, small, out, small_out, *scr):
+    n_rs = len(factors)
+    chunks, rows, cols = send.shape
+    me = lax.axis_index("rows")
+    ctx = lax.axis_index("ctx")
+    fs = [2] + factors[1:]
+    strides, st = [0], 2
+    for f in factors[1:]:
+        strides.append(st)
+        st *= f
+    size = [rows]
+    for f in fs[1:]:
+        size.append(size[-1] // f)
+    pos = [ctx] + [lax.rem(me // strides[i], fs[i]) for i in range(1, n_rs)]
+    off = [0]
+    for i in range(1, n_rs):
+        off.append(off[-1] + pos[i] * size[i])
+    bits = []
+    b = 1
+    while b < lax.axis_size("rows"):
+        bits.append(b)
+        b *= 2
+
+    def peer(i, j):
+        if i == 0:
+            return (me, 1 - ctx)
+        return (me + ((pos[i] ^ j) - pos[i]) * strides[i], ctx)
+
+    core = lax.rem(me, 2)
+    sibling = (me + 1 - 2 * core, ctx)
+
+    def bit_peer(b):
+        return (me + b - 2 * b * lax.rem(me // b, 2), ctx)
+
+    scr = list(scr)
+    acc = scr.pop(0)
+    gath = scr.pop(0)
+    recv = [gath] + [scr.pop(0) for _ in range(1, n_rs)]
+    small_acc, small_recv = scr.pop(0), scr.pop(0)
+    rs_s = [scr.pop(0) for _ in range(n_rs)]
+    rs_r = [scr.pop(0) for _ in range(n_rs)]
+    ag_s = [None] + [scr.pop(0) for _ in range(1, n_rs)]
+    ag_r = [None] + [scr.pop(0) for _ in range(1, n_rs)]
+    core_s, core_r, loc, small_s, small_r = scr
+
+    def part(at, n):
+        return pl.ds(at if isinstance(at, int) else pl.multiple_of(at, 16), n)
+
+    def rs_copy(i, k, j):
+        if i == 0:
+            src, dst = send.at[k], gath.at[k]
+        else:
+            src = acc.at[k, part(off[i - 1] + (pos[i] ^ j) * size[i], size[i])]
+            dst = recv[i].at[k, j - 1]
+        return pltpu.make_async_remote_copy(
+            src, dst, rs_s[i].at[k, j - 1], rs_r[i].at[k, j - 1],
+            device_id=peer(i, j), device_id_type=pl.DeviceIdType.MESH,
+        )
+
+    def ag_copy(i, k, j, arriving):
+        at = off[i - 1] + (pos[i] ^ j) * size[i] if arriving else off[i]
+        ref = gath.at[k, part(at, size[i])]
+        return pltpu.make_async_remote_copy(
+            ref, ref, ag_s[i].at[k, j - 1], ag_r[i].at[k, j - 1],
+            device_id=peer(i, j), device_id_type=pl.DeviceIdType.MESH,
+        )
+
+    def core_copy(k, arriving):
+        to = 1 - core if arriving else core
+        return pltpu.make_async_remote_copy(
+            gath.at[k], out.at[k, to], core_s.at[k], core_r.at[k],
+            device_id=sibling, device_id_type=pl.DeviceIdType.MESH,
+        )
+
+    def own_copy(k):
+        return pltpu.make_async_copy(gath.at[k], out.at[k, core], loc.at[k])
+
+    def reduce_stage(i, k):
+        for j in range(1, fs[i]):
+            rs_copy(i, k, j).wait_recv()
+        here = part(off[i], size[i])
+        if i == 0:
+            v = keep[k].astype(F32) + gath[k].astype(F32)
+        else:
+            v = acc[k, here].astype(F32)
+            for j in range(1, fs[i]):
+                v = v + recv[i][k, j - 1].astype(F32)
+        if i + 1 < n_rs:
+            acc[k, here] = v.astype(BF)
+            for j in range(1, fs[i + 1]):
+                rs_copy(i + 1, k, j).start()
+        else:
+            gath[k, here] = v.astype(BF)
+            for j in range(1, fs[i]):
+                ag_copy(i, k, j, False).start()
+
+    def gather_stage(i, k):
+        for j in range(1, fs[i]):
+            ag_copy(i, k, j, True).wait_recv()
+        if i > 1:
+            for j in range(1, fs[i - 1]):
+                ag_copy(i - 1, k, j, False).start()
+        else:
+            core_copy(k, False).start()
+            own_copy(k).start()
+
+    def small_copy(i):
+        to = (me, 1 - ctx) if i == 0 else bit_peer(bits[i - 1])
+        return pltpu.make_async_remote_copy(
+            small_acc.at[i], small_recv.at[i], small_s.at[i], small_r.at[i],
+            device_id=to, device_id_type=pl.DeviceIdType.MESH,
+        )
+
+    peers = [(me, 1 - ctx), sibling]
+    for i in range(1, n_rs):
+        peers += [peer(i, j) for j in range(1, fs[i])]
+    barrier = pltpu.get_barrier_semaphore()
+    for p in peers:
+        pl.semaphore_signal(barrier, inc=1, device_id=p, device_id_type=pl.DeviceIdType.MESH)
+    pl.semaphore_wait(barrier, len(peers))
+
+    small_acc[0] = small[...]
+    small_copy(0).start()
+
+    def first(k, _):
+        rs_copy(0, k, 1).start()
+        return 0
+
+    lax.fori_loop(0, chunks, first, 0)
+
+    lanes = 2 * n_rs - 1
+    steps = [functools.partial(reduce_stage, i) for i in range(n_rs)]
+    steps += [functools.partial(gather_stage, i) for i in range(n_rs - 1, 0, -1)]
+
+    def step(t, _):
+        for lag in range(lanes - 1, -1, -1):
+            k = t - lag
+
+            @pl.when((k >= 0) & (k < chunks))
+            def _(k=k, lag=lag):
+                steps[lag](k)
+
+        for i in range(len(bits) + 1):
+
+            @pl.when(t == i)
+            def _(i=i):
+                small_copy(i).wait_recv()
+                if i < len(bits):
+                    small_acc[i + 1] = small_acc[i] + small_recv[i]
+                    small_copy(i + 1).start()
+                else:
+                    small_out[...] = small_acc[i] + small_recv[i]
+
+        return 0
+
+    lax.fori_loop(0, chunks + lanes - 1, step, 0)
+
+    def last(k, _):
+        for i in range(n_rs):
+            for j in range(1, fs[i]):
+                rs_copy(i, k, j).wait_send()
+                if i > 0:
+                    ag_copy(i, k, j, False).wait_send()
+        core_copy(k, False).wait_send()
+        core_copy(k, True).wait_recv()
+        own_copy(k).wait()
+        return 0
+
+    lax.fori_loop(0, chunks, last, 0)
+    for i in range(len(bits) + 1):
+        small_copy(i).wait_send()
+
+
+def reduce_call(send, keep, small, factors):
+    chunks, rows, cols = send.shape
     n = 1
     for f in factors:
         n *= f
-    shape = keep.shape
-    short = shape[0] * 2 // n
-    if short < 16:
-        keep = keep.reshape(shape[0] * 16 // short, -1)
-        send = send.reshape(keep.shape)
-    terms = [keep, swap_ctx(send)]
-    for k, (f, st) in enumerate(list(zip(factors, strides_of(factors)))[1:]):
-        parts = add_split(idx, terms, f, 2 + k)
-        terms = [parts[0]] + [swap(parts[j], j * st, n) for j in range(1, f)]
-    [piece] = add_split(idx, terms, 1, 2)
-    return all_gather_pieces(piece, factors, n)
-
-
-def finish_kernel(s, *refs, pieces, slots):
-    out = refs[-1]
-    i = pl.program_id(0)
-    z = 0
-    for slot, f in slots:
-        z = z * f + s[slot]
-    for j, src in enumerate(refs[:-1]):
-
-        @pl.when(i == j)
-        def _(src=src):
-            part = src.shape[0] // pieces
-            for k in range(pieces):
-                rows = pl.ds(pl.multiple_of((k ^ z) * part, part), part)
-                out[k * part : (k + 1) * part, :] = src[rows, :].astype(F32)
-
-
-def finish(idx, groups, shape, place, factors):
+    fs = [2] + factors[1:]
+    levels = 1
+    while n > 1:
+        levels += 1
+        n //= 2
+    size, recv = rows, []
+    for f in fs[1:]:
+        size //= f
+        recv.append(pltpu.VMEM((chunks, f - 1, size, cols), BF))
+    dma = lambda *shape: pltpu.SemaphoreType.DMA(shape)
+    per = lambda k: [dma(chunks, f - 1) for f in fs[k:]]
+    return pl.pallas_call(
+        functools.partial(reduce_kernel, factors),
+        in_specs=[
+            pl.BlockSpec(memory_space=pl.ANY),
+            pl.BlockSpec(memory_space=pltpu.VMEM),
+            pl.BlockSpec(memory_space=pltpu.VMEM),
+        ],
+        out_specs=[pl.BlockSpec(memory_space=pl.ANY), pl.BlockSpec(memory_space=pltpu.VMEM)],
+        out_shape=[struct((chunks, 2, rows, cols), BF), struct(small.shape, F32)],
+        scratch_shapes=[pltpu.VMEM((chunks, rows, cols), BF)] * 2
+        + recv
+        + [pltpu.VMEM((levels,) + small.shape, F32)] * 2
+        + per(0) + per(0) + per(1) + per(1)
+        + [dma(chunks), dma(chunks), dma(chunks), dma(levels), dma(levels)],
+        compiler_params=pltpu.CompilerParams(
+            collective_id=0, has_side_effects=True, vmem_limit_bytes=60 * 2**20
+        ),
+    )(send, keep, small)
+
+
+def sum_over_devices(send, keep, small, factors):
+    chunks, rows, cols = send.shape
     pieces = 1
-    for f in factors[2:]:
+    for f in factors[1:]:
         pieces *= f
-    slots = [(3 + k, f) for k, f in enumerate(factors[2:])]
-    rows, cols = groups[0][0].shape
-    flat = [v for g in groups for v in g]
-
-    def at(i, s):
-        chunk = i // 4
-        core = ((i // 2) % 2) ^ s[1]
-        y = (i % 2) ^ s[2]
-        r, c = place(chunk, core)
-        return (r * 2 + y, c)
+    r = max(rows, 16 * pieces)
+    flat = lambda v: v if r == rows else v.reshape(chunks, r, rows * cols // r)
+    got, small = reduce_call(flat(send), flat(keep), small, factors)
+    return got.reshape(chunks, 2, rows, cols), small
+
+
+def finish_kernel(s, got, g2, g1, go, gq):
+    k = pl.program_id(0) // 2
+    v = got[0, 0].astype(F32)
+
+    def put(out):
+        out[...] = v
+
+    pl.when(k < 4)(lambda: put(g2))
+    pl.when((k >= 4) & (k < 8))(lambda: put(g1))
+    pl.when(k == 8)(lambda: put(go))
+    pl.when(k > 8)(lambda: put(gq))
+
+
+def finish_call(idx, got, ff, d):
+    h = d // 2
+
+    def spec(lo, hi, at):
+        def index(i, s):
+            i = jnp.clip(i, 2 * lo, 2 * hi + 1)
+            return at(i // 2 - lo, i % 2)
+
+        return pl.BlockSpec((h, h), index)
 
     return call(
-        functools.partial(finish_kernel, pieces=pieces, slots=slots),
-        (4 * len(groups),),
+        finish_kernel,
+        (24,),
         1,
-        [const_spec((rows, cols))] * len(flat),
-        pl.BlockSpec((rows, cols), at),
-        struct(shape, F32),
+        [pl.BlockSpec((1, 1, h, h), lambda i, s: (i // 2, i % 2, 0, 0))],
+        [
+            spec(0, 3, lambda k, c: (c * 2 + k // 2, k % 2)),
+            spec(4, 7, lambda k, c: (0, ((k // 2) * 2 + c) * 2 + k % 2)),
+            spec(8, 8, lambda k, c: (0, c)),
+            spec(9, 11, lambda k, c: (0, k * 2 + c)),
+        ],
+        [struct((ff // 2, d), F32), struct((h, ff), F32), struct((h, d), F32), struct((h, 3 * d), F32)],
         [],
-        cost(rows * cols * len(flat), 6 * rows * cols * len(flat)),
-    )(idx, *flat)
-
-
-def finish_all(idx, groups, chunk, blocks, place, factors):
-    rows, cols = chunk
-    shape = (blocks[0] * rows, blocks[1] * cols)
-    r, c = groups[0][0].shape
-    if r * 2 == rows:
-        return finish(idx, groups, shape, place, factors)
-    count = len(groups)
-    flat = finish(idx, groups, (count * 4 * r, c), lambda j, core: (j * 2 + core, 0), factors)
-    flat = flat.reshape(count, 2, rows, cols)
-    out = jnp.zeros(shape, F32)
-    for j in range(count):
-        for core in range(2):
-            a, b = place(j, core)
-            out = lax.dynamic_update_slice(out, flat[j, core], (a * rows, b * cols))
-    return out
+        cost(0, 24 * h * h * 6),
+    )(idx, got)
+
+
+def swap(v, stride, n):
+    return lax.ppermute(v, "rows", [(i, i ^ stride) for i in range(n)])
+
+
+def swap_ctx(v):
+    return lax.ppermute(v, "ctx", [(0, 1), (1, 0)])
 
 
 def local(
@@ -795,31 +963,7 @@
     gf_send, gf_keep, ghid, gp_send, gp_keep, gsent, gmg, gmb, gn12, bn12 = ffn_bwd_call(
         idx, cot, w_fc2, mg, nmid, smid, slope, w_fc1, n1, s1, n2, s2, norm_gain, w_out
     )
-    half = d // 2
-
-    def chunks(*args):
-        return all_reduce(idx, *wgrad(idx, *args), factors)
-
-    got2 = [
-        chunks(mid_pair, cot_pair, ((1, t, half), lambda x, j=j: (x, 0, j)), ((t, d), lambda x: (0, 0)))
-        for j in range(2)
-    ]
-    gf_pair = (gf_keep, swap(gf_send, 1, n))
-    in_pair = core(ffn_in)
-    got1 = [
-        chunks(in_pair, gf_pair, ((t, half), lambda x: (0, x)), ((1, t, ff // 4), lambda x, j=j: (j, 0, 0)))
-        for j in range(2)
-    ]
-    sent_pair = core(sent)
-    gp_pair = (gp_keep, swap(gp_send, 1, n))
-    got_o = [chunks(sent_pair, gp_pair, ((t, half), lambda x: (0, x)), ((t, half), lambda x: (0, 0)))]
     gq_send, gq_keep, hsum = attn_bwd_call(idx, qkv, gsent, sent, lse, start, scale)
-    gq_pair = (gq_keep, swap(gq_send, 1, n))
-    normed_pair = core(normed)
-    got_q = [
-        chunks(normed_pair, gq_pair, ((t, half), lambda x: (0, x)), ((1, t, half), lambda x, j=j: (j, 0, 0)))
-        for j in range(3)
-    ]
     gx, gn0, bn0 = in_bwd_call(idx, gq_send, gq_keep, w_qkv, x, ghid, norm_gain)
     out = out_call(idx, mid_send, mid_keep, w_fc2, x, n1, norm_gain, norm_bias)
 
@@ -827,7 +971,22 @@
     small = jnp.concatenate(
         [jnp.concatenate([gn0, gn12]).reshape(-1), jnp.concatenate([bn0, bn12]).reshape(-1), gmg[0], gmb[0], ghs]
     )
-    small = lax.psum(small, ("rows", "ctx"))
+    pad = -small.shape[0] % 1024
+    small = jnp.pad(small, (0, pad)).reshape(-1, 128)
+    send, keep = wgrad_call(
+        idx,
+        mid_pair,
+        cot_pair,
+        core(ffn_in),
+        (gf_keep, swap(gf_send, 1, n)),
+        core(sent),
+        (gp_keep, swap(gp_send, 1, n)),
+        core(normed),
+        (gq_keep, swap(gq_send, 1, n)),
+    )
+    got, small = sum_over_devices(send, keep, small, factors)
+    small = small.reshape(-1)
+    g2, g1, go, gq = finish_call(idx, got, ff, d)
 
     def take(v, axis):
         size = v.shape[axis] // 2
@@ -837,7 +996,7 @@
     bn = take(small[3 * d : 6 * d].reshape(3, d), 1)
     gmg = take(small[6 * d : 6 * d + ff], 0)
     gmb = take(small[6 * d + ff : 6 * d + 2 * ff], 0)
-    ghs = take(small[6 * d + 2 * ff :], 0)
+    ghs = take(small[6 * d + 2 * ff : 6 * d + 2 * ff + heads], 0)
 
     def halves(v):
         seg = t // 2
@@ -848,10 +1007,6 @@
         hi = jnp.where(ctx == 0, got, mine)
         return jnp.stack([lo, hi])
 
-    g2 = finish_all(idx, got2, (half, d), (4, 1), lambda j, c: (c * 2 + j, 0), factors)
-    g1 = finish_all(idx, got1, (half, d), (1, 4), lambda j, c: (0, j * 2 + c), factors)
-    go = finish_all(idx, got_o, (half, half), (1, 2), lambda j, c: (0, c), factors)
-    gq = finish_all(idx, got_q, (half, half), (1, 6), lambda j, c: (0, j * 2 + c), factors)
     return (halves(out), halves(gx), gq, go, g1, g2, gn, bn, gmg, gmb, ghs)
 
 

time: 600 us -> 418 us (0.70); the launches traced: 590 us -> 416 us
  waiting for transfers between devices: 135 us -> 15.8 us
  starting transfers between devices: 115 us -> 7.45 us
  Pallas kernels: 259 us -> 363 us
  blocking collectives: 38.6 us -> 0 us
  other arithmetic: 16.5 us -> 9.32 us
    ppermute x88 -> x8, waiting for transfers between devices: 108 us -> 2.4 us  [swap(): return lax.ppermute(v, 'rows', [(i, i ^ stride) for i in range(n)])]
    pallas_call x36 -> x3, Pallas kernels: 146 us -> 250 us  [the longest x1 193 us: reduce_call(): pl.pallas_call(functools.partial(reduce_kernel, factors), in_specs=[pl.Bl...]
    ppermute x88 -> x8, starting transfers between devices: 100 us -> 2.21 us  [swap(): return lax.ppermute(v, 'rows', [(i, i ^ stride) for i in range(n)])]
    psum x1 -> x0, blocking collectives: 38.6 us -> none  [local(): small = lax.psum(small, ('rows', 'ctx'))]
    ppermute x12 -> x4, waiting for transfers between devices: 26.7 us -> 13.4 us  [swap_ctx(): return lax.ppermute(v, 'ctx', [(0, 1), (1, 0)])]
    ppermute x12 -> x4, starting transfers between devices: 14.9 us -> 5.23 us  [swap_ctx(): return lax.ppermute(v, 'ctx', [(0, 1), (1, 0)])]
    unnamed x208 -> x38, local copies, waits for them, and re-layouts: 8.45 us -> 1.82 us
    concatenate x8 -> x0, other arithmetic: 6.12 us -> none  [all_gather_pieces(): cur = [jnp.concatenate(cur, axis=0)]]
  transfers between devices with their start and end apart: 100 -> 12, of which waited for: 26 -> 4; matrix products, arithmetic and copies ran while one was open for 5% -> 4% of each run, Pallas kernels for 43% -> 27%
where the time goes in v2:
time: 418 us; the launch traced here: 416 us
  Pallas kernels  363 us (87%)
  local copies, waits for them, and re-layouts  17.1 us (4%)
  waiting for transfers between devices  15.8 us (4%)
  other arithmetic  9.32 us (2%)
  starting transfers between devices  7.45 us (2%)
    pallas_call x1, Pallas kernels, reduce_call(): pl.pallas_call(functools.partial(reduce_kernel, factors), in_specs=[pl.Bl...  193 us
    pallas_call x1, Pallas kernels, wgrad_call(): call(wgrad_kernel, (24,), 1, specs, [pl.BlockSpec((1, h, h), lambda i, s:...  34.2 us
    pallas_call x1, Pallas kernels, ffn_bwd_call(): call(ffn_bwd_kernel, (8,), 1, [const_spec((t, d)), pl.BlockSpec((bw, d),...  29.2 us
    pallas_call x1, Pallas kernels, finish_call(): call(finish_kernel, (24,), 1, [pl.BlockSpec((1, 1, h, h), lambda i, s: (i...  23 us
    pallas_call x1, Pallas kernels, ffn_fwd_call(): call(ffn_fwd_kernel, (8,), 1, [const_spec((t, d)), const_spec((t, d)), co...  22.7 us
    pallas_call x1, Pallas kernels, attn_fwd_call(): call(attn_fwd_kernel, (pairs,), 1, [part(0), part(1), part(2), const_spec...  14.5 us
    pallas_call x1, Pallas kernels, attn_bwd_call(): call(attn_bwd_kernel, (pairs,), 1, [part(0), part(1), part(2), flat, flat...  14.3 us
    ppermute x4, waiting for transfers between devices, swap_ctx(): return lax.ppermute(v, 'ctx', [(0, 1), (1, 0)])  13.4 us
  transfers between devices with their start and end apart: 12, of which 4 were waited for; matrix products, arithmetic and copies ran while one was open for 4% of the time, Pallas kernels for 27%

profile of v2, /device:TPU:0, one launch (start us, length us, event | category | flops | bytes accessed | tf_op | source)
XLA Modules:
  0.0 416.5 jit_solution(8389967216712672485)
XLA Ops:
  0.7 1.2 dynamic-slice_bitcast_fusion.1
  1.9 3.0 collective-permute-start
  4.9 1.1 dynamic-slice_bitcast_fusion
  6.1 1.3 slice.46.b
  7.4 1.3 slice.45.g
  8.8 0.7 broadcast_in_dim_reshape.3.scale
  9.5 0.6 fusion.3
  12.7 0.6 pad_add_fusion.s
  13.3 1.2 compare_select_fusion.3.start
  14.5 3.1 collective-permute-done
  17.7 1.0 pad_maximum_fusion.1.x
  18.7 8.8 %shard_map.203 = (bf16[512,1024]{1,0:T(8,128)(2,1)}, bf16[3,512,1024]{2,1,0:T(8,128)(2,1)}) custom-call(s32[4]{0:T(128)} %pad_add_fusion.s, bf16[512,1024]{1,0:T(8,128)(2,1)} %pad_maximum_fusion.1.x, bf16[1024,3072]{1,0:T(8,128)(2,1)} %w.3, f32[1,1024]{1,0:T(1,128)} %slice.45.g, f32[1,1024]{1,0:T(1,128)} %slice.46.b), custom_call_target="tpu_custom_call" | custom-call | flops 3221225472 | bytes 11534336 | tf_op jit(solution)/shard_map/pallas_call | solution.py:84
  27.5 14.5 %shard_map.204 = (bf16[512,1024]{1,0:T(8,128)(2,1)}, f32[8,2,512]{2,1,0:T(2,128)}) custom-call(s32[4]{0:T(128)} %pad_add_fusion.s, bf16[3,512,1024]{2,1,0:T(8,128)(2,1)} %get-tuple-element.49.q.k.v, bf16[3,512,1024]{2,1,0:T(8,128)(2,1)} %get-tuple-element.49.q.k.v, bf16[3,512,1024]{2,1,0:T(8,128)(2,1)} %get-tuple-element.49.q.k.v, ...), custom_call_target="tpu_custom_call" | custom-call | flops 1073741824 | bytes 4194304 | tf_op jit(solution)/shard_map/pallas_call | solution.py:152
  42.0 22.7 %shard_map.205 = (f32[512,1024]{1,0:T(8,128)}, f32[512,1]{1,0:T(8,128)}, f32[512,1024]{1,0:T(8,128)}, f32[512,1]{1,0:T(8,128)}, bf16[512,1024]{1,0:T(8,128)(2,1)...) custom-call(s32[4]{0:T(128)} %pad_add_fusion.s, ...), custom_call_target="tpu_custom_call" | custom-call | flops 5368709120 | bytes 26214400 | tf_op jit(solution)/shard_map/pallas_call | solution.py:319
  64.7 11.1 %shard_map.206 = bf16[512,1024]{1,0:T(8,128)(2,1)} custom-call(s32[4]{0:T(128)} %pad_add_fusion.s, bf16[2,512,1024]{2,1,0:T(8,128)(2,1)} %get-tuple-element.51.send, bf16[2,512,1024]{2,1,0:T(8,128)(2,1)} %get-tuple-element.52.keep.refs_0_, bf16[4096,1024]{1,0:T(8,128)(2,1)} %w2.3, bf16[512,1024]{1,0:T(8,128)(2,1)} %pad_maximum_fusion.1.x, ...), custom_call_target="tpu_custom_call" | custom-call | flops 4294967296 | bytes 16777216 | tf_op jit(solution)/shard_map/pallas_call | solution.py:386
  75.8 1.9 constant_dynamic-slice_fusion.2
  77.7 2.1 collective-permute-start.1
  79.9 1.1 pad_maximum_fusion.3.cot.refs_2_
  80.9 29.2 %shard_map.207 = (bf16[2,512,1024]{2,1,0:T(8,128)(2,1)}, bf16[2,512,1024]{2,1,0:T(8,128)(2,1)}, f32[512,1024]{1,0:T(8,128)}, bf16[512,512]{1,0:T(8,128)(2,1)}, b...) custom-call(s32[4]{0:T(128)} %pad_add_fusion.s, ...), custom_call_target="tpu_custom_call" | custom-call | flops 9663676416 | bytes 39845888 | tf_op jit(solution)/shard_map/pallas_call | solution.py:480
  110.1 14.3 %shard_map.208 = (bf16[3,512,512]{2,1,0:T(8,128)(2,1)}, bf16[3,512,512]{2,1,0:T(8,128)(2,1)}, f32[8,2,512]{2,1,0:T(2,128)}) custom-call(s32[4]{0:T(128)} %pad_add_fusion.s, bf16[3,512,1024]{2,1,0:T(8,128)(2,1)} %get-tuple-element.49.q.k.v, bf16[3,512,1024]{2,1,0:T(8,128)(2,1)} %get-tuple-element.49.q.k.v, bf16[3,512,1024]{2,1,0:T(8,128)(2,1)} %get-tuple-element.49.q.k.v, ...), custom_call_target="tpu_custom_call" | custom-call | flops 2684354560 | bytes 8388608 | tf_op jit(solution)/shard_map/pallas_call | solution.py:221
  124.5 12.5 %shard_map.209 = (f32[512,1024]{1,0:T(8,128)}, f32[1,1024]{1,0:T(1,128)}, f32[1,1024]{1,0:T(1,128)}) custom-call(s32[4]{0:T(128)} %pad_add_fusion.s, bf16[3,512,512]{2,1,0:T(8,128)(2,1)} %get-tuple-element.62.send, bf16[3,512,512]{2,1,0:T(8,128)(2,1)} %get-tuple-element.63.keep.refs_14_, bf16[1024,3072]{1,0:T(8,128)(2,1)} %w.3, ...), custom_call_target="tpu_custom_call" | custom-call | flops 3221225472 | bytes 18874368 | tf_op jit(solution)/shard_map/pallas_call | solution.py:560
  137.0 1.3 dynamic-slice_convert_fusion
  138.5 0.5 collective-permute-start.10
  139.1 0.4 collective-permute-start.7
  139.5 10.3 %collective-permute-done.3 = bf16[256,1024]{1,0:T(8,128)(2,1)S(1)} collective-permute-done((bf16[256,1024]{1,0:T(8,128)(2,1)S(1)}, bf16[256,1024]{1,0:T(8,128)(2,1)S(1)}, u32[]{:S(2)}, u32[]{:S(2)}) %collective-permute-start.3) | collective-permute-done | bytes 524320 | tf_op jit(solution)/shard_map/ppermute | solution.py:914
  149.8 0.8 copy-done.7
  150.6 0.7 pad_maximum_fusion.4
  151.3 0.6 collective-permute-start.11
  152.3 0.5 collective-permute-start.6
  152.7 0.6 pad_bitcast_fusion.small
  153.4 1.4 select_bitcast_fusion.1
  154.8 1.1 pad_maximum_fusion.2
  155.9 0.3 fusion
  156.2 1.6 pad_maximum_fusion
  157.8 0.1 collective-permute-done.8.refs_9_
  157.9 2.2 collective-permute-done.6.refs_5_
  160.2 0.9 copy-done.16
  161.2 34.2 %shard_map.210 = (bf16[12,512,512]{2,1,0:T(8,128)(2,1)}, bf16[12,512,512]{2,1,0:T(8,128)(2,1)}) custom-call(s32[4]{0:T(128)} %pad_add_fusion.s, bf16[2,512,1024]{2,1,0:T(8,128)(2,1)} %get-tuple-element.52.keep.refs_0_, bf16[2,512,1024]{2,1,0:T(8,128)(2,1)} %collective-permute-done.4.refs_1_, bf16[512,1024]{1,0:T(8,128)(2,1)} %pad_maximum_fusion.3.cot.refs_2_, ...), custom_call_target="tpu_custom_call" | custom-call | flops 12884901888 | bytes 25165824 | tf_op jit(solution)/shard_map/pallas_call | solution.py:627
  195.3 193.0 %shard_map.211 = (bf16[12,2,512,512]{3,2,1,0:T(8,128)(2,1)}, f32[120,128]{1,0:T(8,128)}) custom-call(bf16[12,512,512]{2,1,0:T(8,128)(2,1)} %get-tuple-element.72.send, bf16[12,512,512]{2,1,0:T(8,128)(2,1)} %get-tuple-element.73.keep, f32[120,128]{1,0:T(8,128)} %pad_bitcast_fusion.small), custom_call_target="tpu_custom_call" | custom-call | tf_op jit(solution)/shard_map/pallas_call | solution.py:838
  388.4 0.7 fusion.2
  389.1 0.7 slice_bitcast_fusion
  389.8 0.7 slice.58
  390.5 0.6 dynamic_slice.56
  391.1 0.6 dynamic_slice.55
  391.7 0.6 constant_dynamic-slice_fusion
  392.3 0.6 constant_dynamic-slice_fusion.1
  392.9 23.0 %shard_map.212 = (f32[2048,1024]{1,0:T(8,128)}, f32[512,4096]{1,0:T(8,128)}, f32[512,1024]{1,0:T(8,128)}, f32[512,3072]{1,0:T(8,128)}) custom-call(s32[4]{0:T(128)} %pad_add_fusion.s, bf16[12,2,512,512]{3,2,1,0:T(8,128)(2,1)} %get-tuple-element.81.got), custom_call_target="tpu_custom_call" | custom-call | bytes 37748736 | tf_op jit(solution)/shard_map/pallas_call | solution.py:892
  415.9 0.6 dynamic_slice.57
  (61 shorter events, 1.0 us)
Async XLA Ops:
  0.6 8.8 %copy-start = (s32[2,4]{1,0:T(2,128)S(1)}, s32[2,4]{1,0:T(2,128)}, u32[]{:S(2)}) copy-start(s32[2,4]{1,0:T(2,128)} %param.23) | copy-start | bytes 100
  0.7 17.0 %copy-start.5 = (bf16[2,256,1024]{2,1,0:T(8,128)(2,1)S(1)}, bf16[2,256,1024]{2,1,0:T(8,128)(2,1)}, u32[]{:S(2)}) copy-start(bf16[2,256,1024]{2,1,0:T(8,128)(2,1)} %param.12) | copy-start | bytes 3145732
  0.7 8.0 %copy-start.14 = (f32[16]{0:T(128)S(1)}, f32[16]{0:T(128)}, u32[]{:S(2)}) copy-start(f32[16]{0:T(128)} %param.22) | copy-start | bytes 196
  1.9 15.8 %collective-permute-start = (bf16[256,1024]{1,0:T(8,128)(2,1)S(1)}, bf16[256,1024]{1,0:T(8,128)(2,1)S(1)}, u32[]{:S(2)}, u32[]{:S(2)}) collective-permute-start(bf16[256,1024]{1,0:T(8,128)(2,1)S(1)} %dynamic-slice_bitcast_fusion.1), channel_id=1, source_target_pairs={{0,1},{1,0},{2,3},{3,2},{4,5},{5,4},{6,7},{7,6},{8,9},{9,8},{10,11... | collective-permute-start | bytes 1572872 | tf_op jit(solution)/shard_map/ppermute | solution.py:914
  5.9 73.8 %collective-permute-start.2 = (bf16[256,1024]{1,0:T(8,128)(2,1)S(1)}, bf16[256,1024]{1,0:T(8,128)(2,1)S(1)}, u32[]{:S(2)}, u32[]{:S(2)}) collective-permute-start(bf16[256,1024]{1,0:T(8,128)(2,1)S(1)} %dynamic-slice_bitcast_fusion), channel_id=1, source_target_pairs={{0,1},{1,0},{2,3},{3,2},{4,5},{5,4},{6,7},{7,6},{8,9},{9,8},{10,11... | collective-permute-start | bytes 1572872 | tf_op jit(solution)/shard_map/ppermute | solution.py:914
  64.7 15.1 %copy-start.6 = (bf16[2,256,1024]{2,1,0:T(8,128)(2,1)S(1)}, bf16[2,256,1024]{2,1,0:T(8,128)(2,1)}, u32[]{:S(2)}) copy-start(bf16[2,256,1024]{2,1,0:T(8,128)(2,1)} %param.13) | copy-start | bytes 3145732
  77.7 61.4 %collective-permute-start.1 = (bf16[256,1024]{1,0:T(8,128)(2,1)}, bf16[256,1024]{1,0:T(8,128)(2,1)}, u32[]{:S(2)}, u32[]{:S(2)}) collective-permute-start(bf16[256,1024]{1,0:T(8,128)(2,1)} %constant_dynamic-slice_fusion.2), channel_id=1, source_target_pairs={{0,1},{1,0},{2,3},{3,2},{4,5},{5,4},{6,7},{7,6},{8,9},{9,8},{10,11... | collective-permute-start | bytes 1572872 | tf_op jit(solution)/shard_map/ppermute | solution.py:914
  124.4 26.1 %copy-start.3 = (bf16[2,512,1024]{2,1,0:T(8,128)(2,1)S(1)}, bf16[2,512,1024]{2,1,0:T(8,128)(2,1)}, u32[]{:S(2)}) copy-start(bf16[2,512,1024]{2,1,0:T(8,128)(2,1)} %get-tuple-element.51.send) | copy-start | bytes 6291460
  124.4 26.1 %copy-start.12 = (f32[2,1024]{1,0:T(2,128)S(1)}, f32[2,1024]{1,0:T(2,128)}, u32[]{:S(2)}) copy-start(f32[2,1024]{1,0:T(2,128)} %get-tuple-element.75) | copy-start | bytes 24580
  124.5 26.1 %copy-start.13 = (f32[2,1024]{1,0:T(2,128)S(1)}, f32[2,1024]{1,0:T(2,128)}, u32[]{:S(2)}) copy-start(f32[2,1024]{1,0:T(2,128)} %get-tuple-element.77) | copy-start | bytes 24580
  124.5 27.4 %copy-start.9 = (f32[8,2,512]{2,1,0:T(2,128)S(1)}, f32[8,2,512]{2,1,0:T(2,128)}, u32[]{:S(2)}) copy-start(f32[8,2,512]{2,1,0:T(2,128)} %get-tuple-element.80) | copy-start | bytes 98308
  124.5 27.6 %copy-start.11 = (f32[1,4096]{1,0:T(1,128)S(1)}, f32[1,4096]{1,0:T(1,128)}, u32[]{:S(2)}) copy-start(f32[1,4096]{1,0:T(1,128)} %get-tuple-element.78) | copy-start | bytes 49156
  124.5 27.6 %copy-start.10 = (f32[1,4096]{1,0:T(1,128)S(1)}, f32[1,4096]{1,0:T(1,128)}, u32[]{:S(2)}) copy-start(f32[1,4096]{1,0:T(1,128)} %get-tuple-element.79) | copy-start | bytes 49156
  124.5 28.9 %copy-start.2 = (bf16[512,1024]{1,0:T(8,128)(2,1)S(1)}, bf16[512,1024]{1,0:T(8,128)(2,1)}, u32[]{:S(2)}) copy-start(bf16[512,1024]{1,0:T(8,128)(2,1)} %shard_map.206) | copy-start | bytes 3145732
  138.3 11.4 %collective-permute-start.3 = (bf16[256,1024]{1,0:T(8,128)(2,1)S(1)}, bf16[256,1024]{1,0:T(8,128)(2,1)S(1)}, u32[]{:S(2)}, u32[]{:S(2)}) collective-permute-start(bf16[256,1024]{1,0:T(8,128)(2,1)S(1)} %dynamic-slice_convert_fusion), channel_id=1, source_target_pairs={{0,1},{1,0},{2,3},{3,2},{4,5},{5,4},{6,7},{7,6},{8,9},{9,8},{10,11... | collective-permute-start | bytes 1572872 | tf_op jit(solution)/shard_map/ppermute | solution.py:914
  138.4 13.7 %collective-permute-start.5 = (bf16[512,1024]{1,0:T(8,128)(2,1)}, bf16[512,1024]{1,0:T(8,128)(2,1)}, u32[]{:S(2)}, u32[]{:S(2)}) collective-permute-start(bf16[512,1024]{1,0:T(8,128)(2,1)} %pad_maximum_fusion.3.cot.refs_2_), channel_id=1, source_target_pairs={{0,2},{2,0},{4,6},{6,4},{8,10},{10,8},{12,14},{14,12},{16,18},{18,... | collective-permute-start | bytes 3145736 | tf_op jit(solution)/shard_map/ppermute | solution.py:910
  138.5 13.8 %collective-permute-start.10 = (bf16[512,1024]{1,0:T(8,128)(2,1)}, bf16[512,1024]{1,0:T(8,128)(2,1)}, u32[]{:S(2)}, u32[]{:S(2)}) collective-permute-start(bf16[512,1024]{1,0:T(8,128)(2,1)} %get-tuple-element.71.refs_12_), channel_id=1, source_target_pairs={{0,2},{2,0},{4,6},{6,4},{8,10},{10,8},{12,14},{14,12},{16,18},{18,... | collective-permute-start | bytes 3145736 | tf_op jit(solution)/shard_map/ppermute | solution.py:910
  139.0 12.3 %collective-permute-start.9 = (bf16[512,512]{1,0:T(8,128)(2,1)}, bf16[512,512]{1,0:T(8,128)(2,1)}, u32[]{:S(2)}, u32[]{:S(2)}) collective-permute-start(bf16[512,512]{1,0:T(8,128)(2,1)} %get-tuple-element.70), channel_id=1, source_target_pairs={{0,2},{2,0},{4,6},{6,4},{8,10},{10,8},{12,14},{14,12},{16,18},{18,... | collective-permute-start | bytes 1572872 | tf_op jit(solution)/shard_map/ppermute | solution.py:910
  139.1 21.1 %collective-permute-start.7 = (bf16[2,512,1024]{2,1,0:T(8,128)(2,1)}, bf16[2,512,1024]{2,1,0:T(8,128)(2,1)}, u32[]{:S(2)}, u32[]{:S(2)}) collective-permute-start(bf16[2,512,1024]{2,1,0:T(8,128)(2,1)} %get-tuple-element.68), channel_id=1, source_target_pairs={{0,2},{2,0},{4,6},{6,4},{8,10},{10,8},{12,14},{14,12},{16,18},{18,... | collective-permute-start | bytes 6291464 | tf_op jit(solution)/shard_map/ppermute | solution.py:910
  149.8 0.8 copy-start.7
  150.6 9.6 %collective-permute-start.4 = (bf16[2,512,1024]{2,1,0:T(8,128)(2,1)S(1)}, bf16[2,512,1024]{2,1,0:T(8,128)(2,1)}, u32[]{:S(2)}, u32[]{:S(2)}) collective-permute-start(bf16[2,512,1024]{2,1,0:T(8,128)(2,1)S(1)} %copy-done.3), channel_id=1, source_target_pairs={{0,2},{2,0},{4,6},{6,4},{8,10},{10,8},{12,14},{14,12},{16,18},{18,... | collective-permute-start | bytes 6291464 | tf_op jit(solution)/shard_map/ppermute | solution.py:910
  151.3 8.9 %collective-permute-start.11 = (bf16[3,512,512]{2,1,0:T(8,128)(2,1)}, bf16[3,512,512]{2,1,0:T(8,128)(2,1)}, u32[]{:S(2)}, u32[]{:S(2)}) collective-permute-start(bf16[3,512,512]{2,1,0:T(8,128)(2,1)} %get-tuple-element.62.send), channel_id=1, source_target_pairs={{0,2},{2,0},{4,6},{6,4},{8,10},{10,8},{12,14},{14,12},{16,18},{18,... | collective-permute-start | bytes 4718600 | tf_op jit(solution)/shard_map/ppermute | solution.py:910
  152.2 5.8 %collective-permute-start.8 = (bf16[512,1024]{1,0:T(8,128)(2,1)}, bf16[512,1024]{1,0:T(8,128)(2,1)S(1)}, u32[]{:S(2)}, u32[]{:S(2)}) collective-permute-start(bf16[512,1024]{1,0:T(8,128)(2,1)} %get-tuple-element.50.sent.refs_8_), channel_id=1, source_target_pairs={{0,2},{2,0},{4,6},{6,4},{8,10},{10,8},{12,14},{14,12},{16,18},{18,... | collective-permute-start | bytes 3145736 | tf_op jit(solution)/shard_map/ppermute | solution.py:910
  152.3 7.9 %collective-permute-start.6 = (bf16[512,1024]{1,0:T(8,128)(2,1)}, bf16[512,1024]{1,0:T(8,128)(2,1)S(1)}, u32[]{:S(2)}, u32[]{:S(2)}) collective-permute-start(bf16[512,1024]{1,0:T(8,128)(2,1)} %get-tuple-element.66.refs_4_), channel_id=1, source_target_pairs={{0,2},{2,0},{4,6},{6,4},{8,10},{10,8},{12,14},{14,12},{16,18},{18,... | collective-permute-start | bytes 3145736 | tf_op jit(solution)/shard_map/ppermute | solution.py:910
  153.4 2.5 copy-start.4
  153.4 2.5 copy-start.8
  157.9 2.3 copy-start.15
  160.2 1.0 copy-start.16
  392.9 23.5 %copy-start.1 = (s32[2,4]{1,0:T(2,128)S(1)}, s32[2,4]{1,0:T(2,128)}, u32[]{:S(2)}) copy-start(s32[2,4]{1,0:T(2,128)} %param.23) | copy-start | bytes 100

commit v3 on v0

v3 whole, which is shorter than its diff:
```python
import functools

import jax
import jax.numpy as jnp
from jax import lax
from jax.experimental import pallas as pl
from jax.experimental.pallas import tpu as pltpu
from jax.sharding import PartitionSpec as P

EPS = 1e-05
MASKED = -1e30
BF = jnp.bfloat16
F32 = jnp.float32
REACH = 256
QB = 128


def dot(a, b, ca, cb):
    return lax.dot_general(a, b, (((ca,), (cb,)), ((), ())), preferred_element_type=F32)


def ln_stats(v):
    mean = jnp.mean(v, axis=-1, keepdims=True)
    cen = v - mean
    inv = lax.rsqrt(jnp.mean(cen * cen, axis=-1, keepdims=True) + EPS)
    return cen * inv, inv


def ln_back(e, gain, n, inv):
    a = e * gain
    return inv * (
        a - jnp.mean(a, axis=-1, keepdims=True) - n * jnp.mean(a * n, axis=-1, keepdims=True)
    )


def colsum(v):
    return jnp.sum(v, axis=0, keepdims=True)


def struct(shape, dtype):
    return jax.ShapeDtypeStruct(shape, dtype)


def key_range(i):
    return max(0, i * QB - REACH), (i + 1) * QB


def fill_bias(start, bias, t):
    for i in range(t // QB):
        k0, k1 = key_range(i)
        u = lax.broadcasted_iota(jnp.int32, (k1 - k0, QB), 0) + k0
        q = lax.broadcasted_iota(jnp.int32, (k1 - k0, QB), 1) + i * QB
        first = start[:, i * QB : (i + 1) * QB]
        ok = (u >= first) & (u <= q)
        one = jnp.where(ok, 0.0, MASKED).astype(F32)
        bias[i, 0 : k1 - k0, 0:QB] = one
        bias[i, 0 : k1 - k0, QB : 2 * QB] = one


def both_heads(v, hd):
    lane = lax.broadcasted_iota(jnp.int32, v.shape, 1)
    zero = jnp.zeros_like(v)
    return jnp.concatenate([jnp.where(lane < hd, v, zero), jnp.where(lane < hd, zero, v)], axis=0)


def put_chunk(ref, k, v):
    h, c = v.shape[0], ref.shape[2]
    for m in range(v.shape[1] // c):
        ref[k, m * h : (m + 1) * h, :] = v[:, m * c : (m + 1) * c]


PRE = 3
CHUNKS = 12
F_Q1, F_Q2, F_AT, F_FC, F_NM, F_B1, F_A, F_O, F_B2, F_END = 0, 3, 6, 14, 18, 22, 26, 30, 34, 38
MESH = pl.DeviceIdType.MESH


def remote(src, dst, ss, rs, to):
    return pltpu.make_async_remote_copy(src, dst, ss, rs, device_id=to, device_id_type=MESH)


def head_lanes(scale, pair, shape, hd):
    lane = lax.broadcasted_iota(jnp.int32, shape, 1)
    return jnp.where(lane < hd, scale[2 * pair], scale[2 * pair + 1])


def front_kernel(lengths, scale, gain, offset, mg, mb, h_tok, h_cot, h_wqkv, h_wo, h_w1, h_w2,
                 o_x, o_nrm, o_qkv, o_sent, lse, o_ffn, o_gf, o_gp, o_gs, o_gh, o_out, o_keep, o_last, pre, small,
                 wb, wo, xb, cotb, nrm, qkvb, sent, bias, act, mid, nmid, gfb, r_mid, r_cot, n1, n2, hid, acc, ffn,
                 sendw, keepw, s1, s2, smid, ta, tb, wsem, lsem, osem, ss, rs):
    tick = pl.program_id(0)
    me = lax.axis_index("rows")
    ctx = lax.axis_index("ctx")
    core = lax.rem(me, 2)
    sibling = (me + 1 - 2 * core, ctx)
    other_ctx = (me, 1 - ctx)
    t, d = xb.shape
    seg = t // 2
    blocks = act.shape[0]
    width = blocks * act.shape[2]
    h = d // 2

    def rows_of(c):
        return pl.ds(pl.multiple_of(c * seg, seg), seg)

    def w_copy(ref, i):
        return pltpu.make_async_copy(ref, wb.at[lax.rem(i, 3)], wsem.at[lax.rem(i, 3)])

    def col(ref, i):
        return ref.at[:, pl.ds(pl.multiple_of(i * d, d), d)]

    def row(ref, i):
        return ref.at[pl.ds(pl.multiple_of(i * d, d), d), :]

    def w_start(i):
        pl.when(i < 6)(lambda: w_copy(col(h_wqkv, lax.rem(i, 3)), i).start())
        pl.when((i >= 6) & (i < 10))(lambda: w_copy(col(h_w1, i - 6), i).start())
        pl.when((i >= 10) & (i < 18))(lambda: w_copy(row(h_w2, lax.rem(i - 10, 4)), i).start())
        pl.when((i >= 18) & (i < 22))(lambda: w_copy(col(h_w1, i - 18), i).start())

    def w_next(i):
        w_copy(row(h_w2, 0), i).wait()
        w_start(i + 2)
        return wb.at[lax.rem(i, 3)]

    def tok_copy():
        return remote(h_tok.at[1 - ctx], xb.at[rows_of(ctx)], ss.at[0], rs.at[0], other_ctx)

    def cot_copy():
        return remote(h_cot.at[1 - ctx], cotb.at[rows_of(ctx)], ss.at[1], rs.at[1], other_ctx)

    def cot_core():
        return remote(cotb, r_cot, ss.at[2], rs.at[2], sibling)

    def mid_core(i):
        return remote(mid.at[2 * i + 1 - core], r_mid.at[i], ss.at[3 + i], rs.at[3 + i], sibling)

    def pre_copy(k):
        return remote(sendw.at[k], pre.at[k], ss.at[5 + k], rs.at[5 + k], other_ctx)

    def load_copy(j):
        src, dst = [(h_tok.at[ctx], xb.at[rows_of(ctx)]), (h_cot.at[ctx], cotb.at[rows_of(ctx)]), (h_wo, wo)][j]
        return pltpu.make_async_copy(src, dst, lsem.at[j])

    outs = [(xb, o_x), (nrm, o_nrm), (qkvb, o_qkv), (sent, o_sent), (ffn, o_ffn), (qkvb.at[0], o_gp), (qkvb.at[1], o_gs),
            (hid, o_gh), (qkvb.at[2], o_out), (keepw, o_keep), (sendw.at[pl.ds(PRE, 1)], o_last), (gfb, o_gf)]

    def out_copy(j):
        return pltpu.make_async_copy(outs[j][0], outs[j][1], osem.at[j])

    @pl.when(tick == 0)
    def _():
        barrier = pltpu.get_barrier_semaphore()
        for p in (other_ctx, sibling):
            pl.semaphore_signal(barrier, inc=1, device_id=p, device_id_type=MESH)
        load_copy(0).start()
        w_start(0)
        w_start(1)
        load_copy(1).start()
        load_copy(2).start()
        pl.semaphore_wait(barrier, 2)
        tok_copy().start()
        cot_copy().start()
        small[...] = jnp.zeros_like(small)
        at = lax.broadcasted_iota(jnp.int32, (1, t), 1)
        start = jnp.zeros((1, t), jnp.int32)
        bound = jnp.int32(0)
        for i in range(lengths.shape[1]):
            bound = bound + lengths[ctx, i]
            start = jnp.where(at >= bound, bound, start)
        fill_bias(start, bias, t)
        load_copy(0).wait()

    @pl.when(tick == F_Q2)
    def _():
        tok_copy().wait_recv()
        out_copy(0).start()

    for own in (True, False):
        first = F_Q1 if own else F_Q2
        here = rows_of(ctx if own else 1 - ctx)

        @pl.when(tick == first)
        def _(here=here):
            n, _ = ln_stats(xb[here, :].astype(F32))
            nrm[here, :] = (n * gain[0:1, :] + offset[0:1, :]).astype(BF)

        @pl.when((tick >= first) & (tick < first + 3))
        def _(here=here, first=first):
            w = w_next(tick)
            qkvb[tick - first, here, :] = dot(nrm[here, :], w[...], 1, 0).astype(BF)

    @pl.when(tick == F_AT)
    def _():
        out_copy(1).start()
        out_copy(2).start()
        cot_copy().wait_recv()
        load_copy(1).wait()
        cot_core().start()

    @pl.when((tick >= F_AT) & (tick < F_FC))
    def _():
        pair = tick - F_AT
        hd = 64
        at = pl.ds(pl.multiple_of(pair * 128, 128), 128)
        vt = qkvb[2, :, at].astype(F32).T.astype(BF)
        sc = head_lanes(scale, pair, (1, 128), hd)
        for i in range(t // QB):
            k0, k1 = key_range(i)
            qs = slice(i * QB, (i + 1) * QB)
            qm = (both_heads(qkvb[0, qs, at], hd) * (hd**-0.5)).astype(BF)
            st = dot(qkvb[1, k0:k1, at], qm, 1, 1) + bias[i, 0 : k1 - k0, :]
            top = jnp.max(st, axis=0, keepdims=True)
            pt = jnp.exp(st - top)
            total = jnp.sum(pt, axis=0, keepdims=True)
            ot = dot(vt[:, k0:k1], pt.astype(BF), 1, 0) * (1.0 / total)
            o = jnp.concatenate([ot[0:hd, 0:QB], ot[hd:, QB:]], axis=0).T
            sent[qs, at] = (o * sc).astype(BF)
            ls = top + jnp.log(total)
            lse[pair, 0:1, qs] = ls[:, 0:QB]
            lse[pair, 1:2, qs] = ls[:, QB:]

    @pl.when(tick == F_FC)
    def _():
        out_copy(3).start()
        load_copy(2).wait()
        n, inv = ln_stats(dot(sent[...], wo[...], 1, 0))
        n1[...] = n
        s1[...] = inv
        hidden = xb[...].astype(F32) + n * gain[1:2, :] + offset[1:2, :]
        hid[...] = hidden
        n, inv = ln_stats(hidden)
        n2[...] = n
        s2[...] = inv
        ffn[...] = (n * gain[2:3, :] + offset[2:3, :]).astype(BF)
        ta[...] = jnp.zeros_like(ta)
        out_copy(4).start()

    @pl.when((tick >= F_FC) & (tick < F_NM))
    def _():
        i = tick - F_FC
        w = w_next(6 + i)
        f = dot(ffn[...], w[...], 1, 0)
        phi = 0.5 + 0.5 * lax.erf(f * (0.5**0.5))
        a = f * phi
        gfb[i] = (phi + f * (jnp.exp(-0.5 * f * f) * 0.3989422804014327)).astype(BF)
        act[i] = a
        ta[...] += jnp.sum(a, axis=-1, keepdims=True)

    @pl.when(tick == F_NM)
    def _():
        mean = ta[...] * (1.0 / width)
        sq = jnp.zeros_like(mean)
        for j in range(blocks):
            c = act[j] - mean
            act[j] = c
            sq += jnp.sum(c * c, axis=-1, keepdims=True)
        smid[...] = lax.rsqrt(sq * (1.0 / width) + EPS)
        ta[...] = jnp.zeros_like(ta)
        tb[...] = jnp.zeros_like(tb)

    @pl.when((tick >= F_NM) & (tick < F_B1))
    def _():
        i = tick - F_NM
        n = act[i] * smid[...]
        nmid[i] = n.astype(BF)
        vec = pl.ds(pl.multiple_of(i * d, d), d)
        mid[i] = (n * mg[:, vec] + mb[:, vec]).astype(BF)
        pl.when(lax.rem(i, 2) == 1 - core)(lambda: mid_core(i // 2).start())

    @pl.when(tick == F_B1)
    def _():
        out_copy(1).wait()
        out_copy(2).wait()

    @pl.when((tick >= F_B1) & (tick < F_A))
    def _():
        i = tick - F_B1
        w = w_next(10 + i)
        e = dot(cotb[...], w[...], 1, 1)
        n = nmid[i].astype(F32)
        vec = pl.ds(pl.multiple_of(i * d, d), d)
        small[pl.ds(6 + i, 1), :] = colsum(e * n)
        small[pl.ds(6 + blocks + i, 1), :] = colsum(e)
        a = e * mg[:, vec]
        act[i] = a
        ta[...] += jnp.sum(a, axis=-1, keepdims=True)
        tb[...] += jnp.sum(a * n, axis=-1, keepdims=True)

    @pl.when(tick == F_A)
    def _():
        cot_core().wait_recv()
        mid_core(0).wait_recv()
        mid_core(1).wait_recv()

    @pl.when((tick >= F_A) & (tick < F_O))
    def _():
        k = tick - F_A
        a_at = pl.ds(pl.multiple_of((k // 2) * h, h), h)
        b_at = pl.ds(pl.multiple_of(lax.rem(k, 2) * h, h), h)
        for far in (True, False):
            x = 1 - ctx if far else ctx
            v = dot(mid[2 * x + core, :, a_at], cotb[:, b_at], 0, 0) + dot(r_mid[x, :, a_at], r_cot[:, b_at], 0, 0)
            put_chunk(sendw if far else keepw, k, v.astype(BF))
            if far:
                pl.when(k < PRE)(lambda: pre_copy(k).start())

    @pl.when(tick == F_O)
    def _():
        out_copy(9).start()
        out_copy(10).start()

    @pl.when((tick >= F_O) & (tick < F_B2))
    def _():
        i = tick - F_O
        w = w_next(14 + i)
        hid[...] += dot(mid[i], w[...], 1, 0)

    @pl.when(tick == F_B2 - 1)
    def _():
        qkvb[2] = hid[...].astype(BF)
        out_copy(8).start()

    @pl.when((tick >= F_B2) & (tick < F_END))
    def _():
        i = tick - F_B2
        w = w_next(18 + i)
        n = nmid[i].astype(F32)
        a = act[i] - ta[...] * (1.0 / width) - n * (tb[...] * (1.0 / width))
        gf = (a * smid[...] * gfb[i].astype(F32)).astype(BF)
        gfb[i] = gf
        v = dot(gf, w[...], 1, 1)

        @pl.when(i == 0)
        def _():
            acc[...] = v

        @pl.when(i > 0)
        def _():
            acc[...] += v

    @pl.when(tick == F_END - 1)
    def _():
        out_copy(11).start()
        e = acc[...]
        n = n2[...]
        small[2:3, :] = colsum(e * n)
        small[5:6, :] = colsum(e)
        gh = cotb[...].astype(F32) + ln_back(e, gain[2:3, :], n, s2[...])
        hid[...] = gh
        out_copy(7).start()
        n = n1[...]
        small[1:2, :] = colsum(gh * n)
        small[4:5, :] = colsum(gh)
        gp = ln_back(gh, gain[1:2, :], n, s1[...]).astype(BF)
        qkvb[0] = gp
        out_copy(5).start()
        qkvb[1] = dot(gp, wo[...], 1, 1).astype(BF)
        out_copy(6).start()
        for j in (0, 3, 4, 5, 6, 7, 8, 9, 10, 11):
            out_copy(j).wait()
        tok_copy().wait_send()
        cot_copy().wait_send()
        cot_core().wait_send()
        mid_core(0).wait_send()
        mid_core(1).wait_send()
        for k in range(PRE):
            pre_copy(k).wait()


def front_call(rows, cols, lengths, scale, gain, offset, mg, mb, tok, cot, wqkv, wo, w1, w2):
    seg, d = tok.shape[1:]
    t = 2 * seg
    ff = w1.shape[1]
    blocks = ff // d
    pairs = d // 128
    any_ = pl.BlockSpec(memory_space=pl.ANY)
    smem = pl.BlockSpec(memory_space=pltpu.SMEM)
    whole = lambda shape: pl.BlockSpec(shape, lambda i: (0,) * len(shape))
    vm = lambda *shape: pltpu.VMEM(shape, BF)
    vf = lambda *shape: pltpu.VMEM(shape, F32)
    dma = lambda n: pltpu.SemaphoreType.DMA((n,))
    small = (6 + 2 * blocks + 2, d)
    td = struct((t, d), BF)
    return pl.pallas_call(
        front_kernel,
        grid=(F_END,),
        in_specs=[smem, smem, whole((3, d)), whole((3, d)), whole((1, ff)), whole((1, ff))] + [any_] * 6,
        out_specs=[any_] * 4 + [whole((pairs, 2, t))] + [any_] * 9 + [whole(small)],
        out_shape=[
            td, td, struct((3, t, d), BF), td, struct((pairs, 2, t), F32), td, struct((blocks, t, d), BF), td, td,
            struct((t, d), F32), td, struct((4, rows, cols), BF), struct((1, rows, cols), BF),
            struct((PRE, rows, cols), BF), struct(small, F32),
        ],
        scratch_shapes=[
            vm(3, d, d), vm(d, d), vm(t, d), vm(t, d), vm(t, d), vm(3, t, d), vm(t, d), vf(t // QB, QB + REACH, 2 * QB),
            vf(blocks, t, d), vm(blocks, t, d), vm(blocks, t, d), vm(blocks, t, d), vm(2, t, d), vm(t, d),
            vf(t, d), vf(t, d), vf(t, d), vf(t, d), vm(t, d), vm(4, rows, cols), vm(4, rows, cols),
            vf(t, 1), vf(t, 1), vf(t, 1), vf(t, 1), vf(t, 1), dma(3), dma(3), dma(12), dma(8), dma(8),
        ],
        compiler_params=pltpu.CompilerParams(collective_id=1, has_side_effects=True, vmem_limit_bytes=60 * 2**20),
    )(lengths, scale, gain, offset, mg, mb, tok, cot, wqkv, wo, w1, w2)


def factors_of(n):
    out, want, rest = [2], 2, n // 2
    while rest > 1:
        f = min(want, rest)
        out.append(f)
        rest //= f
        want *= 2
    return out


T_ATT, T_WO, T_W1, T_WQ, T_IN, T_TAIL = 0, 8, 9, 13, 16, 22


DEPTH = 2
EVENT_TICKS = (0, 1, 2, 3, 8, 10, 12, 14, 16, 18, 20)


def event_at(i):
    done = jnp.maximum(i - T_TAIL, 0)
    for at in EVENT_TICKS:
        done = done + jnp.where(i > at, 1, 0)
    return done


def tick_count(n_events):
    return T_TAIL + n_events - len(EVENT_TICKS)


def main_kernel(factors, lengths, scale, q, k, v, gs, sn, lse, wq, gain,
                h_sent, h_ffn, h_gf, h_gp, h_nrm, h_last, h_keep, h_pre, h_x, h_ghid, h_small, h_out,
                out, gx_own, gx_got, small_out, out_got, *scr):
    tick = pl.program_id(0)
    n_rs = len(factors)
    chunks, rows, cols = out.shape[0], out.shape[2], out.shape[3]
    t, d = h_sent.shape
    hd2 = d // 2
    me = lax.axis_index("rows")
    ctx = lax.axis_index("ctx")
    fs = [2] + factors[1:]
    strides, st = [0], 2
    for f in factors[1:]:
        strides.append(st)
        st *= f
    size = [rows]
    for f in fs[1:]:
        size.append(size[-1] // f)
    pos = [ctx] + [lax.rem(me // strides[i], fs[i]) for i in range(1, n_rs)]
    off = [0]
    for i in range(1, n_rs):
        off.append(off[-1] + pos[i] * size[i])
    bits = []
    b = 1
    while b < lax.axis_size("rows"):
        bits.append(b)
        b *= 2

    def peer(i, j):
        if i == 0:
            return (me, 1 - ctx)
        return (me + ((pos[i] ^ j) - pos[i]) * strides[i], ctx)

    core = lax.rem(me, 2)
    sibling = (me + 1 - 2 * core, ctx)
    other_ctx = (me, 1 - ctx)

    def bit_peer(b):
        return (me + b - 2 * b * lax.rem(me // b, 2), ctx)

    scr = list(scr)
    take = lambda n: [scr.pop(0) for _ in range(n)]
    sendb, acc, gath = take(3)
    recv = [gath] + take(n_rs - 1)
    small_acc, small_recv = take(2)
    o_sent, o_ffn, o_gf, o_gp, o_nrm = take(5)
    r_sent, r_ffn, r_gf, r_gp, r_nrm, r_gq = take(6)
    gall, bias, gk, gv, gqt, xb, gh, gn_acc, gx_send = take(9)
    rs_s, rs_r = take(n_rs), take(n_rs)
    ag_s, ag_r = [None] + take(n_rs - 1), [None] + take(n_rs - 1)
    core_s, core_r, loc, small_s, small_r, swap_s, swap_r, load, gx_s, gx_r = take(10)

    def part(at, n):
        return pl.ds(at if isinstance(at, int) else pl.multiple_of(at, 16), n)

    def rs_copy(i, c, j):
        if i == 0:
            src, dst = sendb.at[c - PRE], gath.at[c]
        else:
            src = acc.at[c, part(off[i - 1] + (pos[i] ^ j) * size[i], size[i])]
            dst = recv[i].at[c, j - 1]
        return remote(src, dst, rs_s[i].at[c, j - 1], rs_r[i].at[c, j - 1], peer(i, j))

    def ag_copy(i, c, j, arriving):
        at = off[i - 1] + (pos[i] ^ j) * size[i] if arriving else off[i]
        ref = gath.at[c, part(at, size[i])]
        return remote(ref, ref, ag_s[i].at[c, j - 1], ag_r[i].at[c, j - 1], peer(i, j))

    def core_copy(c, arriving):
        to = 1 - core if arriving else core
        return remote(gath.at[c], out.at[c, to], core_s.at[c], core_r.at[c], sibling)

    def own_copy(c):
        return pltpu.make_async_copy(gath.at[c], out.at[c, core], loc.at[c])

    def reduce_stage(i, c):
        if i == 0:
            @pl.when(c >= PRE)
            def _():
                rs_copy(0, c, 1).wait_recv()
        else:
            for j in range(1, fs[i]):
                rs_copy(i, c, j).wait_recv()
        here = part(off[i], size[i])
        val = acc[c, here].astype(F32)
        if i == 0:
            val = val + gath[c].astype(F32)
        else:
            for j in range(1, fs[i]):
                val = val + recv[i][c, j - 1].astype(F32)
        if i + 1 < n_rs:
            acc[c, here] = val.astype(BF)
            for j in range(1, fs[i + 1]):
                rs_copy(i + 1, c, j).start()
        else:
            gath[c, here] = val.astype(BF)
            for j in range(1, fs[i]):
                ag_copy(i, c, j, False).start()

    def gather_stage(i, c):
        for j in range(1, fs[i]):
            ag_copy(i, c, j, True).wait_recv()
        if i > 1:
            for j in range(1, fs[i - 1]):
                ag_copy(i - 1, c, j, False).start()
        else:
            core_copy(c, False).start()
            own_copy(c).start()

    def small_copy(i):
        to = other_ctx if i == 0 else bit_peer(bits[i - 1])
        return remote(small_acc.at[i], small_recv.at[i], small_s.at[i], small_r.at[i], to)

    mine = pl.ds(pl.multiple_of(core * hd2, hd2), hd2)
    theirs = pl.ds(pl.multiple_of((1 - core) * hd2, hd2), hd2)
    swaps = [(h_sent, r_sent), (h_gp.at[:, theirs], r_gp), (h_ffn, r_ffn), (h_gf.at[1 - core], r_gf.at[0]), (h_nrm, r_nrm),
             (h_gf.at[3 - core], r_gf.at[1])]
    loads = [(h_sent, o_sent), (h_gp.at[:, mine], o_gp), (h_ffn, o_ffn), (h_gf.at[core], o_gf.at[0]), (h_nrm, o_nrm),
             (h_x, xb), (h_ghid, gh), (h_small, small_acc.at[0]), (h_last.at[0], sendb.at[0]),
             (h_keep, acc.at[pl.ds(0, 4)]), (h_pre, gath.at[pl.ds(0, PRE)]), (h_gf.at[2 + core], o_gf.at[1])]

    def swap_copy(j):
        return remote(swaps[j][0], swaps[j][1], swap_s.at[j], swap_r.at[j], sibling)

    def gq_copy():
        return remote(gall.at[1 - core], r_gq, swap_s.at[6], swap_r.at[6], sibling)

    def load_copy(j):
        return pltpu.make_async_copy(loads[j][0], loads[j][1], load.at[j])

    seg = t // 2

    def rows_of(c):
        return pl.ds(pl.multiple_of(c * seg, seg), seg)

    def gx_copy():
        return remote(gx_send, gx_got, gx_s.at[0], gx_r.at[0], other_ctx)

    def out_copy():
        return remote(h_out.at[rows_of(1 - ctx)], out_got, gx_s.at[1], gx_r.at[1], other_ctx)

    @pl.when(tick == 0)
    def _():
        peers = [other_ctx, sibling]
        for i in range(1, n_rs):
            peers += [peer(i, j) for j in range(1, fs[i])]
        barrier = pltpu.get_barrier_semaphore()
        for p in peers:
            pl.semaphore_signal(barrier, inc=1, device_id=p, device_id_type=MESH)
        for j in (10, 9, 8, 0, 1, 2, 3, 11, 4, 5, 6, 7):
            load_copy(j).start()
        pl.semaphore_wait(barrier, len(peers))
        for j in (0, 1, 2, 3, 5, 4):
            swap_copy(j).start()
        for j in (10, 9, 8):
            load_copy(j).wait()
        rs_copy(0, PRE, 1).start()
        out_copy().start()
        at = lax.broadcasted_iota(jnp.int32, (1, t), 1)
        start = jnp.zeros((1, t), jnp.int32)
        bound = jnp.int32(0)
        for i in range(lengths.shape[1]):
            bound = bound + lengths[ctx, i]
            start = jnp.where(at >= bound, bound, start)
        fill_bias(start, bias, t)
        load_copy(7).wait()

    @pl.when(tick < T_WO)
    def _():
        hd = q.shape[2] // 2
        kt = k[0].astype(F32).T.astype(BF)
        gsf = gs[...].astype(F32)
        prod = (gsf * sn[...].astype(F32)).T
        d0 = jnp.sum(prod[0:hd], axis=0, keepdims=True)
        d1 = jnp.sum(prod[hd:], axis=0, keepdims=True)
        lane = lax.broadcasted_iota(jnp.int32, (1, d), 1)
        h0 = jnp.sum(d0, axis=-1, keepdims=True)
        h1 = jnp.sum(d1, axis=-1, keepdims=True)
        small_acc[0, 14:15, :] += jnp.where(lane == 2 * tick, h0, 0.0) + jnp.where(lane == 2 * tick + 1, h1, 0.0)
        ga = (gsf * head_lanes(scale, tick, (1, 2 * hd), hd)).astype(BF)
        gk[...] = jnp.zeros_like(gk)
        gv[...] = jnp.zeros_like(gv)
        for i in range(t // QB):
            k0, k1 = key_range(i)
            qs = slice(i * QB, (i + 1) * QB)
            qm = (both_heads(q[0, qs, :], hd) * (hd**-0.5)).astype(BF)
            gm = both_heads(ga[qs, :], hd)
            sc = dot(k[0, k0:k1, :], qm, 1, 1) + bias[i, 0 : k1 - k0, :]
            ls = jnp.concatenate([lse[0, 0:1, qs], lse[0, 1:2, qs]], axis=1)
            dd = jnp.concatenate([d0[:, qs], d1[:, qs]], axis=1)
            pt = jnp.exp(sc - ls)
            gp = dot(v[0, k0:k1, :], gm, 1, 1)
            ds = (pt * (gp - dd)).astype(BF)
            gv[k0:k1, :] += dot(pt.astype(BF), gm, 1, 0)
            gk[k0:k1, :] += dot(ds, qm, 1, 0)
            gq = dot(kt[:, k0:k1], ds, 1, 0) * (hd**-0.5)
            gqt[:, qs] = jnp.concatenate([gq[0:hd, 0:QB], gq[hd:, QB:]], axis=0)
        half = tick // (T_WO // 2)
        at = pl.ds(pl.multiple_of(lax.rem(tick, T_WO // 2) * 128, 128), 128)
        gall[half, 0, :, at] = gqt[...].T.astype(BF)
        gall[half, 1, :, at] = gk[...].astype(BF)
        gall[half, 2, :, at] = gv[...].astype(BF)

    @pl.when(tick == T_WO - 1)
    def _():
        gq_copy().start()

    def wgrad(c, a0, a1, b0, b1):
        for far in (True, False):
            x = 1 - ctx if far else ctx
            val = (dot(a0(x), b0, 0, 0) + dot(a1(x), b1, 0, 0)).astype(BF)
            put_chunk(sendb if far else acc, c - PRE if far else c, val)
            if far:
                rs_copy(0, c, 1).start()

    def half_of(ref):
        return lambda x: ref[:, pl.ds(pl.multiple_of(x * hd2, 128), hd2)]

    @pl.when(tick == T_WO)
    def _():
        for j in (0, 1):
            load_copy(j).wait()
            swap_copy(j).wait_recv()
        wgrad(4, half_of(o_sent), half_of(r_sent), o_gp[...], r_gp[...])

    @pl.when(tick == T_W1)
    def _():
        for j in (2, 3):
            load_copy(j).wait()
            swap_copy(j).wait_recv()
        load_copy(11).wait()
        swap_copy(5).wait_recv()

    @pl.when((tick >= T_W1) & (tick < T_WQ))
    def _():
        c = tick - T_W1
        b = lambda ref: ref[c // 2, :, pl.ds(pl.multiple_of(lax.rem(c, 2) * hd2, 128), hd2)]
        wgrad(c + 5, half_of(o_ffn), half_of(r_ffn), b(o_gf), b(r_gf))

    @pl.when(tick == T_WQ)
    def _():
        load_copy(4).wait()
        swap_copy(4).wait_recv()
        gq_copy().wait_recv()

    @pl.when((tick >= T_WQ) & (tick < T_IN))
    def _():
        c = tick - T_WQ
        wgrad(c + 9, half_of(o_nrm), half_of(r_nrm), gall[core, c], r_gq[c])

    @pl.when((tick >= T_IN) & (tick < T_TAIL))
    def _():
        j = tick - T_IN
        val = dot(gall[lax.rem(j, 2), j // 2], wq[...], 1, 1)

        @pl.when(j == 0)
        def _():
            gn_acc[...] = val

        @pl.when(j > 0)
        def _():
            gn_acc[...] += val

    @pl.when(tick == T_TAIL - 1)
    def _():
        load_copy(5).wait()
        load_copy(6).wait()
        e = gn_acc[...]
        n, inv = ln_stats(xb[...].astype(F32))
        small_acc[0, 0:1, :] = colsum(e * n)
        small_acc[0, 3:4, :] = colsum(e)
        gh[...] += ln_back(e, gain[0:1, :], n, inv)
        gx_send[...] = gh[rows_of(1 - ctx), :].astype(BF)
        gx_copy().start()
        gx_own[...] = gh[rows_of(ctx), :]
        small_copy(0).start()

    def guarded(f, i, c):
        pl.when((c >= 0) & (c < chunks))(lambda: f(i, c))

    event = event_at(tick)
    fire = event_at(tick + 1) > event
    lanes = [(reduce_stage, i) for i in range(n_rs)] + [(gather_stage, i) for i in range(n_rs - 1, 0, -1)]

    @pl.when(fire)
    def _():
        for lag in range(len(lanes) - 1, -1, -1):
            f, i = lanes[lag]
            guarded(f, i, event - DEPTH * lag)

    for i in range(len(bits) + 1):

        @pl.when(tick == T_TAIL + 1 + i)
        def _(i=i):
            small_copy(i).wait_recv()
            if i < len(bits):
                small_acc[i + 1] = small_acc[i] + small_recv[i]
                small_copy(i + 1).start()
            else:
                small_out[...] = small_acc[i] + small_recv[i]

    @pl.when(tick == pl.num_programs(0) - 1)
    def _():
        def finish(c, _):
            for i in range(n_rs):
                for j in range(1, fs[i]):
                    if i == 0:
                        @pl.when(c >= PRE)
                        def _():
                            rs_copy(0, c, 1).wait_send()
                    else:
                        rs_copy(i, c, j).wait_send()
                        ag_copy(i, c, j, False).wait_send()
            core_copy(c, False).wait_send()
            core_copy(c, True).wait_recv()
            own_copy(c).wait()
            return 0

        lax.fori_loop(0, chunks, finish, 0)
        for i in range(len(bits) + 1):
            small_copy(i).wait_send()
        for j in range(6):
            swap_copy(j).wait_send()
        gq_copy().wait_send()
        gx_copy().wait()
        out_copy().wait()


def main_call(factors, rows, cols, lengths, scale, qkv, gsent, sent, lse, w_qkv, gain, ffn_in, gf, gp, normed, last,
              keep, pre, x, ghid, small, out):
    t, d = sent.shape
    h = d // 2
    n = 1
    for f in factors:
        n *= f
    fs = [2] + factors[1:]
    levels = 1
    while n > 1:
        levels += 1
        n //= 2
    size, recv = rows, []
    for f in fs[1:]:
        size //= f
        recv.append(pltpu.VMEM((CHUNKS, f - 1, size, cols), BF))
    dma = lambda *shape: pltpu.SemaphoreType.DMA(shape)
    per = lambda k: [dma(CHUNKS, f - 1) for f in fs[k:]]
    vm = lambda *shape: pltpu.VMEM(shape, BF)
    vf = lambda *shape: pltpu.VMEM(shape, F32)
    pair = lambda i: jnp.minimum(i, T_WO - 1)
    part = lambda j: pl.BlockSpec((1, t, 128), lambda i: (j, 0, pair(i)))
    flat = pl.BlockSpec((t, 128), lambda i: (0, pair(i)))
    whole = lambda shape: pl.BlockSpec(shape, lambda i: (0,) * len(shape))
    wcol = lambda i: jnp.clip(i - T_IN, 0, 5)
    any_ = pl.BlockSpec(memory_space=pl.ANY)
    lanes = 2 * len(fs) - 1
    events = CHUNKS + DEPTH * (lanes - 1)
    return pl.pallas_call(
        functools.partial(main_kernel, factors),
        grid=(tick_count(events),),
        in_specs=[
            pl.BlockSpec(memory_space=pltpu.SMEM), pl.BlockSpec(memory_space=pltpu.SMEM),
            part(0), part(1), part(2), flat, flat,
            pl.BlockSpec((1, 2, t), lambda i: (pair(i), 0, 0)),
            pl.BlockSpec((d, h), lambda i: (0, wcol(i))),
            whole((3, d)),
        ] + [any_] * 12,
        out_specs=[any_, whole((t // 2, d)), any_, whole(small.shape), any_],
        out_shape=[
            struct((CHUNKS, 2, rows, cols), BF), struct((t // 2, d), F32), struct((t // 2, d), BF), struct(small.shape, F32),
            struct((t // 2, d), BF),
        ],
        scratch_shapes=[vm(CHUNKS - PRE, rows, cols), vm(CHUNKS, rows, cols), vm(CHUNKS, rows, cols)]
        + recv
        + [vf(levels, *small.shape)] * 2
        + [vm(t, d), vm(t, d), vm(2, t, d), vm(t, h), vm(t, d)]
        + [vm(t, d), vm(t, d), vm(2, t, d), vm(t, h), vm(t, d), vm(3, t, h)]
        + [vm(2, 3, t, h), vf(t // QB, QB + REACH, 2 * QB), vf(t, 128), vf(t, 128), vf(128, t), vm(t, d), vf(t, d), vf(t, d),
           vm(t // 2, d)]
        + per(0) + per(0) + per(1) + per(1)
        + [dma(CHUNKS), dma(CHUNKS), dma(CHUNKS), dma(levels), dma(levels), dma(7), dma(7), dma(12), dma(2), dma(2)],
        compiler_params=pltpu.CompilerParams(collective_id=0, has_side_effects=True, vmem_limit_bytes=60 * 2**20),
    )(lengths, scale, qkv, qkv, qkv, gsent, sent, lse, w_qkv, gain,
      sent, ffn_in, gf, gp, normed, last, keep, pre, x, ghid, small, out)


def finish_kernel(got, g2, g1, go, gq):
    k = pl.program_id(0) // 2
    h = g2.shape[0]
    c = got.shape[3]

    def put(out):
        for m in range(h // c):
            out[:, m * c : (m + 1) * c] = got[0, 0, m * h : (m + 1) * h, :].astype(F32)

    pl.when(k < 4)(lambda: put(g2))
    pl.when(k == 4)(lambda: put(go))
    pl.when((k > 4) & (k < 9))(lambda: put(g1))
    pl.when(k > 8)(lambda: put(gq))


def finish_call(got, ff, d):
    h = d // 2
    rows, cols = got.shape[2:]

    def spec(lo, hi, at):
        def index(i):
            i = jnp.clip(i, 2 * lo, 2 * hi + 1)
            return at(i // 2 - lo, i % 2)

        return pl.BlockSpec((h, h), index)

    return pl.pallas_call(
        finish_kernel,
        grid=(24,),
        in_specs=[pl.BlockSpec((1, 1, rows, cols), lambda i: (i // 2, i % 2, 0, 0))],
        out_specs=[
            spec(0, 3, lambda k, c: (c * 2 + k // 2, k % 2)),
            spec(5, 8, lambda k, c: (0, ((k // 2) * 2 + c) * 2 + k % 2)),
            spec(4, 4, lambda k, c: (0, c)),
            spec(9, 11, lambda k, c: (0, k * 2 + c)),
        ],
        out_shape=[struct((ff // 2, d), F32), struct((h, ff), F32), struct((h, d), F32), struct((h, 3 * d), F32)],
        compiler_params=pltpu.CompilerParams(vmem_limit_bytes=60 * 2**20),
    )(got)


def local(
    tokens, cotangent, w_qkv, w_out, w_fc1, w_fc2, norm_gain, norm_bias, mid_gain, mid_bias, head_scale, doc_lengths
):
    n = lax.axis_size("rows")
    factors = factors_of(n)
    d = tokens.shape[2]
    ff = w_fc1.shape[1]
    heads = head_scale.shape[0]
    ctx = lax.axis_index("ctx")
    mg, mb = mid_gain[None, :], mid_bias[None, :]
    pieces = 1
    for f in factors[1:]:
        pieces *= f
    half = d // 2
    rows = max(half, 16 * pieces)
    cols = half * half // rows
    x, normed, qkv, sent, lse, ffn_in, gf, gp, gsent, ghid, out, keep, last, pre, small = front_call(
        rows, cols, doc_lengths, head_scale, norm_gain, norm_bias, mg, mb, tokens, cotangent, w_qkv, w_out, w_fc1, w_fc2
    )
    got, gx_own, gx_got, small, out_got = main_call(
        factors, rows, cols, doc_lengths, head_scale, qkv, gsent, sent, lse, w_qkv, norm_gain, ffn_in, gf, gp, normed, last,
        keep, pre, x, ghid, small, out,
    )
    g2, g1, go, gq = finish_call(got, ff, d)
    gx_got = gx_got.astype(F32)
    gx = jnp.stack([jnp.where(ctx == 0, gx_own, gx_got), jnp.where(ctx == 0, gx_got, gx_own)])

    def take(v, axis):
        size = v.shape[axis] // 2
        return lax.dynamic_slice_in_dim(v, ctx * size, size, axis)

    nm = ff // d
    gn = take(small[0:3], 1)
    bn = take(small[3:6], 1)
    gmg = take(small[6 : 6 + nm].reshape(-1), 0)
    gmb = take(small[6 + nm : 6 + 2 * nm].reshape(-1), 0)
    ghs = take(small[6 + 2 * nm, 0:heads] / head_scale, 0)

    seg = out_got.shape[0]
    out_own = lax.dynamic_slice_in_dim(out, ctx * seg, seg, 0)
    out = jnp.stack([jnp.where(ctx == 0, out_own, out_got), jnp.where(ctx == 0, out_got, out_own)])
    return (out, gx, gq, go, g1, g2, gn, bn, gmg, gmb, ghs)


def solution(mesh):
    rows = P("rows", "ctx", None)
    in_specs = (rows, rows) + (P(),) * 9 + (P("rows", None),)
    ctx0 = P("ctx", None)
    out_specs = (rows, rows, ctx0, ctx0, ctx0, ctx0, P(None, "ctx"), P(None, "ctx"), P("ctx"), P("ctx"), P("ctx"))
    return jax.shard_map(local, mesh=mesh, in_specs=in_specs, out_specs=out_specs, check_vma=False)
```

time: 1480 us -> 301 us (0.20)
  waiting for transfers between devices: 971 us -> 0 us
  Pallas kernels: 0 us -> 291 us
  matrix products: 209 us -> 0 us
  local copies, waits for them, and re-layouts: 125 us -> 2.45 us
  blocking collectives: 88.8 us -> 0 us
  other arithmetic: 48.8 us -> 4.2 us
  between operations: 16.3 us -> 0.74 us
    reduce_scatter x4 -> x0, waiting for transfers between devices: 486 us -> none  [the longest x1 192 us: local(): lax.psum_scatter(grad_fc2, 'ctx', scatter_dimension=0, tiled=True)]
    psum x1 -> x0, waiting for transfers between devices: 383 us -> none  [local(): lax.psum((share[0], share[1], share[2], share[3], share[4], share[5], sha...]
    pallas_call x0 -> x3, Pallas kernels: none -> 291 us  [the longest x1 171 us: main_call(): pl.pallas_call(functools.partial(main_kernel, factors), grid=(tick_count(...]
    dot_general x18 -> x0, matrix products: 209 us -> none  [the longest x4 37.9 us: times_transposed(): lax.dot_general(left_mat, right_mat, (((1,), (1,)), ((), ())), preferred_...]
    all_to_all x3 -> x0, waiting for transfers between devices: 95.7 us -> none  [the longest x1 36.7 us: local(): lax.all_to_all(qkv_local, 'ctx', split_axis=3, concat_axis=1, tiled=True)]
    psum x1 -> x0, blocking collectives: 65 us -> none  [local(): lax.psum((share[0], share[1], share[2], share[3], share[4], share[5], sha...]
    unnamed x116 -> x11, local copies, waits for them, and re-layouts: 56.7 us -> 0.03 us
    all_to_all x5 -> x0, local copies, waits for them, and re-layouts: 30.5 us -> none  [the longest x2 14.7 us: local(): lax.all_to_all(qkv_local, 'ctx', split_axis=3, concat_axis=1, tiled=True)]
  transfers between devices with their start and end apart: 10 -> 0, of which waited for: 8 -> 0; matrix products, arithmetic and copies ran while one was open for 12% -> 0% of each run, Pallas kernels for 0% -> 0%
where the time goes in v3:
time: 301 us; the launch traced here: 299 us
  Pallas kernels  291 us (97%)
  other arithmetic  4.2 us (1%)
    pallas_call x1, Pallas kernels, main_call(): pl.pallas_call(functools.partial(main_kernel, factors), grid=(tick_count(...  171 us
    pallas_call x1, Pallas kernels, front_call(): pl.pallas_call(front_kernel, grid=(F_END,), in_specs=[smem, smem, whole((...  98.8 us
    pallas_call x1, Pallas kernels, finish_call(): pl.pallas_call(finish_kernel, grid=(24,), in_specs=[pl.BlockSpec((1, 1, r...  21.3 us

profile of v3, /device:TPU:0, one launch (start us, length us, event | category | flops | bytes accessed | tf_op | source)
XLA Modules:
  0.0 298.7 jit_solution(16091391415065196063)
XLA Ops:
  0.7 98.8 %shard_map.203 = (bf16[512,1024]{1,0:T(8,128)(2,1)}, bf16[512,1024]{1,0:T(8,128)(2,1)}, bf16[3,512,1024]{2,1,0:T(8,128)(2,1)}, bf16[512,1024]{1,0:T(8,128)(2,1)}...) custom-call(s32[2,4]{1,0:T(2,128)} %lengths.3, ...), custom_call_target="tpu_custom_call" | custom-call | tf_op jit(solution)/shard_map/pallas_call | solution.py:385
  99.5 0.0 copy-start
  99.5 171.2 %shard_map.204 = (bf16[12,2,512,512]{3,2,1,0:T(8,128)(2,1)}, f32[256,1024]{1,0:T(8,128)}, bf16[256,1024]{1,0:T(8,128)(2,1)}, f32[16,1024]{1,0:T(8,128)}, bf16[256,1024]{1,0:T(8,128)(2,1)}) custom-call(s32[2,4]{1,0:T(2,128)} %lengths.3, f32[16]{0:T(128)} %scale.3, bf16[3,512,1024]{2,1,0:T(8,128)(2,1)} %get-tuple-element.36.q.k.v, ...), custom_call_target="tpu_custom_call" | custom-call | tf_op jit(solution)/shard_map/pallas_call | solution.py:789
  270.7 0.0 copy-start.3
  270.7 0.0 copy-start.4
  270.7 0.0 copy-start.1
  270.7 0.0 copy-start.2
  270.7 0.0 copy-done
  270.7 1.4 select_bitcast_fusion.1
  272.2 1.1 pad_maximum_fusion.1
  273.2 0.0 copy-done.3
  273.2 0.0 copy-done.4
  273.2 0.6 dynamic_slice.23
  273.9 0.6 constant_dynamic-slice_fusion
  274.5 0.6 dynamic_slice.22
  275.1 0.6 dynamic_slice.21
  275.7 0.0 copy-done.1
  275.7 0.0 copy-done.2
  275.7 0.3 fusion
  275.9 1.5 pad_maximum_fusion
  277.4 21.3 %shard_map.205 = (f32[2048,1024]{1,0:T(8,128)}, f32[512,4096]{1,0:T(8,128)}, f32[512,1024]{1,0:T(8,128)}, f32[512,3072]{1,0:T(8,128)}) custom-call(bf16[12,2,512,512]{3,2,1,0:T(8,128)(2,1)} %get-tuple-element.53.got), custom_call_target="tpu_custom_call" | custom-call | tf_op jit(solution)/shard_map/pallas_call | solution.py:844
  (4 shorter events, 0.0 us)
Async XLA Ops:
  99.5 171.2 %copy-start = (bf16[512,1024]{1,0:T(8,128)(2,1)S(1)}, bf16[512,1024]{1,0:T(8,128)(2,1)}, u32[]{:S(2)}) copy-start(bf16[512,1024]{1,0:T(8,128)(2,1)} %get-tuple-element.35.h_out) | copy-start | bytes 3145732
  270.7 2.5 copy-start.3
  270.7 2.5 copy-start.4
  270.7 5.0 %copy-start.1 = (f32[256,1024]{1,0:T(8,128)S(1)}, f32[256,1024]{1,0:T(8,128)}, u32[]{:S(2)}) copy-start(f32[256,1024]{1,0:T(8,128)} %get-tuple-element.51) | copy-start | bytes 3145732
  270.7 5.0 %copy-start.2 = (bf16[256,1024]{1,0:T(8,128)(2,1)S(1)}, bf16[256,1024]{1,0:T(8,128)(2,1)}, u32[]{:S(2)}) copy-start(bf16[256,1024]{1,0:T(8,128)(2,1)} %get-tuple-element.52) | copy-start | bytes 1572868

commit v4 on v3

--- a/solution.py
+++ b/solution.py
@@ -65,13 +65,18 @@
 
 def put_chunk(ref, k, v):
     h, c = v.shape[0], ref.shape[2]
-    for m in range(v.shape[1] // c):
-        ref[k, m * h : (m + 1) * h, :] = v[:, m * c : (m + 1) * c]
-
-
-PRE = 3
-CHUNKS = 12
-F_Q1, F_Q2, F_AT, F_FC, F_NM, F_B1, F_A, F_O, F_B2, F_END = 0, 3, 6, 14, 18, 22, 26, 30, 34, 38
+    groups = ref.shape[1] // h
+    for j in range(SUB):
+        for m in range(groups):
+            at = (j * groups + m) * c
+            ref[SUB * k + j, m * h : (m + 1) * h, :] = v[:, at : at + c]
+
+
+BLOCKS = 12
+SUB = 2
+CHUNKS = BLOCKS * SUB
+PRE = 3 * SUB
+F_Q1, F_Q2, F_AT, F_FC, F_NM, F_A, F_B1, F_O, F_B2, F_END = 0, 3, 6, 14, 18, 22, 26, 30, 34, 38
 MESH = pl.DeviceIdType.MESH
 
 
@@ -143,7 +148,7 @@
         return pltpu.make_async_copy(src, dst, lsem.at[j])
 
     outs = [(xb, o_x), (nrm, o_nrm), (qkvb, o_qkv), (sent, o_sent), (ffn, o_ffn), (qkvb.at[0], o_gp), (qkvb.at[1], o_gs),
-            (hid, o_gh), (qkvb.at[2], o_out), (keepw, o_keep), (sendw.at[pl.ds(PRE, 1)], o_last), (gfb, o_gf)]
+            (hid, o_gh), (qkvb.at[2], o_out), (keepw, o_keep), (sendw.at[pl.ds(PRE, 4 * SUB - PRE)], o_last), (gfb, o_gf)]
 
     def out_copy(j):
         return pltpu.make_async_copy(outs[j][0], outs[j][1], osem.at[j])
@@ -261,19 +266,20 @@
 
     @pl.when((tick >= F_NM) & (tick < F_B1))
     def _():
-        i = tick - F_NM
+        j = tick - F_NM
+        i = lax.rem(j, 2) * 2 + jnp.where(j < 2, 1 - core, core)
         n = act[i] * smid[...]
         nmid[i] = n.astype(BF)
         vec = pl.ds(pl.multiple_of(i * d, d), d)
         mid[i] = (n * mg[:, vec] + mb[:, vec]).astype(BF)
-        pl.when(lax.rem(i, 2) == 1 - core)(lambda: mid_core(i // 2).start())
-
-    @pl.when(tick == F_B1)
+        pl.when(j < 2)(lambda: mid_core(j).start())
+
+    @pl.when(tick == F_A)
     def _():
         out_copy(1).wait()
         out_copy(2).wait()
 
-    @pl.when((tick >= F_B1) & (tick < F_A))
+    @pl.when((tick >= F_B1) & (tick < F_O))
     def _():
         i = tick - F_B1
         w = w_next(10 + i)
@@ -293,7 +299,7 @@
         mid_core(0).wait_recv()
         mid_core(1).wait_recv()
 
-    @pl.when((tick >= F_A) & (tick < F_O))
+    @pl.when((tick >= F_A) & (tick < F_B1))
     def _():
         k = tick - F_A
         a_at = pl.ds(pl.multiple_of((k // 2) * h, h), h)
@@ -303,7 +309,9 @@
             v = dot(mid[2 * x + core, :, a_at], cotb[:, b_at], 0, 0) + dot(r_mid[x, :, a_at], r_cot[:, b_at], 0, 0)
             put_chunk(sendw if far else keepw, k, v.astype(BF))
             if far:
-                pl.when(k < PRE)(lambda: pre_copy(k).start())
+                for j in range(SUB):
+                    c = SUB * k + j
+                    pl.when(c < PRE)(lambda c=c: pre_copy(c).start())
 
     @pl.when(tick == F_O)
     def _():
@@ -389,45 +397,63 @@
         out_specs=[any_] * 4 + [whole((pairs, 2, t))] + [any_] * 9 + [whole(small)],
         out_shape=[
             td, td, struct((3, t, d), BF), td, struct((pairs, 2, t), F32), td, struct((blocks, t, d), BF), td, td,
-            struct((t, d), F32), td, struct((4, rows, cols), BF), struct((1, rows, cols), BF),
+            struct((t, d), F32), td, struct((4 * SUB, rows, cols), BF), struct((4 * SUB - PRE, rows, cols), BF),
             struct((PRE, rows, cols), BF), struct(small, F32),
         ],
         scratch_shapes=[
             vm(3, d, d), vm(d, d), vm(t, d), vm(t, d), vm(t, d), vm(3, t, d), vm(t, d), vf(t // QB, QB + REACH, 2 * QB),
             vf(blocks, t, d), vm(blocks, t, d), vm(blocks, t, d), vm(blocks, t, d), vm(2, t, d), vm(t, d),
-            vf(t, d), vf(t, d), vf(t, d), vf(t, d), vm(t, d), vm(4, rows, cols), vm(4, rows, cols),
-            vf(t, 1), vf(t, 1), vf(t, 1), vf(t, 1), vf(t, 1), dma(3), dma(3), dma(12), dma(8), dma(8),
+            vf(t, d), vf(t, d), vf(t, d), vf(t, d), vm(t, d), vm(4 * SUB, rows, cols), vm(4 * SUB, rows, cols),
+            vf(t, 1), vf(t, 1), vf(t, 1), vf(t, 1), vf(t, 1), dma(3), dma(3), dma(12), dma(5 + PRE), dma(5 + PRE),
         ],
         compiler_params=pltpu.CompilerParams(collective_id=1, has_side_effects=True, vmem_limit_bytes=60 * 2**20),
     )(lengths, scale, gain, offset, mg, mb, tok, cot, wqkv, wo, w1, w2)
 
 
 def factors_of(n):
-    out, want, rest = [2], 2, n // 2
-    while rest > 1:
-        f = min(want, rest)
-        out.append(f)
-        rest //= f
-        want *= 2
+    out = []
+    while n > 1:
+        out.append(2)
+        n //= 2
     return out
 
 
 T_ATT, T_WO, T_W1, T_WQ, T_IN, T_TAIL = 0, 8, 9, 13, 16, 22
 
 
-DEPTH = 2
-EVENT_TICKS = (0, 1, 2, 3, 8, 10, 12, 14, 16, 18, 20)
-
-
-def event_at(i):
-    done = jnp.maximum(i - T_TAIL, 0)
-    for at in EVENT_TICKS:
-        done = done + jnp.where(i > at, 1, 0)
+def lags_of(n_rs):
+    return (0,) + tuple(range(2, 2 * n_rs - 1)) + (2 * n_rs,)
+
+
+T_OUT = 4
+
+
+EVENT_TICKS = tuple(range(T_TAIL))
+AHEAD = 16
+
+
+def count_before(ticks, i):
+    done = 0
+    for at in sorted(set(ticks)):
+        done = done + jnp.where(i > at, ticks.count(at), 0)
     return done
 
 
+def event_ticks(n_events):
+    more = n_events - len(EVENT_TICKS)
+    return EVENT_TICKS + tuple(range(T_TAIL, T_TAIL + more))
+
+
+def send_ticks(n_events):
+    made = [0] * (4 * SUB - PRE)
+    for at in tuple(range(T_WO, T_WO + 1)) + tuple(range(T_W1, T_WQ)) + tuple(range(T_WQ, T_IN)):
+        made += [at] * SUB
+    events = event_ticks(n_events)
+    return tuple(max(at, events[max(PRE + j - AHEAD, 0)]) for j, at in enumerate(made))
+
+
 def tick_count(n_events):
-    return T_TAIL + n_events - len(EVENT_TICKS)
+    return T_TAIL + max(n_events - len(EVENT_TICKS), 10)
 
 
 def main_kernel(factors, lengths, scale, q, k, v, gs, sn, lse, wq, gain,
@@ -548,8 +574,8 @@
     swaps = [(h_sent, r_sent), (h_gp.at[:, theirs], r_gp), (h_ffn, r_ffn), (h_gf.at[1 - core], r_gf.at[0]), (h_nrm, r_nrm),
              (h_gf.at[3 - core], r_gf.at[1])]
     loads = [(h_sent, o_sent), (h_gp.at[:, mine], o_gp), (h_ffn, o_ffn), (h_gf.at[core], o_gf.at[0]), (h_nrm, o_nrm),
-             (h_x, xb), (h_ghid, gh), (h_small, small_acc.at[0]), (h_last.at[0], sendb.at[0]),
-             (h_keep, acc.at[pl.ds(0, 4)]), (h_pre, gath.at[pl.ds(0, PRE)]), (h_gf.at[2 + core], o_gf.at[1])]
+             (h_x, xb), (h_ghid, gh), (h_small, small_acc.at[0]), (h_last, sendb.at[pl.ds(0, 4 * SUB - PRE)]),
+             (h_keep, acc.at[pl.ds(0, 4 * SUB)]), (h_pre, gath.at[pl.ds(0, PRE)]), (h_gf.at[2 + core], o_gf.at[1])]
 
     def swap_copy(j):
         return remote(swaps[j][0], swaps[j][1], swap_s.at[j], swap_r.at[j], sibling)
@@ -586,8 +612,6 @@
             swap_copy(j).start()
         for j in (10, 9, 8):
             load_copy(j).wait()
-        rs_copy(0, PRE, 1).start()
-        out_copy().start()
         at = lax.broadcasted_iota(jnp.int32, (1, t), 1)
         start = jnp.zeros((1, t), jnp.int32)
         bound = jnp.int32(0)
@@ -608,7 +632,10 @@
         lane = lax.broadcasted_iota(jnp.int32, (1, d), 1)
         h0 = jnp.sum(d0, axis=-1, keepdims=True)
         h1 = jnp.sum(d1, axis=-1, keepdims=True)
-        small_acc[0, 14:15, :] += jnp.where(lane == 2 * tick, h0, 0.0) + jnp.where(lane == 2 * tick + 1, h1, 0.0)
+        small_acc[0, 14:15, :] += (
+            jnp.where(lane == 2 * tick, h0 / scale[2 * tick], 0.0)
+            + jnp.where(lane == 2 * tick + 1, h1 / scale[2 * tick + 1], 0.0)
+        )
         ga = (gsf * head_lanes(scale, tick, (1, 2 * hd), hd)).astype(BF)
         gk[...] = jnp.zeros_like(gk)
         gv[...] = jnp.zeros_like(gv)
@@ -641,12 +668,14 @@
         for far in (True, False):
             x = 1 - ctx if far else ctx
             val = (dot(a0(x), b0, 0, 0) + dot(a1(x), b1, 0, 0)).astype(BF)
-            put_chunk(sendb if far else acc, c - PRE if far else c, val)
-            if far:
-                rs_copy(0, c, 1).start()
+            put_chunk(sendb if far else acc, c - PRE // SUB if far else c, val)
 
     def half_of(ref):
         return lambda x: ref[:, pl.ds(pl.multiple_of(x * hd2, 128), hd2)]
+
+    @pl.when(tick == T_OUT)
+    def _():
+        out_copy().start()
 
     @pl.when(tick == T_WO)
     def _():
@@ -710,15 +739,25 @@
     def guarded(f, i, c):
         pl.when((c >= 0) & (c < chunks))(lambda: f(i, c))
 
-    event = event_at(tick)
-    fire = event_at(tick + 1) > event
     lanes = [(reduce_stage, i) for i in range(n_rs)] + [(gather_stage, i) for i in range(n_rs - 1, 0, -1)]
 
-    @pl.when(fire)
+    lags = lags_of(n_rs)
+    n_events = chunks + lags[-1]
+    sends = send_ticks(n_events)
+
+    def send(c, _):
+        rs_copy(0, c, 1).start()
+        return 0
+
+    lax.fori_loop(PRE + count_before(sends, tick), PRE + count_before(sends, tick + 1), send, 0)
+    events = event_ticks(n_events)
+    event = count_before(events, tick)
+
+    @pl.when(count_before(events, tick + 1) > event)
     def _():
         for lag in range(len(lanes) - 1, -1, -1):
             f, i = lanes[lag]
-            guarded(f, i, event - DEPTH * lag)
+            guarded(f, i, event - lags[lag])
 
     for i in range(len(bits) + 1):
 
@@ -784,8 +823,7 @@
     whole = lambda shape: pl.BlockSpec(shape, lambda i: (0,) * len(shape))
     wcol = lambda i: jnp.clip(i - T_IN, 0, 5)
     any_ = pl.BlockSpec(memory_space=pl.ANY)
-    lanes = 2 * len(fs) - 1
-    events = CHUNKS + DEPTH * (lanes - 1)
+    events = CHUNKS + lags_of(len(fs))[-1]
     return pl.pallas_call(
         functools.partial(main_kernel, factors),
         grid=(tick_count(events),),
@@ -815,45 +853,113 @@
       sent, ffn_in, gf, gp, normed, last, keep, pre, x, ghid, small, out)
 
 
-def finish_kernel(got, g2, g1, go, gq):
-    k = pl.program_id(0) // 2
-    h = g2.shape[0]
+SLOTS = 8
+
+
+def finish_kernel(small, got, gx_own, gx_got, own, away, out, gx, g2, g1, go, gq, gn, bn, gmg, gmb, ghs,
+                  inb, outb, low, wide, isem, osem, sems):
+    ctx = lax.axis_index("ctx")
+    seg, d = gx_own.shape
+    h = d // 2
     c = got.shape[3]
-
-    def put(out):
-        for m in range(h // c):
-            out[:, m * c : (m + 1) * c] = got[0, 0, m * h : (m + 1) * h, :].astype(F32)
-
-    pl.when(k < 4)(lambda: put(g2))
-    pl.when(k == 4)(lambda: put(go))
-    pl.when((k > 4) & (k < 9))(lambda: put(g1))
-    pl.when(k > 8)(lambda: put(gq))
-
-
-def finish_call(got, ff, d):
+    blocks = (small.shape[0] - 8) // 2
+
+    def copy(src, dst, j):
+        return pltpu.make_async_copy(src, dst, sems.at[j])
+
+    ins = [
+        copy(gx_got, low.at[0], 0),
+        copy(own.at[pl.ds(pl.multiple_of(ctx * seg, seg), seg)], low.at[1], 1),
+        copy(away, low.at[2], 2),
+        copy(gx_own, wide.at[1], 3),
+    ]
+    outs = [
+        copy(wide.at[0], gx.at[1 - ctx], 4),
+        copy(low.at[1], out.at[ctx], 5),
+        copy(low.at[2], out.at[1 - ctx], 6),
+        copy(wide.at[1], gx.at[ctx], 7),
+    ]
+
+    def place(i):
+        k, core = i // 2, i % 2
+        if k < 4:
+            ref, r, col = g2, core * 2 + k // 2, k % 2
+        elif k == 4:
+            ref, r, col = go, 0, core
+        elif k < 9:
+            ref, r, col = g1, 0, (((k - 5) // 2) * 2 + core) * 2 + (k - 5) % 2
+        else:
+            ref, r, col = gq, 0, (k - 9) * 2 + core
+        return ref.at[pl.ds(r * h, h), pl.ds(col * h, h)]
+
+    def load(i):
+        src = got.at[pl.ds(i // 2 * SUB, SUB), i % 2]
+        return pltpu.make_async_copy(src, inb.at[i % SLOTS], isem.at[i % SLOTS])
+
+    def store(i):
+        return pltpu.make_async_copy(outb.at[i % SLOTS], place(i), osem.at[i % SLOTS])
+
+    count = 2 * BLOCKS
+    for i in range(SLOTS):
+        load(i).start()
+    for v in ins:
+        v.start()
+    half = pl.ds(pl.multiple_of(ctx * h, h), h)
+    gn[...] = small[0:3, half]
+    bn[...] = small[3:6, half]
+    for j in range(blocks // 2):
+        at = slice(j * d, (j + 1) * d)
+        gmg[:, at] = small[pl.ds(6 + ctx * (blocks // 2) + j, 1), :]
+        gmb[:, at] = small[pl.ds(6 + blocks + ctx * (blocks // 2) + j, 1), :]
+    n = ghs.shape[1]
+    row = small[6 + 2 * blocks : 7 + 2 * blocks, :]
+    ghs[...] = jnp.where(ctx == 0, row[:, 0:n], row[:, n : 2 * n])
+    for i in range(count):
+        load(i).wait()
+        if i >= SLOTS:
+            store(i - SLOTS).wait()
+        groups = h // c // SUB
+        for j in range(SUB):
+            for m in range(groups):
+                at = (j * groups + m) * c
+                outb[i % SLOTS, :, at : at + c] = inb[i % SLOTS, j, m * h : (m + 1) * h, :].astype(F32)
+        store(i).start()
+        if i + SLOTS < count:
+            load(i + SLOTS).start()
+        if i == SLOTS:
+            for j in range(4):
+                ins[j].wait()
+                if j == 0:
+                    wide[0] = low[0].astype(F32)
+                outs[j].start()
+    for i in range(count - SLOTS, count):
+        store(i).wait()
+    for v in outs:
+        v.wait()
+
+
+def finish_call(small, got, gx_own, gx_got, own, away, ff, heads):
+    seg, d = gx_own.shape
     h = d // 2
     rows, cols = got.shape[2:]
-
-    def spec(lo, hi, at):
-        def index(i):
-            i = jnp.clip(i, 2 * lo, 2 * hi + 1)
-            return at(i // 2 - lo, i % 2)
-
-        return pl.BlockSpec((h, h), index)
-
+    any_ = pl.BlockSpec(memory_space=pl.ANY)
+    vmem = pl.BlockSpec(memory_space=pltpu.VMEM)
+    dma = lambda n: pltpu.SemaphoreType.DMA((n,))
     return pl.pallas_call(
         finish_kernel,
-        grid=(24,),
-        in_specs=[pl.BlockSpec((1, 1, rows, cols), lambda i: (i // 2, i % 2, 0, 0))],
-        out_specs=[
-            spec(0, 3, lambda k, c: (c * 2 + k // 2, k % 2)),
-            spec(5, 8, lambda k, c: (0, ((k // 2) * 2 + c) * 2 + k % 2)),
-            spec(4, 4, lambda k, c: (0, c)),
-            spec(9, 11, lambda k, c: (0, k * 2 + c)),
+        in_specs=[vmem] + [any_] * 5,
+        out_specs=[any_] * 6 + [vmem] * 5,
+        out_shape=[
+            struct((2, seg, d), BF), struct((2, seg, d), F32), struct((ff // 2, d), F32), struct((h, ff), F32),
+            struct((h, d), F32), struct((h, 3 * d), F32), struct((3, h), F32), struct((3, h), F32),
+            struct((1, ff // 2), F32), struct((1, ff // 2), F32), struct((1, heads // 2), F32),
         ],
-        out_shape=[struct((ff // 2, d), F32), struct((h, ff), F32), struct((h, d), F32), struct((h, 3 * d), F32)],
+        scratch_shapes=[
+            pltpu.VMEM((SLOTS, SUB, rows, cols), BF), pltpu.VMEM((SLOTS, h, h), F32),
+            pltpu.VMEM((3, seg, d), BF), pltpu.VMEM((2, seg, d), F32), dma(SLOTS), dma(SLOTS), dma(8),
+        ],
         compiler_params=pltpu.CompilerParams(vmem_limit_bytes=60 * 2**20),
-    )(got)
+    )(small, got, gx_own, gx_got, own, away)
 
 
 def local(
@@ -864,14 +970,13 @@
     d = tokens.shape[2]
     ff = w_fc1.shape[1]
     heads = head_scale.shape[0]
-    ctx = lax.axis_index("ctx")
     mg, mb = mid_gain[None, :], mid_bias[None, :]
     pieces = 1
     for f in factors[1:]:
         pieces *= f
     half = d // 2
     rows = max(half, 16 * pieces)
-    cols = half * half // rows
+    cols = half * half // rows // SUB
     x, normed, qkv, sent, lse, ffn_in, gf, gp, gsent, ghid, out, keep, last, pre, small = front_call(
         rows, cols, doc_lengths, head_scale, norm_gain, norm_bias, mg, mb, tokens, cotangent, w_qkv, w_out, w_fc1, w_fc2
     )
@@ -879,25 +984,8 @@
         factors, rows, cols, doc_lengths, head_scale, qkv, gsent, sent, lse, w_qkv, norm_gain, ffn_in, gf, gp, normed, last,
         keep, pre, x, ghid, small, out,
     )
-    g2, g1, go, gq = finish_call(got, ff, d)
-    gx_got = gx_got.astype(F32)
-    gx = jnp.stack([jnp.where(ctx == 0, gx_own, gx_got), jnp.where(ctx == 0, gx_got, gx_own)])
-
-    def take(v, axis):
-        size = v.shape[axis] // 2
-        return lax.dynamic_slice_in_dim(v, ctx * size, size, axis)
-
-    nm = ff // d
-    gn = take(small[0:3], 1)
-    bn = take(small[3:6], 1)
-    gmg = take(small[6 : 6 + nm].reshape(-1), 0)
-    gmb = take(small[6 + nm : 6 + 2 * nm].reshape(-1), 0)
-    ghs = take(small[6 + 2 * nm, 0:heads] / head_scale, 0)
-
-    seg = out_got.shape[0]
-    out_own = lax.dynamic_slice_in_dim(out, ctx * seg, seg, 0)
-    out = jnp.stack([jnp.where(ctx == 0, out_own, out_got), jnp.where(ctx == 0, out_got, out_own)])
-    return (out, gx, gq, go, g1, g2, gn, bn, gmg, gmb, ghs)
+    out, gx, g2, g1, go, gq, gn, bn, gmg, gmb, ghs = finish_call(small, got, gx_own, gx_got, out, out_got, ff, heads)
+    return (out, gx, gq, go, g1, g2, gn, bn, gmg.reshape(-1), gmb.reshape(-1), ghs.reshape(-1))
 
 
 def solution(mesh):

time: 301 us -> 282 us (0.937)
  Pallas kernels: 291 us -> 281 us
  other arithmetic: 4.2 us -> 0 us
    pallas_call x1, Pallas kernels: 21.3 us -> 15.5 us  [finish_call(): pl.pallas_call(finish_kernel, in_specs=[vmem] + [any_] * 5, out_specs=[an...]
    pallas_call x1, Pallas kernels: 98.8 us -> 93.4 us  [front_call(): pl.pallas_call(front_kernel, grid=(F_END,), in_specs=[smem, smem, whole((...]
    another operation x4 -> x0, other arithmetic: 4.19 us -> none  [the longest x2 2.48 us: local(): jnp.stack([jnp.where(ctx == 0, out_own, out_got), jnp.where(ctx == 0, out...]
where the time goes in v4:
time: 282 us; the launch traced here: 281 us
  Pallas kernels  281 us (100%)
    pallas_call x1, Pallas kernels, main_call(): pl.pallas_call(functools.partial(main_kernel, factors), grid=(tick_count(...  172 us
    pallas_call x1, Pallas kernels, front_call(): pl.pallas_call(front_kernel, grid=(F_END,), in_specs=[smem, smem, whole((...  93.4 us
    pallas_call x1, Pallas kernels, finish_call(): pl.pallas_call(finish_kernel, in_specs=[vmem] + [any_] * 5, out_specs=[an...  15.5 us

profile of v4, /device:TPU:0, one launch (start us, length us, event | category | flops | bytes accessed | tf_op | source)
XLA Modules:
  0.0 281.4 jit_solution(2570033972853927397)
XLA Ops:
  0.6 93.4 %shard_map.203 = (bf16[512,1024]{1,0:T(8,128)(2,1)}, bf16[512,1024]{1,0:T(8,128)(2,1)}, bf16[3,512,1024]{2,1,0:T(8,128)(2,1)}, bf16[512,1024]{1,0:T(8,128)(2,1)}...) custom-call(s32[2,4]{1,0:T(2,128)} %lengths.3, ...), custom_call_target="tpu_custom_call" | custom-call | tf_op jit(solution)/shard_map/pallas_call | solution.py:393
  94.1 171.6 %shard_map.204 = (bf16[24,2,512,256]{3,2,1,0:T(8,128)(2,1)}, f32[256,1024]{1,0:T(8,128)}, bf16[256,1024]{1,0:T(8,128)(2,1)}, f32[16,1024]{1,0:T(8,128)}, bf16[256,1024]{1,0:T(8,128)(2,1)}) custom-call(s32[2,4]{1,0:T(2,128)} %lengths.3, f32[16]{0:T(128)} %scale.3, bf16[3,512,1024]{2,1,0:T(8,128)(2,1)} %get-tuple-element.42.q.k.v, ...), custom_call_target="tpu_custom_call" | custom-call | tf_op jit(solution)/shard_map/pallas_call | solution.py:827
  265.7 15.5 %shard_map.205 = (bf16[2,256,1024]{2,1,0:T(8,128)(2,1)}, f32[2,256,1024]{2,1,0:T(8,128)}, f32[2048,1024]{1,0:T(8,128)}, f32[512,4096]{1,0:T(8,128)}, f32[512,102...) custom-call(f32[16,1024]{1,0:T(8,128)} %get-tuple-element.57.small, ...), custom_call_target="tpu_custom_call" | custom-call | tf_op jit(solution)/shard_map/pallas_call | solution.py:948

commit v5 on v4

--- a/solution.py
+++ b/solution.py
@@ -418,14 +418,16 @@
     return out
 
 
-T_ATT, T_WO, T_W1, T_WQ, T_IN, T_TAIL = 0, 8, 9, 13, 16, 22
+ATT_TICKS = (0, 1, 2, 4, 5, 7, 8, 10)
+WG_TICKS = (3, 6, 9, 11, 12, 13, 14, 15)
+T_IN, T_TAIL = 16, 22
 
 
 def lags_of(n_rs):
     return (0,) + tuple(range(2, 2 * n_rs - 1)) + (2 * n_rs,)
 
 
-T_OUT = 4
+T_OUT = 26
 
 
 EVENT_TICKS = tuple(range(T_TAIL))
@@ -446,7 +448,7 @@
 
 def send_ticks(n_events):
     made = [0] * (4 * SUB - PRE)
-    for at in tuple(range(T_WO, T_WO + 1)) + tuple(range(T_W1, T_WQ)) + tuple(range(T_WQ, T_IN)):
+    for at in WG_TICKS:
         made += [at] * SUB
     events = event_ticks(n_events)
     return tuple(max(at, events[max(PRE + j - AHEAD, 0)]) for j, at in enumerate(made))
@@ -621,7 +623,9 @@
         fill_bias(start, bias, t)
         load_copy(7).wait()
 
-    @pl.when(tick < T_WO)
+    pair = count_before(ATT_TICKS, tick)
+
+    @pl.when(count_before(ATT_TICKS, tick + 1) > pair)
     def _():
         hd = q.shape[2] // 2
         kt = k[0].astype(F32).T.astype(BF)
@@ -633,10 +637,10 @@
         h0 = jnp.sum(d0, axis=-1, keepdims=True)
         h1 = jnp.sum(d1, axis=-1, keepdims=True)
         small_acc[0, 14:15, :] += (
-            jnp.where(lane == 2 * tick, h0 / scale[2 * tick], 0.0)
-            + jnp.where(lane == 2 * tick + 1, h1 / scale[2 * tick + 1], 0.0)
+            jnp.where(lane == 2 * pair, h0 / scale[2 * pair], 0.0)
+            + jnp.where(lane == 2 * pair + 1, h1 / scale[2 * pair + 1], 0.0)
         )
-        ga = (gsf * head_lanes(scale, tick, (1, 2 * hd), hd)).astype(BF)
+        ga = (gsf * head_lanes(scale, pair, (1, 2 * hd), hd)).astype(BF)
         gk[...] = jnp.zeros_like(gk)
         gv[...] = jnp.zeros_like(gv)
         for i in range(t // QB):
@@ -654,13 +658,14 @@
             gk[k0:k1, :] += dot(ds, qm, 1, 0)
             gq = dot(kt[:, k0:k1], ds, 1, 0) * (hd**-0.5)
             gqt[:, qs] = jnp.concatenate([gq[0:hd, 0:QB], gq[hd:, QB:]], axis=0)
-        half = tick // (T_WO // 2)
-        at = pl.ds(pl.multiple_of(lax.rem(tick, T_WO // 2) * 128, 128), 128)
+        per_core = len(ATT_TICKS) // 2
+        half = pair // per_core
+        at = pl.ds(pl.multiple_of(lax.rem(pair, per_core) * 128, 128), 128)
         gall[half, 0, :, at] = gqt[...].T.astype(BF)
         gall[half, 1, :, at] = gk[...].astype(BF)
         gall[half, 2, :, at] = gv[...].astype(BF)
 
-    @pl.when(tick == T_WO - 1)
+    @pl.when(tick == ATT_TICKS[-1])
     def _():
         gq_copy().start()
 
@@ -676,15 +681,16 @@
     @pl.when(tick == T_OUT)
     def _():
         out_copy().start()
-
-    @pl.when(tick == T_WO)
+        gx_copy().start()
+
+    @pl.when(tick == WG_TICKS[0])
     def _():
         for j in (0, 1):
             load_copy(j).wait()
             swap_copy(j).wait_recv()
         wgrad(4, half_of(o_sent), half_of(r_sent), o_gp[...], r_gp[...])
 
-    @pl.when(tick == T_W1)
+    @pl.when(tick == WG_TICKS[1])
     def _():
         for j in (2, 3):
             load_copy(j).wait()
@@ -692,21 +698,24 @@
         load_copy(11).wait()
         swap_copy(5).wait_recv()
 
-    @pl.when((tick >= T_W1) & (tick < T_WQ))
-    def _():
-        c = tick - T_W1
+    block = count_before(WG_TICKS, tick)
+    makes = count_before(WG_TICKS, tick + 1) > block
+
+    @pl.when(makes & (block >= 1) & (block < 5))
+    def _():
+        c = block - 1
         b = lambda ref: ref[c // 2, :, pl.ds(pl.multiple_of(lax.rem(c, 2) * hd2, 128), hd2)]
         wgrad(c + 5, half_of(o_ffn), half_of(r_ffn), b(o_gf), b(r_gf))
 
-    @pl.when(tick == T_WQ)
+    @pl.when(tick == WG_TICKS[5])
     def _():
         load_copy(4).wait()
         swap_copy(4).wait_recv()
         gq_copy().wait_recv()
 
-    @pl.when((tick >= T_WQ) & (tick < T_IN))
-    def _():
-        c = tick - T_WQ
+    @pl.when(makes & (block >= 5))
+    def _():
+        c = block - 5
         wgrad(c + 9, half_of(o_nrm), half_of(r_nrm), gall[core, c], r_gq[c])
 
     @pl.when((tick >= T_IN) & (tick < T_TAIL))
@@ -732,7 +741,6 @@
         small_acc[0, 3:4, :] = colsum(e)
         gh[...] += ln_back(e, gain[0:1, :], n, inv)
         gx_send[...] = gh[rows_of(1 - ctx), :].astype(BF)
-        gx_copy().start()
         gx_own[...] = gh[rows_of(ctx), :]
         small_copy(0).start()
 
@@ -817,7 +825,7 @@
     per = lambda k: [dma(CHUNKS, f - 1) for f in fs[k:]]
     vm = lambda *shape: pltpu.VMEM(shape, BF)
     vf = lambda *shape: pltpu.VMEM(shape, F32)
-    pair = lambda i: jnp.minimum(i, T_WO - 1)
+    pair = lambda i: jnp.minimum(count_before(ATT_TICKS, i), len(ATT_TICKS) - 1)
     part = lambda j: pl.BlockSpec((1, t, 128), lambda i: (j, 0, pair(i)))
     flat = pl.BlockSpec((t, 128), lambda i: (0, pair(i)))
     whole = lambda shape: pl.BlockSpec(shape, lambda i: (0,) * len(shape))

time: 282 us -> 272 us (0.965)
  Pallas kernels: 281 us -> 271 us
    pallas_call x1, Pallas kernels: 172 us -> 162 us  [main_call(): pl.pallas_call(functools.partial(main_kernel, factors), grid=(tick_count(...]
where the time goes in v5:
time: 272 us
  Pallas kernels  271 us (100%)
    pallas_call x1, Pallas kernels, main_call(): pl.pallas_call(functools.partial(main_kernel, factors), grid=(tick_count(...  162 us
    pallas_call x1, Pallas kernels, front_call(): pl.pallas_call(front_kernel, grid=(F_END,), in_specs=[smem, smem, whole((...  93.4 us
    pallas_call x1, Pallas kernels, finish_call(): pl.pallas_call(finish_kernel, in_specs=[vmem] + [any_] * 5, out_specs=[an...  15.5 us

profile of v5, /device:TPU:0, one launch (start us, length us, event | category | flops | bytes accessed | tf_op | source)
XLA Modules:
  0.0 271.8 jit_solution(2999348633188575304)
XLA Ops:
  0.6 93.4 %shard_map.203 = (bf16[512,1024]{1,0:T(8,128)(2,1)}, bf16[512,1024]{1,0:T(8,128)(2,1)}, bf16[3,512,1024]{2,1,0:T(8,128)(2,1)}, bf16[512,1024]{1,0:T(8,128)(2,1)}...) custom-call(s32[2,4]{1,0:T(2,128)} %lengths.3, ...), custom_call_target="tpu_custom_call" | custom-call | tf_op jit(solution)/shard_map/pallas_call | solution.py:393
  94.1 162.1 %shard_map.204 = (bf16[24,2,512,256]{3,2,1,0:T(8,128)(2,1)}, f32[256,1024]{1,0:T(8,128)}, bf16[256,1024]{1,0:T(8,128)(2,1)}, f32[16,1024]{1,0:T(8,128)}, bf16[256,1024]{1,0:T(8,128)(2,1)}) custom-call(s32[2,4]{1,0:T(2,128)} %lengths.3, f32[16]{0:T(128)} %scale.3, bf16[3,512,1024]{2,1,0:T(8,128)(2,1)} %get-tuple-element.42.q.k.v, ...), custom_call_target="tpu_custom_call" | custom-call | tf_op jit(solution)/shard_map/pallas_call | solution.py:835
  256.1 15.5 %shard_map.205 = (bf16[2,256,1024]{2,1,0:T(8,128)(2,1)}, f32[2,256,1024]{2,1,0:T(8,128)}, f32[2048,1024]{1,0:T(8,128)}, f32[512,4096]{1,0:T(8,128)}, f32[512,102...) custom-call(f32[16,1024]{1,0:T(8,128)} %get-tuple-element.57.small, ...), custom_call_target="tpu_custom_call" | custom-call | tf_op jit(solution)/shard_map/pallas_call | solution.py:956

commit v6 on v5

--- a/solution.py
+++ b/solution.py
@@ -75,8 +75,8 @@
 BLOCKS = 12
 SUB = 2
 CHUNKS = BLOCKS * SUB
-PRE = 3 * SUB
-F_Q1, F_Q2, F_AT, F_FC, F_NM, F_A, F_B1, F_O, F_B2, F_END = 0, 3, 6, 14, 18, 22, 26, 30, 34, 38
+PRE = 2 * SUB
+F_Q1, F_Q2, F_AT, F_FC, F_NM, F_A, F_B1, F_O, F_B2, F_END = 0, 3, 6, 10, 14, 18, 22, 26, 30, 34
 MESH = pl.DeviceIdType.MESH
 
 
@@ -205,25 +205,25 @@
 
     @pl.when((tick >= F_AT) & (tick < F_FC))
     def _():
-        pair = tick - F_AT
         hd = 64
-        at = pl.ds(pl.multiple_of(pair * 128, 128), 128)
-        vt = qkvb[2, :, at].astype(F32).T.astype(BF)
-        sc = head_lanes(scale, pair, (1, 128), hd)
-        for i in range(t // QB):
-            k0, k1 = key_range(i)
-            qs = slice(i * QB, (i + 1) * QB)
-            qm = (both_heads(qkvb[0, qs, at], hd) * (hd**-0.5)).astype(BF)
-            st = dot(qkvb[1, k0:k1, at], qm, 1, 1) + bias[i, 0 : k1 - k0, :]
-            top = jnp.max(st, axis=0, keepdims=True)
-            pt = jnp.exp(st - top)
-            total = jnp.sum(pt, axis=0, keepdims=True)
-            ot = dot(vt[:, k0:k1], pt.astype(BF), 1, 0) * (1.0 / total)
-            o = jnp.concatenate([ot[0:hd, 0:QB], ot[hd:, QB:]], axis=0).T
-            sent[qs, at] = (o * sc).astype(BF)
-            ls = top + jnp.log(total)
-            lse[pair, 0:1, qs] = ls[:, 0:QB]
-            lse[pair, 1:2, qs] = ls[:, QB:]
+        for pair in (2 * (tick - F_AT), 2 * (tick - F_AT) + 1):
+            at = pl.ds(pl.multiple_of(pair * 128, 128), 128)
+            vt = qkvb[2, :, at].astype(F32).T.astype(BF)
+            sc = head_lanes(scale, pair, (1, 128), hd)
+            for i in range(t // QB):
+                k0, k1 = key_range(i)
+                qs = slice(i * QB, (i + 1) * QB)
+                qm = (both_heads(qkvb[0, qs, at], hd) * (hd**-0.5)).astype(BF)
+                st = dot(qkvb[1, k0:k1, at], qm, 1, 1) + bias[i, 0 : k1 - k0, :]
+                top = jnp.max(st, axis=0, keepdims=True)
+                pt = jnp.exp(st - top)
+                total = jnp.sum(pt, axis=0, keepdims=True)
+                ot = dot(vt[:, k0:k1], pt.astype(BF), 1, 0) * (1.0 / total)
+                o = jnp.concatenate([ot[0:hd, 0:QB], ot[hd:, QB:]], axis=0).T
+                sent[qs, at] = (o * sc).astype(BF)
+                ls = top + jnp.log(total)
+                lse[pair, 0:1, qs] = ls[:, 0:QB]
+                lse[pair, 1:2, qs] = ls[:, QB:]
 
     @pl.when(tick == F_FC)
     def _():
@@ -427,7 +427,7 @@
     return (0,) + tuple(range(2, 2 * n_rs - 1)) + (2 * n_rs,)
 
 
-T_OUT = 26
+T_OUT = 25
 
 
 EVENT_TICKS = tuple(range(T_TAIL))

time: 272 us -> 266 us (0.978)
  Pallas kernels: 271 us -> 265 us
    pallas_call x1, Pallas kernels: 93.4 us -> 87.7 us  [front_call(): pl.pallas_call(front_kernel, grid=(F_END,), in_specs=[smem, smem, whole((...]
where the time goes in v6:
time: 266 us; the launch traced here: 265 us
  Pallas kernels  265 us (100%)
    pallas_call x1, Pallas kernels, main_call(): pl.pallas_call(functools.partial(main_kernel, factors), grid=(tick_count(...  161 us
    pallas_call x1, Pallas kernels, front_call(): pl.pallas_call(front_kernel, grid=(F_END,), in_specs=[smem, smem, whole((...  87.7 us
    pallas_call x1, Pallas kernels, finish_call(): pl.pallas_call(finish_kernel, in_specs=[vmem] + [any_] * 5, out_specs=[an...  15.5 us

profile of v6, /device:TPU:0, one launch (start us, length us, event | category | flops | bytes accessed | tf_op | source)
XLA Modules:
  0.0 265.4 jit_solution(13943731128107256479)
XLA Ops:
  0.6 87.7 %shard_map.203 = (bf16[512,1024]{1,0:T(8,128)(2,1)}, bf16[512,1024]{1,0:T(8,128)(2,1)}, bf16[3,512,1024]{2,1,0:T(8,128)(2,1)}, bf16[512,1024]{1,0:T(8,128)(2,1)}...) custom-call(s32[2,4]{1,0:T(2,128)} %lengths.3, ...), custom_call_target="tpu_custom_call" | custom-call | tf_op jit(solution)/shard_map/pallas_call | solution.py:393
  88.4 161.4 %shard_map.204 = (bf16[24,2,512,256]{3,2,1,0:T(8,128)(2,1)}, f32[256,1024]{1,0:T(8,128)}, bf16[256,1024]{1,0:T(8,128)(2,1)}, f32[16,1024]{1,0:T(8,128)}, bf16[256,1024]{1,0:T(8,128)(2,1)}) custom-call(s32[2,4]{1,0:T(2,128)} %lengths.3, f32[16]{0:T(128)} %scale.3, bf16[3,512,1024]{2,1,0:T(8,128)(2,1)} %get-tuple-element.42.q.k.v, ...), custom_call_target="tpu_custom_call" | custom-call | tf_op jit(solution)/shard_map/pallas_call | solution.py:835
  249.7 15.5 %shard_map.205 = (bf16[2,256,1024]{2,1,0:T(8,128)(2,1)}, f32[2,256,1024]{2,1,0:T(8,128)}, f32[2048,1024]{1,0:T(8,128)}, f32[512,4096]{1,0:T(8,128)}, f32[512,102...) custom-call(f32[16,1024]{1,0:T(8,128)} %get-tuple-element.57.small, ...), custom_call_target="tpu_custom_call" | custom-call | tf_op jit(solution)/shard_map/pallas_call | solution.py:956

commit v7 on v6

--- a/solution.py
+++ b/solution.py
@@ -165,7 +165,6 @@
         load_copy(2).start()
         pl.semaphore_wait(barrier, 2)
         tok_copy().start()
-        cot_copy().start()
         small[...] = jnp.zeros_like(small)
         at = lax.broadcasted_iota(jnp.int32, (1, t), 1)
         start = jnp.zeros((1, t), jnp.int32)
@@ -179,6 +178,7 @@
     @pl.when(tick == F_Q2)
     def _():
         tok_copy().wait_recv()
+        cot_copy().start()
         out_copy(0).start()
 
     for own in (True, False):
@@ -199,9 +199,6 @@
     def _():
         out_copy(1).start()
         out_copy(2).start()
-        cot_copy().wait_recv()
-        load_copy(1).wait()
-        cot_core().start()
 
     @pl.when((tick >= F_AT) & (tick < F_FC))
     def _():
@@ -228,6 +225,9 @@
     @pl.when(tick == F_FC)
     def _():
         out_copy(3).start()
+        cot_copy().wait_recv()
+        load_copy(1).wait()
+        cot_core().start()
         load_copy(2).wait()
         n, inv = ln_stats(dot(sent[...], wo[...], 1, 0))
         n1[...] = n

time: 266 us -> 257 us (0.966)
  Pallas kernels: 265 us -> 256 us
    pallas_call x1, Pallas kernels: 87.7 us -> 79.5 us  [front_call(): pl.pallas_call(front_kernel, grid=(F_END,), in_specs=[smem, smem, whole((...]
where the time goes in v7:
time: 257 us
  Pallas kernels  256 us (100%)
    pallas_call x1, Pallas kernels, main_call(): pl.pallas_call(functools.partial(main_kernel, factors), grid=(tick_count(...  161 us
    pallas_call x1, Pallas kernels, front_call(): pl.pallas_call(front_kernel, grid=(F_END,), in_specs=[smem, smem, whole((...  79.5 us
    pallas_call x1, Pallas kernels, finish_call(): pl.pallas_call(finish_kernel, in_specs=[vmem] + [any_] * 5, out_specs=[an...  15.5 us

profile of v7, /device:TPU:0, one launch (start us, length us, event | category | flops | bytes accessed | tf_op | source)
XLA Modules:
  0.0 257.1 jit_solution(5258640975017187046)
XLA Ops:
  0.6 79.5 %shard_map.203 = (bf16[512,1024]{1,0:T(8,128)(2,1)}, bf16[512,1024]{1,0:T(8,128)(2,1)}, bf16[3,512,1024]{2,1,0:T(8,128)(2,1)}, bf16[512,1024]{1,0:T(8,128)(2,1)}...) custom-call(s32[2,4]{1,0:T(2,128)} %lengths.3, ...), custom_call_target="tpu_custom_call" | custom-call | tf_op jit(solution)/shard_map/pallas_call | solution.py:393
  80.1 161.3 %shard_map.204 = (bf16[24,2,512,256]{3,2,1,0:T(8,128)(2,1)}, f32[256,1024]{1,0:T(8,128)}, bf16[256,1024]{1,0:T(8,128)(2,1)}, f32[16,1024]{1,0:T(8,128)}, bf16[256,1024]{1,0:T(8,128)(2,1)}) custom-call(s32[2,4]{1,0:T(2,128)} %lengths.3, f32[16]{0:T(128)} %scale.3, bf16[3,512,1024]{2,1,0:T(8,128)(2,1)} %get-tuple-element.42.q.k.v, ...), custom_call_target="tpu_custom_call" | custom-call | tf_op jit(solution)/shard_map/pallas_call | solution.py:835
  241.5 15.5 %shard_map.205 = (bf16[2,256,1024]{2,1,0:T(8,128)(2,1)}, f32[2,256,1024]{2,1,0:T(8,128)}, f32[2048,1024]{1,0:T(8,128)}, f32[512,4096]{1,0:T(8,128)}, f32[512,102...) custom-call(f32[16,1024]{1,0:T(8,128)} %get-tuple-element.57.small, ...), custom_call_target="tpu_custom_call" | custom-call | tf_op jit(solution)/shard_map/pallas_call | solution.py:956
